TPU v7x, 32 devices: a whole 2x2x4 slice. The times are simulated.
32 devices in a mesh: section: 2 (over x), ctx: 4 (over y, core), wt: 4 (over z).
Axes of the slice: x: 2, y: 2, z: 4, core: 2. Of those that a mesh axis runs over, the one named last changes fastest.
Arguments:
- feed: bfloat16 [2, 2, 4, 1024, 1600], P('section', None, 'wt', 'ctx'), may hold values from -6 to 6
- block_order: int32 [8], replicated, may hold values from 0 to 7, as said below
- attn_gain: bfloat16 [2, 1600], P('section', 'wt'), may hold values from 0.5 to 1.5
- attn_shift: bfloat16 [2, 1600], P('section', 'wt'), may hold values from -3 to 3
- w_qkv: bfloat16 [2, 1600, 4800], P('section', 'wt'), may hold values from -0.15625 to 0.15625
- query_bias: bfloat16 [2, 1600], P('section', 'wt'), may hold values from -3 to 3
- value_bias: bfloat16 [2, 1600], P('section', 'wt'), may hold values from -3 to 3
- w_proj: bfloat16 [2, 1600, 1600], P('section', 'wt'), may hold values from -1.75 to 1.75
- proj_bias: bfloat16 [2, 1600], P('section', 'wt'), may hold values from -3 to 3
- mlp_gain: bfloat16 [2, 1600], P('section', 'wt'), may hold values from 0.5 to 1.5
- mlp_shift: bfloat16 [2, 1600], P('section', 'wt'), may hold values from -3 to 3
- w_fc: bfloat16 [2, 1600, 6400], P('section', 'wt'), may hold values from -0.15625 to 0.15625
- fc_bias: bfloat16 [2, 6400], P('section', 'wt'), may hold values from -3 to 3
- w_out: bfloat16 [2, 6400, 1600], P('section', 'wt'), may hold values from -0.078125 to 0.078125
- out_bias: bfloat16 [2, 1600], P('section', 'wt'), may hold values from -3 to 3
Outputs:
- result: bfloat16 [2, 2, 4, 1024, 1600], P('section', None, 'wt', 'ctx')
- attn_gain_grad: float32 [2, 1600], P('section', 'wt')
- attn_shift_grad: float32 [2, 1600], P('section', 'wt')
- w_qkv_grad: float32 [2, 1600, 4800], P('section', 'wt')
- query_bias_grad: float32 [2, 1600], P('section', 'wt')
- value_bias_grad: float32 [2, 1600], P('section', 'wt')
- w_proj_grad: float32 [2, 1600, 1600], P('section', 'wt')
- proj_bias_grad: float32 [2, 1600], P('section', 'wt')
- mlp_gain_grad: float32 [2, 1600], P('section', 'wt')
- mlp_shift_grad: float32 [2, 1600], P('section', 'wt')
- w_fc_grad: float32 [2, 1600, 6400], P('section', 'wt')
- fc_bias_grad: float32 [2, 6400], P('section', 'wt')
- w_out_grad: float32 [2, 6400, 1600], P('section', 'wt')
- out_bias_grad: float32 [2, 1600], P('section', 'wt')
Inputs may be any that keep to these rules, and one draw needn't show every extreme that they name: `block_order`: A permutation of the 8 blocks of a sequence, the same for every sequence: entry t names the block stored in slot t; slots 2 * c and 2 * c + 1 hold blocks b and 7 - b for some b.
All inputs are finite; a program needn't handle non-finite values.
Results may differ from a plain program's by a relative error of at most 0.017.
Values may be sent and summed in bfloat16 or wider, within the bound.
No kernel may reach another device: no remote copies, remote signals or barrier semaphores. Data moves between devices by JAX's collectives and lax.ppermute only.
A program may use at most 512 MiB of HBM per device.

v0:
```python
import math

import jax
import jax.numpy as jnp
from jax import lax
from jax.sharding import PartitionSpec as P

HEADS = 25
HEAD_DIM = 64


EPS = 1e-05
NEG = -1000000000.0


def passed_along(value, axis, steps):
    count = lax.axis_size(axis)
    initial, last = (max(0, -steps), min(count, count - steps))
    return lax.ppermute(value, axis, [(source, source + steps) for source in range(initial, last)])


def shortened(array):

    def short(part):
        return part.astype(jnp.bfloat16) if part.dtype == jnp.float32 else part

    return jax.tree.map(short, array)


def layer_norm(values):
    center = values - jnp.mean(values, -1, keepdims=True)
    spread = jnp.mean(center * center, -1, keepdims=True)
    return center * lax.rsqrt(spread + EPS)


def norm_affine(values, gain, shift):
    return layer_norm(values) * gain + shift


def gelu_tanh(values):
    return jax.nn.gelu(values, approximate=True)


def positions(order, first_slot, count, block):
    offsets = jnp.arange(count, dtype=jnp.int32)
    slots = first_slot + offsets // block
    table = (slots[:, None] == jnp.arange(order.shape[0], dtype=jnp.int32)[None, :]).astype(
        jnp.int32
    )
    return jnp.sum(table * order[None, :], 1) * block + offsets % block


def head_slice(array, start, span, group):
    return lax.dynamic_slice_in_dim(array, start, span, 1).reshape(array.shape[0], group, HEAD_DIM)


def attend(query_low, pairs, allowed):
    rows_here = query_low.shape[0]
    width = query_low.shape[1]
    group = math.gcd(HEADS, 5)
    span = group * HEAD_DIM
    scale = HEAD_DIM ** (-0.5)

    def per_group(index, carry):
        outputs, log_totals = carry
        start = index * span
        query = head_slice(query_low, start, span, group)
        keyed = head_slice(pairs, start, span, group)
        valued = head_slice(pairs, width + start, span, group)
        scores = (
            jnp.einsum("qhd,khd->hqk", query, keyed, preferred_element_type=jnp.float32) * scale
        )
        scores = jnp.where(allowed[None], scores, NEG)
        highest = jnp.max(scores, -1, keepdims=True)
        exponent = jnp.exp(scores - highest)
        totals = jnp.sum(exponent, -1, keepdims=True)
        chance_low = (exponent / totals).astype(jnp.bfloat16)
        mixed = jnp.einsum("hqk,khd->qhd", chance_low, valued, preferred_element_type=jnp.float32)
        outputs = lax.dynamic_update_slice_in_dim(outputs, mixed.reshape(rows_here, span), start, 1)
        log_totals = lax.dynamic_update_slice_in_dim(
            log_totals, (highest + jnp.log(totals))[:, :, 0], index * group, 0
        )
        return (outputs, log_totals)

    initial = (
        jnp.zeros((rows_here, width), jnp.float32),
        jnp.zeros((HEADS, rows_here), jnp.float32),
    )
    return lax.fori_loop(0, HEADS // group, per_group, initial)


def attend_back(query_low, pairs, grad_mixed, log_totals, allowed):
    rows_here = query_low.shape[0]
    width = query_low.shape[1]
    keys_all = pairs.shape[0]
    group = math.gcd(HEADS, 5)
    span = group * HEAD_DIM
    scale = HEAD_DIM ** (-0.5)

    def per_group(index, carry):
        grad_query, term = carry
        start = index * span
        query = head_slice(query_low, start, span, group)
        keyed = head_slice(pairs, start, span, group)
        valued = head_slice(pairs, width + start, span, group)
        grad_out = head_slice(grad_mixed, start, span, group)
        scores = (
            jnp.einsum("qhd,khd->hqk", query, keyed, preferred_element_type=jnp.float32) * scale
        )
        scores = jnp.where(allowed[None], scores, NEG)
        lse_part = lax.dynamic_slice_in_dim(log_totals, index * group, group, 0)
        chance = jnp.exp(scores - lse_part[:, :, None])
        chance_low = chance.astype(jnp.bfloat16)
        grad_chance = jnp.einsum(
            "qhd,khd->hqk", grad_out, valued, preferred_element_type=jnp.float32
        )
        inner = jnp.sum(chance * grad_chance, -1, keepdims=True)
        grad_scores = (chance * (grad_chance - inner)).astype(jnp.bfloat16)
        query_part = (
            jnp.einsum("hqk,khd->qhd", grad_scores, keyed, preferred_element_type=jnp.float32)
            * scale
        )
        key_part = (
            jnp.einsum("hqk,qhd->khd", grad_scores, query, preferred_element_type=jnp.float32)
            * scale
        )
        value_part = jnp.einsum(
            "hqk,qhd->khd", chance_low, grad_out, preferred_element_type=jnp.float32
        )
        grad_query = lax.dynamic_update_slice_in_dim(
            grad_query, query_part.reshape(rows_here, span), start, 1
        )
        term = lax.dynamic_update_slice_in_dim(term, key_part.reshape(keys_all, span), start, 1)
        term = lax.dynamic_update_slice_in_dim(
            term, value_part.reshape(keys_all, span), width + start, 1
        )
        return (grad_query, term)

    initial = (
        jnp.zeros((rows_here, width), jnp.float32),
        jnp.zeros((keys_all, 2 * width), jnp.float32),
    )
    return lax.fori_loop(0, HEADS // group, per_group, initial)


def forward_layer(entering, params, allowed):
    (
        attn_gain,
        attn_shift,
        w_qkv,
        query_bias,
        value_bias,
        w_proj,
        proj_bias,
        mlp_gain,
        mlp_shift,
        w_fc,
        fc_bias,
        w_out,
        out_bias,
    ) = params
    width = w_proj.shape[0]
    stream = entering.astype(jnp.float32)
    normed = norm_affine(
        stream, attn_gain.astype(jnp.float32), attn_shift.astype(jnp.float32)
    ).astype(jnp.bfloat16)
    project = jnp.dot(normed, w_qkv, preferred_element_type=jnp.float32)
    query_low = (project[:, :width] + query_bias.astype(jnp.float32)).astype(jnp.bfloat16)
    pairs_low = jnp.concatenate(
        [project[:, width : 2 * width], project[:, 2 * width :] + value_bias.astype(jnp.float32)], 1
    ).astype(jnp.bfloat16)
    pairs = lax.all_gather(pairs_low, "ctx", axis=0, tiled=True)
    mixed, log_totals = attend(query_low, pairs, allowed)
    mixed_low = mixed.astype(jnp.bfloat16)
    middle = stream + (
        jnp.dot(mixed_low, w_proj, preferred_element_type=jnp.float32)
        + proj_bias.astype(jnp.float32)
    )
    second = norm_affine(
        middle, mlp_gain.astype(jnp.float32), mlp_shift.astype(jnp.float32)
    ).astype(jnp.bfloat16)
    hidden = jnp.dot(second, w_fc, preferred_element_type=jnp.float32) + fc_bias.astype(jnp.float32)
    active = gelu_tanh(hidden).astype(jnp.bfloat16)
    final = middle + (
        jnp.dot(active, w_out, preferred_element_type=jnp.float32) + out_bias.astype(jnp.float32)
    )
    kept = (entering, normed, query_low, pairs_low, log_totals, mixed_low, middle, second, hidden)
    return (final.astype(jnp.bfloat16), kept)


def backward_layer(coming, kept, params, allowed):
    (
        attn_gain,
        attn_shift,
        w_qkv,
        query_bias,
        value_bias,
        w_proj,
        proj_bias,
        mlp_gain,
        mlp_shift,
        w_fc,
        fc_bias,
        w_out,
        out_bias,
    ) = params
    entering, normed, query_low, pairs_low, log_totals, mixed_low, middle, second, hidden = kept
    width = w_proj.shape[0]
    grad_final = coming.astype(jnp.float32)
    grad_out_bias = jnp.sum(grad_final, 0)
    active = gelu_tanh(hidden).astype(jnp.bfloat16)
    grad_w_out = jnp.einsum("rf,rd->fd", active, coming, preferred_element_type=jnp.float32)
    grad_active = jnp.einsum("rd,fd->rf", coming, w_out, preferred_element_type=jnp.float32)
    unused, gelu_pull = jax.vjp(gelu_tanh, hidden)
    grad_hidden = gelu_pull(grad_active)[0].astype(jnp.bfloat16)
    grad_fc_bias = jnp.sum(grad_hidden.astype(jnp.float32), 0)
    grad_w_fc = jnp.einsum("rd,rf->df", second, grad_hidden, preferred_element_type=jnp.float32)
    grad_second = jnp.einsum("rf,df->rd", grad_hidden, w_fc, preferred_element_type=jnp.float32)
    unused, second_pull = jax.vjp(
        norm_affine, middle, mlp_gain.astype(jnp.float32), mlp_shift.astype(jnp.float32)
    )
    grad_norm, grad_mlp_gain, grad_mlp_shift = second_pull(grad_second)
    grad_middle = grad_final + grad_norm
    branch_low = grad_middle.astype(jnp.bfloat16)
    grad_proj_bias = jnp.sum(branch_low.astype(jnp.float32), 0)
    grad_w_proj = jnp.einsum("rd,re->de", mixed_low, branch_low, preferred_element_type=jnp.float32)
    grad_mixed = jnp.einsum(
        "re,de->rd", branch_low, w_proj, preferred_element_type=jnp.float32
    ).astype(jnp.bfloat16)
    pairs = lax.all_gather(pairs_low, "ctx", axis=0, tiled=True)
    grad_query, term = attend_back(query_low, pairs, grad_mixed, log_totals, allowed)
    grad_pairs = lax.psum_scatter(term.astype(jnp.bfloat16), "ctx", scatter_dimension=0, tiled=True)
    query_grad_low = grad_query.astype(jnp.bfloat16)
    grad_query_bias = jnp.sum(query_grad_low.astype(jnp.float32), 0)
    grad_value_bias = jnp.sum(grad_pairs[:, width:].astype(jnp.float32), 0)
    grad_project = jnp.concatenate([query_grad_low, grad_pairs], 1)
    grad_w_qkv = jnp.einsum("rd,re->de", normed, grad_project, preferred_element_type=jnp.float32)
    grad_normed = jnp.einsum("re,de->rd", grad_project, w_qkv, preferred_element_type=jnp.float32)
    unused, first_pull = jax.vjp(
        norm_affine,
        entering.astype(jnp.float32),
        attn_gain.astype(jnp.float32),
        attn_shift.astype(jnp.float32),
    )
    grad_entry, grad_attn_gain, grad_attn_shift = first_pull(grad_normed)
    grads = (
        grad_attn_gain,
        grad_attn_shift,
        grad_w_qkv,
        grad_query_bias,
        grad_value_bias,
        grad_w_proj,
        grad_proj_bias,
        grad_mlp_gain,
        grad_mlp_shift,
        grad_w_fc,
        grad_fc_bias,
        grad_w_out,
        grad_out_bias,
    )
    return (grad_middle + grad_entry, grads)


def body(
    feed,
    block_order,
    attn_gain,
    attn_shift,
    w_qkv,
    query_bias,
    value_bias,
    w_proj,
    proj_bias,
    mlp_gain,
    mlp_shift,
    w_fc,
    fc_bias,
    w_out,
    out_bias,
):
    shards = (
        attn_gain,
        attn_shift,
        w_qkv,
        query_bias,
        value_bias,
        w_proj,
        proj_bias,
        mlp_gain,
        mlp_shift,
        w_fc,
        fc_bias,
        w_out,
        out_bias,
    )
    gathered = (
        lax.all_gather(attn_gain, "wt", axis=1, tiled=True),
        lax.all_gather(attn_shift, "wt", axis=1, tiled=True),
        lax.all_gather(w_qkv, "wt", axis=1, tiled=True),
        lax.all_gather(query_bias, "wt", axis=1, tiled=True),
        lax.all_gather(value_bias, "wt", axis=1, tiled=True),
        lax.all_gather(w_proj, "wt", axis=1, tiled=True),
        lax.all_gather(proj_bias, "wt", axis=1, tiled=True),
        lax.all_gather(mlp_gain, "wt", axis=1, tiled=True),
        lax.all_gather(mlp_shift, "wt", axis=1, tiled=True),
        lax.all_gather(w_fc, "wt", axis=1, tiled=True),
        lax.all_gather(fc_bias, "wt", axis=1, tiled=True),
        lax.all_gather(w_out, "wt", axis=1, tiled=True),
        lax.all_gather(out_bias, "wt", axis=1, tiled=True),
    )
    params = tuple((piece[0] for piece in gathered))
    first_section = lax.axis_index("section") == 0
    micro = feed.shape[1]
    rows_here = feed.shape[3]
    block = rows_here // 2
    ctx_count = lax.axis_size("ctx")
    length = rows_here * ctx_count
    pos_query = positions(block_order, 2 * lax.axis_index("ctx"), rows_here, block)
    pos_key = positions(block_order, 0, length, block)
    allowed = pos_key[None, :] <= pos_query[:, None]
    local = feed[0, :, 0]
    received = jnp.zeros_like(local[0])
    forward_out = []
    kept_all = []
    for tick in range(micro + 1):
        entering = jnp.where(first_section, local[min(tick, micro - 1)], received)
        leaving, kept = forward_layer(entering, params, allowed)
        forward_out.append(leaving)
        kept_all.append(kept)
        if tick < micro:
            received = passed_along(leaving, "section", 1)

    def pick(early, late):
        return jnp.where(first_section, early, late)

    totals = tuple((jnp.zeros(piece.shape[1:], jnp.float32) for piece in shards))
    returned = jnp.zeros_like(local[0])
    grads_in = []
    for tick in range(micro + 1):
        coming = jnp.where(first_section, returned, local[min(tick, micro - 1)])
        kept = jax.tree.map(pick, kept_all[max(tick - 1, 0)], kept_all[min(tick + 1, micro)])
        grad_in, grads = backward_layer(coming, kept, params, allowed)
        useful = jnp.where(first_section, tick >= 1, tick < micro)
        grads = tuple((jnp.where(useful, piece, 0.0) for piece in grads))
        grad_low = grad_in.astype(jnp.bfloat16)
        grads_in.append(grad_low)
        shares = jax.tree.map(
            lambda part: part.astype(jnp.float32),
            lax.psum_scatter(shortened(grads), "wt", scatter_dimension=0, tiled=True),
        )
        totals = tuple((before + after for before, after in zip(totals, shares)))
        if tick < micro:
            returned = passed_along(grad_low, "section", -1)
    summed = jax.tree.map(lambda part: part.astype(jnp.float32), lax.psum(shortened(totals), "ctx"))
    result = jnp.where(first_section, jnp.stack(grads_in[1:]), jnp.stack(forward_out[1:]))
    result = result.reshape(1, micro, 1, rows_here, result.shape[-1])
    return (result,) + tuple((piece[None] for piece in summed))


def solution(mesh):
    return jax.shard_map(
        body,
        mesh=mesh,
        in_specs=(
            P("section", None, "wt", "ctx", None),
            P(),
            P("section", "wt"),
            P("section", "wt"),
            P("section", "wt", None),
            P("section", "wt"),
            P("section", "wt"),
            P("section", "wt", None),
            P("section", "wt"),
            P("section", "wt"),
            P("section", "wt"),
            P("section", "wt", None),
            P("section", "wt"),
            P("section", "wt", None),
            P("section", "wt"),
        ),
        out_specs=(
            P("section", None, "wt", "ctx", None),
            P("section", "wt"),
            P("section", "wt"),
            P("section", "wt", None),
            P("section", "wt"),
            P("section", "wt"),
            P("section", "wt", None),
            P("section", "wt"),
            P("section", "wt"),
            P("section", "wt"),
            P("section", "wt", None),
            P("section", "wt"),
            P("section", "wt", None),
            P("section", "wt"),
        ),
        check_vma=False,
    )
```

profile of v0, /device:TPU:1, one launch (start us, length us, event | category | flops | bytes accessed | tf_op | source)
XLA Modules:
  0.0 5664.4 jit_solution(5115425042290599788)
XLA Ops:
  12.5 17.2 all-reduce.37
  31.1 248.1 %all-gather.13.cloned.1.call-done = bf16[1,1600,4800]{2,1,0:T(8,128)(2,1)} async-done(((bf16[1,400,4800]{2,1,0:T(8,128)(2,1)}), bf16[1,1600,4800]{2,1,0:T(8,128)(2,1)}) %all-gather.13.cloned.1.call-update) | async-done | bytes 15360016 | tf_op jit(solution)/shard_map/all_gather | solution.py:299
  279.2 14.7 fusion.79
  302.6 11.0 all-gather.11.cloned.1.call-start
  314.0 34.8 all-gather.15.cloned.1.call-done
  349.7 43.0 while.108
  392.7 56.8 %all-gather.17.cloned.1.call-done = bf16[1,1600,1600]{2,1,0:T(8,128)(2,1)} async-done(((bf16[1,400,1600]{2,1,0:T(8,128)(2,1)}), bf16[1,1600,1600]{2,1,0:T(8,128)(2,1)}) %all-gather.17.cloned.1.call-update) | async-done | bytes 5120016 | tf_op jit(solution)/shard_map/all_gather | solution.py:302
  455.0 343.0 %all-gather.19.cloned.1.call-done = bf16[1,1600,6400]{2,1,0:T(8,128)(2,1)} async-done(((bf16[1,400,6400]{2,1,0:T(8,128)(2,1)}), bf16[1,1600,6400]{2,1,0:T(8,128)(2,1)}) %all-gather.19.cloned.1.call-update) | async-done | bytes 20480016 | tf_op jit(solution)/shard_map/all_gather | solution.py:306
  798.0 12.7 fusion.81
  810.7 349.6 %all-gather.11.cloned.1.call-done = bf16[1,6400,1600]{2,1,0:T(8,128)(2,1)} async-done(((bf16[1,1600,1600]{2,1,0:T(8,128)(2,1)}), bf16[1,6400,1600]{2,1,0:T(8,128)(2,1)}) %all-gather.11.cloned.1.call-update) | async-done | bytes 20480016 | tf_op jit(solution)/shard_map/all_gather | solution.py:308
  1160.3 17.4 fusion.241
  1181.0 17.0 collective-permute-done
  1200.4 14.8 fusion.77
  1223.6 49.2 all-gather.21.cloned.1.call-done
  1273.8 42.8 while.109
  1322.9 12.7 fusion.84
  1335.6 17.5 fusion.236
  1356.3 17.6 collective-permute-done.2
  1377.5 14.8 fusion.73
  1401.5 22.3 convert_reduce_fusion.1
  1424.4 26.6 all-gather.25.cloned.1.call-done
  1451.9 42.9 while.111
  1504.5 13.0 multiply_reduce_fusion.5
  1528.4 83.8 %while.110 = (s32[]{:T(128)}, bf16[256,1600]{0,1:T(8,128)(2,1)}, bf16[1024,3200]{0,1:T(8,128)(2,1)}, bf16[1024,3200]{0,1:T(8,128)(2,1)}, bf16[256,1600]{0,1:T(8,...) while((s32[]{:T(128)}, bf16[256,1600]{0,1:T(8,128)(2,1)}, ...), condition=%wide.region_24.25_spmd.clone, body=%wide.region_22.24_spmd.clone.sunk | while | flops 859601664 | bytes 66462088 | solution.py:143
  1614.5 57.7 %reduce-scatter.16.cloned.1.call-done = bf16[256,3200]{0,1:T(8,128)(2,1)} async-done(((bf16[1024,3200]{0,1:T(8,128)(2,1)}), bf16[256,3200]{0,1:T(8,128)(2,1)}) %reduce-scatter.16.cloned.1.call-update) | async-done | bytes 1638416 | tf_op jit(solution)/shard_map/reduce_scatter | solution.py:232
  1672.2 10.7 fusion.409
  1689.2 9.9 fusion.87
  1700.8 8.5 collective-permute-done.1
  1711.4 20.5 fusion.429
  1731.9 14.3 multiply_reduce_fusion.4
  1759.3 84.5 %while.112 = (s32[]{:T(128)}, bf16[256,1600]{0,1:T(8,128)(2,1)}, bf16[1024,3200]{0,1:T(8,128)(2,1)}, bf16[1024,3200]{0,1:T(8,128)(2,1)}, bf16[256,1600]{0,1:T(8,...) while((s32[]{:T(128)}, bf16[256,1600]{0,1:T(8,128)(2,1)}, ...), condition=%wide.region_44.45_spmd.clone, body=%wide.region_42.44_spmd.clone.sunk | while | flops 859601664 | bytes 66462088 | solution.py:143
  1844.5 59.5 %reduce-scatter.18.cloned.1.call-done = bf16[256,3200]{0,1:T(8,128)(2,1)} async-done(((bf16[1024,3200]{0,1:T(8,128)(2,1)}), bf16[256,3200]{0,1:T(8,128)(2,1)}) %reduce-scatter.18.cloned.1.call-update) | async-done | bytes 1638416 | tf_op jit(solution)/shard_map/reduce_scatter | solution.py:232
  1904.0 10.5 fusion.410
  1919.3 19.6 collective-permute-done.3
  1941.1 20.2 convert_reduce_fusion
  1961.3 13.7 multiply_reduce_fusion.3
  1986.4 84.4 %while.113 = (s32[]{:T(128)}, bf16[256,1600]{0,1:T(8,128)(2,1)S(1)}, bf16[1024,3200]{0,1:T(8,128)(2,1)}, bf16[1024,3200]{0,1:T(8,128)(2,1)}, bf16[256,1600]{0,1:...) while((s32[]{:T(128)}, bf16[256,1600]{0,1:T(8,128)(2,1)S(1)}, ...), condition=%wide.region_56.57_spmd.clone, body=%wide.region_54.56_spmd.clone.sunk | while | flops 859601664 | bytes 66462088 | solution.py:143
  2091.8 13.5 select_convert_fusion.3
  2105.5 12.3 convolution_convert_fusion.1
  2118.9 12.2 select_convert_fusion.2
  2132.5 14.1 select_convert_fusion.1
  2147.8 13.7 convolution_convert_fusion
  2162.7 14.2 select_convert_fusion
  2178.3 9.8 select_convert_fusion.5
  2189.2 9.9 convolution_convert_fusion.2
  2200.2 10.1 select_convert_fusion.4
  2228.9 98.1 %reduce-scatter.30.cloned.1.call-done = bf16[400,1600]{1,0:T(8,128)(2,1)} async-done(((bf16[1600,1600]{1,0:T(8,128)(2,1)}), bf16[400,1600]{1,0:T(8,128)(2,1)}) %reduce-scatter.30.cloned.1.call-update) | async-done | bytes 1280016 | tf_op jit(solution)/shard_map/reduce_scatter | solution.py:349
  2327.0 98.1 %reduce-scatter.32.cloned.1.call-done = bf16[400,1600]{1,0:T(8,128)(2,1)} async-done(((bf16[1600,1600]{1,0:T(8,128)(2,1)}), bf16[400,1600]{1,0:T(8,128)(2,1)}) %reduce-scatter.32.cloned.1.call-update) | async-done | bytes 1280016 | tf_op jit(solution)/shard_map/reduce_scatter | solution.py:349
  2430.2 9.8 fusion.411
  2442.7 324.9 %reduce-scatter.34.cloned.1.call-done = bf16[400,6400]{1,0:T(8,128)(2,1)} async-done(((bf16[1600,6400]{1,0:T(8,128)(2,1)}), bf16[400,6400]{1,0:T(8,128)(2,1)}) %reduce-scatter.34.cloned.1.call-update) | async-done | bytes 5120016 | tf_op jit(solution)/shard_map/reduce_scatter | solution.py:349
  2767.6 343.0 %reduce-scatter.36.cloned.1.call-done = bf16[400,6400]{1,0:T(8,128)(2,1)} async-done(((bf16[1600,6400]{1,0:T(8,128)(2,1)}), bf16[400,6400]{1,0:T(8,128)(2,1)}) %reduce-scatter.36.cloned.1.call-update) | async-done | bytes 5120016 | tf_op jit(solution)/shard_map/reduce_scatter | solution.py:349
  3110.6 343.2 %reduce-scatter.38.cloned.1.call-done = bf16[400,6400]{1,0:T(8,128)(2,1)} async-done(((bf16[1600,6400]{1,0:T(8,128)(2,1)}), bf16[400,6400]{1,0:T(8,128)(2,1)}) %reduce-scatter.38.cloned.1.call-update) | async-done | bytes 5120016 | tf_op jit(solution)/shard_map/reduce_scatter | solution.py:349
  3453.9 9.6 fusion.154
  3463.4 346.6 %reduce-scatter.40.cloned.1.call-done = bf16[1600,1600]{1,0:T(8,128)(2,1)} async-done(((bf16[6400,1600]{1,0:T(8,128)(2,1)}), bf16[1600,1600]{1,0:T(8,128)(2,1)}) %reduce-scatter.40.cloned.1.call-update) | async-done | bytes 5120016 | tf_op jit(solution)/shard_map/reduce_scatter | solution.py:349
  3810.1 357.0 %reduce-scatter.42.cloned.1.call-done = bf16[1600,1600]{1,0:T(8,128)(2,1)} async-done(((bf16[6400,1600]{1,0:T(8,128)(2,1)}), bf16[1600,1600]{1,0:T(8,128)(2,1)}) %reduce-scatter.42.cloned.1.call-update) | async-done | bytes 5120016 | tf_op jit(solution)/shard_map/reduce_scatter | solution.py:349
  4167.1 357.0 %reduce-scatter.44.cloned.1.call-done = bf16[1600,1600]{1,0:T(8,128)(2,1)} async-done(((bf16[6400,1600]{1,0:T(8,128)(2,1)}), bf16[1600,1600]{1,0:T(8,128)(2,1)}) %reduce-scatter.44.cloned.1.call-update) | async-done | bytes 5120016 | tf_op jit(solution)/shard_map/reduce_scatter | solution.py:349
  4524.1 9.9 fusion.141
  4534.0 254.6 %reduce-scatter.22.cloned.1.call-done = bf16[400,4800]{1,0:T(8,128)(2,1)} async-done(((bf16[1600,4800]{1,0:T(8,128)(2,1)}), bf16[400,4800]{1,0:T(8,128)(2,1)}) %reduce-scatter.22.cloned.1.call-update) | async-done | bytes 3840016 | tf_op jit(solution)/shard_map/reduce_scatter | solution.py:349
  4788.6 263.7 %reduce-scatter.24.cloned.1.call-done = bf16[400,4800]{1,0:T(8,128)(2,1)} async-done(((bf16[1600,4800]{1,0:T(8,128)(2,1)}), bf16[400,4800]{1,0:T(8,128)(2,1)}) %reduce-scatter.24.cloned.1.call-update) | async-done | bytes 3840016 | tf_op jit(solution)/shard_map/reduce_scatter | solution.py:349
  5052.3 263.8 %reduce-scatter.26.cloned.1.call-done = bf16[400,4800]{1,0:T(8,128)(2,1)} async-done(((bf16[1600,4800]{1,0:T(8,128)(2,1)}), bf16[400,4800]{1,0:T(8,128)(2,1)}) %reduce-scatter.26.cloned.1.call-update) | async-done | bytes 3840016 | tf_op jit(solution)/shard_map/reduce_scatter | solution.py:349
  5325.0 17.9 fusion.255
  5347.8 14.8 all-reduce.43.cloned.1.call-done
  5369.7 12.3 all-reduce.38
  5387.2 253.0 %all-reduce.45.cloned.1.call-done = (bf16[1,400,4800]{2,1,0:T(8,128)(2,1)}, bf16[1,400,1600]{2,1,0:T(8,128)(2,1)}, bf16[1,400,6400]{2,1,0:T(8,128)(2,1)}, bf16[1,1600,1600]{2,1,0:T(8,128)(2,1)}) async-done(((bf16[1,400,4800]{2,1,0:T(8,128)(2,1)}, bf16[1,400,1600]{2,1,0:T(8,128)(2,1)}, bf16[1,400,6400]{2,1,0:T(8,128)(2,1)}, bf16[1,1600,1600]{2,1,0:T(8,128)(2,1)}), (bf16[1,400,4800]{2,1,0:T(8,128)(2,1)}, ...) | async-done | bytes 15360016 | tf_op jit(solution)/shard_map/psum | solution.py:354
  (970 shorter events, 599.8 us)
Async XLA Ops:
  7.3 22.5 copy-start.3
  7.3 271.9 %all-gather.13.cloned.1.call-start = ((), (), s32[]{:S(2)}) async-start(), calls=%async_computation.16 | async-start | bytes 19456000 | tf_op jit(solution)/shard_map/all_gather | solution.py:299
  8.0 340.7 %all-gather.15.cloned.1.call-start = ((), (), s32[]{:S(2)}) async-start(), calls=%async_computation.17 | async-start | bytes 8192000 | tf_op jit(solution)/shard_map/all_gather | solution.py:172
  29.7 1347.8 %copy-start.96 = (f32[1600]{0:T(1024)}, f32[1600]{0:T(1024)S(1)}, u32[]{:S(2)}) copy-start(f32[1600]{0:T(1024)S(1)} %add.1206) | copy-start | bytes 19204
  29.7 1347.8 %copy-start.70 = (f32[1600]{0:T(1024)}, f32[1600]{0:T(1024)S(1)}, u32[]{:S(2)}) copy-start(f32[1600]{0:T(1024)S(1)} %mul.1063) | copy-start | bytes 19204
  30.0 263.9 %copy-start.99 = (f32[256]{0:T(256)}, f32[256]{0:T(256)S(1)}, u32[]{:S(2)}) copy-start(f32[256]{0:T(256)S(1)} %broadcast_multiply_fusion.11) | copy-start | bytes 3076
  31.1 262.8 %copy-start.123 = (f32[256]{0:T(256)}, f32[256]{0:T(256)S(1)}, u32[]{:S(2)}) copy-start(f32[256]{0:T(256)S(1)} %add_rsqrt_fusion.5) | copy-start | bytes 3076
  301.2 148.3 %all-gather.17.cloned.1.call-start = ((), (), s32[]{:S(2)}) async-start(), calls=%async_computation.18 | async-start | bytes 6656000 | tf_op jit(solution)/shard_map/all_gather | solution.py:302
  302.0 496.0 %all-gather.19.cloned.1.call-start = ((), (), s32[]{:S(2)}) async-start(), calls=%async_computation.19 | async-start | bytes 25600000 | tf_op jit(solution)/shard_map/all_gather | solution.py:306
  302.6 857.7 %all-gather.11.cloned.1.call-start = ((), (), s32[]{:S(2)}) async-start(), calls=%async_computation.15 | async-start | bytes 26624000 | tf_op jit(solution)/shard_map/all_gather | solution.py:308
  313.6 959.2 %all-gather.21.cloned.1.call-start = ((), (), s32[]{:S(2)}) async-start(), calls=%async_computation.20 | async-start | bytes 8192000 | tf_op jit(solution)/shard_map/all_gather | solution.py:172
  313.7 1009.2 %copy-start.68 = (f32[6400]{0:T(1024)}, f32[6400]{0:T(1024)S(1)}, u32[]{:S(2)}) copy-start(f32[6400]{0:T(1024)S(1)} %add.1211) | copy-start | bytes 76804
  313.7 1187.1 %copy-start.59 = (f32[1600]{0:T(1024)}, f32[1600]{0:T(1024)S(1)}, u32[]{:S(2)}) copy-start(f32[1600]{0:T(1024)S(1)} %add.1210) | copy-start | bytes 19204
  313.7 1021.9 %copy-start.94 = (f32[1600]{0:T(1024)}, f32[1600]{0:T(1024)S(1)}, u32[]{:S(2)}) copy-start(f32[1600]{0:T(1024)S(1)} %add.1212) | copy-start | bytes 19204
  392.7 56.8 %copy-start.73 = (f32[25,256]{1,0:T(8,128)}, f32[25,256]{1,0:T(8,128)S(1)}, u32[]{:S(2)}) copy-start(f32[25,256]{1,0:T(8,128)S(1)} %get-tuple-element.1078) | copy-start | bytes 76804
  454.7 705.6 %copy-start = (f32[256,1600]{0,1:T(8,128)}, f32[256,1600]{0,1:T(8,128)S(1)}, u32[]{:S(2)}) copy-start(f32[256,1600]{0,1:T(8,128)S(1)} %get-tuple-element.1469) | copy-start | bytes 4915204
  454.7 356.0 %copy-start.77 = (f32[256]{0:T(256)}, f32[256]{0:T(256)S(1)}, u32[]{:S(2)}) copy-start(f32[256]{0:T(256)S(1)} %broadcast_multiply_fusion.10) | copy-start | bytes 3076
  455.0 355.7 %copy-start.79 = (f32[256]{0:T(256)}, f32[256]{0:T(256)S(1)}, u32[]{:S(2)}) copy-start(f32[256]{0:T(256)S(1)} %add_rsqrt_fusion.4) | copy-start | bytes 3076
  1177.7 20.3 collective-permute-start
  1199.9 15.4 copy-start.22
  1200.4 16.6 copy-start.27
  1223.1 227.9 %all-gather.25.cloned.1.call-start = ((), (), s32[]{:S(2)}) async-start(), calls=%async_computation.23 | async-start | bytes 8192000 | tf_op jit(solution)/shard_map/all_gather | solution.py:172
  1353.1 20.8 collective-permute-start.2
  1377.0 15.4 copy-start.24
  1377.5 16.6 copy-start.46
  1401.5 122.3 %all-gather.23.cloned.1.call-start = ((), (), s32[]{:S(2)}) async-start(), calls=%async_computation.21 | async-start | bytes 8192000 | tf_op jit(solution)/shard_map/all_gather | solution.py:230
  1423.9 248.3 %reduce-scatter.16.cloned.1.call-start = ((), (), s32[]{:S(2)}) async-start(), calls=%async_computation.22 | async-start | bytes 8192000 | tf_op jit(solution)/shard_map/reduce_scatter | solution.py:232
  1504.2 17.0 slice-start.15
  1504.5 16.7 slice-start.16
  1612.2 60.0 %copy-start.30 = (bf16[256,1600]{0,1:T(8,128)(2,1)S(1)}, bf16[256,1600]{0,1:T(8,128)(2,1)}, u32[]{:S(2)}) copy-start(bf16[256,1600]{0,1:T(8,128)(2,1)} %get-tuple-element.1405) | copy-start | bytes 2457604
  1612.2 60.0 %copy-start.71 = (f32[1600]{0:T(1024)S(1)}, f32[1600]{0:T(1024)}, u32[]{:S(2)}) copy-start(f32[1600]{0:T(1024)} %copy-done.70) | copy-start | bytes 19204
  1612.2 142.5 %all-gather.27.cloned.1.call-start = ((), (), s32[]{:S(2)}) async-start(), calls=%async_computation.24 | async-start | bytes 8192000 | tf_op jit(solution)/shard_map/all_gather | solution.py:230
  1614.4 289.6 %reduce-scatter.18.cloned.1.call-start = ((), (), s32[]{:S(2)}) async-start(), calls=%async_computation.25 | async-start | bytes 8192000 | tf_op jit(solution)/shard_map/reduce_scatter | solution.py:232
  1672.2 16.9 slice-start.6
  1672.2 16.9 slice-start.7
  1672.2 16.9 slice-start.8
  1672.2 16.9 slice-start.9
  1687.8 21.5 collective-permute-start.1
  1711.4 35.2 copy-start.19
  1711.4 20.5 copy-start.18
  1843.8 60.2 %copy-start.38 = (bf16[256,1600]{0,1:T(8,128)(2,1)S(1)}, bf16[256,1600]{0,1:T(8,128)(2,1)}, u32[]{:S(2)}) copy-start(bf16[256,1600]{0,1:T(8,128)(2,1)} %get-tuple-element.1399) | copy-start | bytes 2457604
  1843.8 60.2 %copy-start.56 = (bf16[256,1600]{0,1:T(8,128)(2,1)S(1)}, bf16[256,1600]{0,1:T(8,128)(2,1)}, u32[]{:S(2)}) copy-start(bf16[256,1600]{0,1:T(8,128)(2,1)} %get-tuple-element.1084) | copy-start | bytes 2457604
  1843.8 138.9 %all-gather.29.cloned.1.call-start = ((), (), s32[]{:S(2)}) async-start(), calls=%async_computation.26 | async-start | bytes 8192000 | tf_op jit(solution)/shard_map/all_gather | solution.py:230
  1844.4 354.7 %reduce-scatter.20.cloned.1.call-start = ((), (), s32[]{:S(2)}) async-start(), calls=%async_computation.27 | async-start | bytes 8192000 | tf_op jit(solution)/shard_map/reduce_scatter | solution.py:232
  1917.8 21.2 collective-permute-start.3
  1941.1 34.5 copy-start.43
  2071.7 157.3 %reduce-scatter.28.cloned.1.call-start = ((), (), s32[]{:S(2)}) async-start(), calls=%async_computation.31 | async-start | bytes 6656000 | tf_op jit(solution)/shard_map/reduce_scatter | solution.py:349
  2078.2 248.8 %reduce-scatter.30.cloned.1.call-start = ((), (), s32[]{:S(2)}) async-start(), calls=%async_computation.32 | async-start | bytes 6656000 | tf_op jit(solution)/shard_map/reduce_scatter | solution.py:349
  2084.7 340.4 %reduce-scatter.32.cloned.1.call-start = ((), (), s32[]{:S(2)}) async-start(), calls=%async_computation.33 | async-start | bytes 6656000 | tf_op jit(solution)/shard_map/reduce_scatter | solution.py:349
  2090.0 677.7 %reduce-scatter.34.cloned.1.call-start = ((), (), s32[]{:S(2)}) async-start(), calls=%async_computation.34 | async-start | bytes 25600000 | tf_op jit(solution)/shard_map/reduce_scatter | solution.py:349
  2105.4 1005.2 %reduce-scatter.36.cloned.1.call-start = ((), (), s32[]{:S(2)}) async-start(), calls=%async_computation.35 | async-start | bytes 25600000 | tf_op jit(solution)/shard_map/reduce_scatter | solution.py:349
  2117.7 1336.1 %reduce-scatter.38.cloned.1.call-start = ((), (), s32[]{:S(2)}) async-start(), calls=%async_computation.36 | async-start | bytes 25600000 | tf_op jit(solution)/shard_map/reduce_scatter | solution.py:349
  2131.1 1679.0 %reduce-scatter.40.cloned.1.call-start = ((), (), s32[]{:S(2)}) async-start(), calls=%async_computation.37 | async-start | bytes 26624000 | tf_op jit(solution)/shard_map/reduce_scatter | solution.py:349
  2146.7 2020.4 %reduce-scatter.42.cloned.1.call-start = ((), (), s32[]{:S(2)}) async-start(), calls=%async_computation.38 | async-start | bytes 26624000 | tf_op jit(solution)/shard_map/reduce_scatter | solution.py:349
  2161.6 2362.5 %reduce-scatter.44.cloned.1.call-start = ((), (), s32[]{:S(2)}) async-start(), calls=%async_computation.39 | async-start | bytes 26624000 | tf_op jit(solution)/shard_map/reduce_scatter | solution.py:349
  2177.0 2611.6 %reduce-scatter.22.cloned.1.call-start = ((), (), s32[]{:S(2)}) async-start(), calls=%async_computation.28 | async-start | bytes 19456000 | tf_op jit(solution)/shard_map/reduce_scatter | solution.py:349
  2188.1 2864.2 %reduce-scatter.24.cloned.1.call-start = ((), (), s32[]{:S(2)}) async-start(), calls=%async_computation.29 | async-start | bytes 19456000 | tf_op jit(solution)/shard_map/reduce_scatter | solution.py:349
  2199.1 3117.0 %reduce-scatter.26.cloned.1.call-start = ((), (), s32[]{:S(2)}) async-start(), calls=%async_computation.30 | async-start | bytes 19456000 | tf_op jit(solution)/shard_map/reduce_scatter | solution.py:349
  2210.4 3152.2 %all-reduce.43.cloned.1.call-start = ((), (), s32[]{:S(2)}) async-start(), calls=%async_computation.40 | async-start | bytes 282624
  2220.2 210.0 %copy-start.42 = (bf16[256,1600]{0,1:T(8,128)(2,1)S(1)}, bf16[256,1600]{0,1:T(8,128)(2,1)}, u32[]{:S(2)}) copy-start(bf16[256,1600]{0,1:T(8,128)(2,1)} %get-tuple-element.1390) | copy-start | bytes 2457604
  2442.7 3197.5 %all-reduce.45.cloned.1.call-start = ((), (), s32[]{:S(2)}) async-start(), calls=%async_computation.41 | async-start | bytes 31334400 | tf_op jit(solution)/shard_map/psum | solution.py:354
  5325.0 18.0 copy-start.12
  5325.0 18.0 copy-start.45
  5325.0 18.0 copy-start.93
  (151 other events, 585.0 us)
Sparse Core Ops, SparseCore 0:
  9.7 269.4 all-gather.12
  301.4 47.3 all-gather.14
  350.3 99.1 all-gather.16
  450.9 347.0 all-gather.18
  799.4 360.8 all-gather.10
  1223.2 49.5 all-gather.20
  1401.6 49.3 all-gather.24
  1452.5 48.7 all-gather.22
  1612.3 59.8 reduce-scatter.15
  1673.7 49.1 all-gather.26
  1844.0 59.9 reduce-scatter.17
  1905.9 49.1 all-gather.28
  2070.9 60.3 reduce-scatter.19
  2133.6 95.3 reduce-scatter.27
  2231.2 95.7 reduce-scatter.29
  2329.3 95.7 reduce-scatter.31
  2427.4 340.1 reduce-scatter.33
  2769.9 340.7 reduce-scatter.35
  3113.1 340.7 reduce-scatter.37
  3456.1 353.9 reduce-scatter.39
  3812.5 354.6 reduce-scatter.41
  4169.5 354.5 reduce-scatter.43
  4526.5 262.0 reduce-scatter.21
  4790.9 261.3 reduce-scatter.23
  5054.7 261.3 reduce-scatter.25
  5321.8 40.8 all-reduce.42
  5366.4 273.7 all-reduce.44
where the time goes:
time: 5680 us; the launch traced here: 5660 us
  waiting for transfers between devices  4610 us (81%)
  matrix products  617 us (11%)
  other arithmetic  182 us (3%)
  local copies, waits for them, and re-layouts  179 us (3%)
    reduce_scatter x12, waiting for transfers between devices, body(): lax.psum_scatter(shortened(grads), 'wt', scatter_dimension=0, tiled=True)  3060 us
    all_gather x1, waiting for transfers between devices, body(): lax.all_gather(w_out, 'wt', axis=1, tiled=True)  350 us
    all_gather x1, waiting for transfers between devices, body(): lax.all_gather(w_fc, 'wt', axis=1, tiled=True)  343 us
    psum x1, waiting for transfers between devices, body(): lax.psum(shortened(totals), 'ctx')  253 us
    all_gather x1, waiting for transfers between devices, body(): lax.all_gather(w_qkv, 'wt', axis=1, tiled=True)  248 us
    reduce_scatter x3, waiting for transfers between devices, backward_layer(): lax.psum_scatter(term.astype(jnp.bfloat16), 'ctx', scatter_dimension=0, t...  117 us
  transfers between devices with their start and end apart: 31, of which 27 were waited for; matrix products, arithmetic and copies ran while one was open for 9% of the time, Pallas kernels for 0%

commit v1 on v0

v1 whole, which is shorter than its diff:
```python
import functools
import math

import jax
import jax.numpy as jnp
from jax import lax
from jax.experimental import pallas as pl
from jax.experimental.pallas import tpu as pltpu
from jax.sharding import PartitionSpec as P

HEAD_DIM = 64
NEG = -1000000000.0
LANES = 128


def nt_dot(left, right):
    return lax.dot_general(left, right, (((1,), (1,)), ((), ())), preferred_element_type=jnp.float32)


def nn_dot(left, right):
    return jnp.dot(left, right, preferred_element_type=jnp.float32)


def causal_scores(keys, query, tile):
    scores = nt_dot(keys, query)
    edge = scores.shape[0] - tile
    key_at = lax.broadcasted_iota(jnp.int32, (tile, tile), 0)
    query_at = lax.broadcasted_iota(jnp.int32, (tile, tile), 1)
    last = jnp.where(key_at <= query_at, scores[edge:], NEG)
    return jnp.concatenate([scores[:edge], last], 0) if edge else last


def attend_kernel(block, tile, heads, place, qkv, out, log_total, query, keyed, valued, mixed):
    length, three = qkv.shape
    span = three // 3
    lane = lax.broadcasted_iota(jnp.int32, (tile, LANES), 1)

    def pair(index, carry):
        start = pl.multiple_of(index * LANES, LANES)
        for at in range(length // block):
            rows = pl.ds(pl.multiple_of(place[at] * block, block), block)
            here = pl.ds(at * block, block)
            query[here, :] = qkv[rows, pl.ds(start, LANES)] * (HEAD_DIM ** (-0.5))
            keyed[here, :] = qkv[rows, pl.ds(span + start, LANES)]
            valued[:, here] = qkv[rows, pl.ds(2 * span + start, LANES)].T

        for half in range(2):

            @pl.when(2 * index + half < heads)
            def _():
                mine = (lane < HEAD_DIM) if half == 0 else (lane >= HEAD_DIM)
                features = slice(half * HEAD_DIM, (half + 1) * HEAD_DIM)
                for at in range(length // tile):
                    seen = (at + 1) * tile
                    cols = slice(at * tile, seen)
                    part = jnp.where(mine, query[cols, :], 0)
                    scores = causal_scores(keyed[:seen, :], part, tile)
                    highest = jnp.max(scores, 0, keepdims=True)
                    exponent = jnp.exp(scores - highest)
                    total = jnp.sum(exponent, 0, keepdims=True)
                    result = nn_dot(valued[features, :seen], exponent.astype(jnp.bfloat16))
                    mixed[features, cols] = result * (1.0 / total)
                    log_total[pl.ds(2 * index + half, 1), cols] = highest + jnp.log(total)

        for at in range(length // block):
            rows = pl.ds(pl.multiple_of(place[at] * block, block), block)
            out[rows, pl.ds(start, LANES)] = mixed[:, at * block : (at + 1) * block].T.astype(out.dtype)
        return carry

    mixed[...] = jnp.zeros_like(mixed)
    lax.fori_loop(0, span // LANES, pair, 0)


def attend(place, qkv, heads, block):
    length, three = qkv.shape
    span = three // 3
    tile = min(256, length)
    rows = -(-span // HEAD_DIM // 8) * 8
    vmem = pl.BlockSpec(memory_space=pltpu.VMEM)
    return pl.pallas_call(
        functools.partial(attend_kernel, block, tile, heads),
        out_shape=(
            jax.ShapeDtypeStruct((length, span), jnp.bfloat16),
            jax.ShapeDtypeStruct((rows, length), jnp.float32),
        ),
        in_specs=[pl.BlockSpec(memory_space=pltpu.SMEM), vmem],
        out_specs=(vmem, vmem),
        scratch_shapes=[
            pltpu.VMEM((length, LANES), jnp.bfloat16),
            pltpu.VMEM((length, LANES), jnp.bfloat16),
            pltpu.VMEM((LANES, length), jnp.bfloat16),
            pltpu.VMEM((LANES, length), jnp.float32),
        ],
        compiler_params=pltpu.CompilerParams(vmem_limit_bytes=40 * 1024 * 1024),
        cost_estimate=pl.CostEstimate(
            flops=3 * heads * length * length * HEAD_DIM,
            bytes_accessed=2 * length * 4 * span,
            transcendentals=heads * length * length // 2,
        ),
    )(place, qkv)


def attend_back_kernel(
    block, tile, heads, place, qkv, grad_mixed, log_total, out,
    query, keyed, keyed_t, valued, grad, grad_query, grad_key, grad_value,
):
    length, three = qkv.shape
    span = three // 3
    scale = HEAD_DIM ** (-0.5)
    lane = lax.broadcasted_iota(jnp.int32, (tile, LANES), 1)

    def pair(index, carry):
        start = pl.multiple_of(index * LANES, LANES)
        for at in range(length // block):
            rows = pl.ds(pl.multiple_of(place[at] * block, block), block)
            here = pl.ds(at * block, block)
            query[here, :] = qkv[rows, pl.ds(start, LANES)] * scale
            key_part = qkv[rows, pl.ds(span + start, LANES)]
            keyed[here, :] = key_part
            keyed_t[:, here] = key_part.T
            valued[here, :] = qkv[rows, pl.ds(2 * span + start, LANES)]
            grad[here, :] = grad_mixed[rows, pl.ds(start, LANES)]
        grad_query[...] = jnp.zeros_like(grad_query)
        grad_key[...] = jnp.zeros_like(grad_key)
        grad_value[...] = jnp.zeros_like(grad_value)

        for half in range(2):

            @pl.when(2 * index + half < heads)
            def _():
                mine = (lane < HEAD_DIM) if half == 0 else (lane >= HEAD_DIM)
                features = slice(half * HEAD_DIM, (half + 1) * HEAD_DIM)
                for at in range(length // tile):
                    seen = (at + 1) * tile
                    cols = slice(at * tile, seen)
                    part = jnp.where(mine, query[cols, :], 0)
                    grad_part = jnp.where(mine, grad[cols, :], 0)
                    scores = causal_scores(keyed[:seen, :], part, tile)
                    chance = jnp.exp(scores - log_total[pl.ds(2 * index + half, 1), cols])
                    grad_chance = nt_dot(valued[:seen, :], grad_part)
                    inner = jnp.sum(chance * grad_chance, 0, keepdims=True)
                    grad_scores = (chance * (grad_chance - inner)).astype(jnp.bfloat16)
                    grad_value[:seen, :] += nn_dot(chance.astype(jnp.bfloat16), grad_part)
                    grad_key[:seen, :] += nn_dot(grad_scores, part)
                    grad_query[features, cols] = nn_dot(keyed_t[features, :seen], grad_scores) * scale

        for at in range(length // block):
            rows = pl.ds(pl.multiple_of(place[at] * block, block), block)
            here = slice(at * block, (at + 1) * block)
            out[rows, pl.ds(start, LANES)] = grad_query[:, here].T.astype(out.dtype)
            out[rows, pl.ds(span + start, LANES)] = grad_key[here, :].astype(out.dtype)
            out[rows, pl.ds(2 * span + start, LANES)] = grad_value[here, :].astype(out.dtype)
        return carry

    lax.fori_loop(0, span // LANES, pair, 0)


def attend_back(place, qkv, grad_mixed, log_total, heads, block):
    length, three = qkv.shape
    span = three // 3
    tile = min(256, length)
    vmem = pl.BlockSpec(memory_space=pltpu.VMEM)
    return pl.pallas_call(
        functools.partial(attend_back_kernel, block, tile, heads),
        out_shape=jax.ShapeDtypeStruct((length, three), jnp.bfloat16),
        in_specs=[pl.BlockSpec(memory_space=pltpu.SMEM), vmem, vmem, vmem],
        out_specs=vmem,
        scratch_shapes=[
            pltpu.VMEM((length, LANES), jnp.bfloat16),
            pltpu.VMEM((length, LANES), jnp.bfloat16),
            pltpu.VMEM((LANES, length), jnp.bfloat16),
            pltpu.VMEM((length, LANES), jnp.bfloat16),
            pltpu.VMEM((length, LANES), jnp.bfloat16),
            pltpu.VMEM((LANES, length), jnp.float32),
            pltpu.VMEM((length, LANES), jnp.float32),
            pltpu.VMEM((length, LANES), jnp.float32),
        ],
        compiler_params=pltpu.CompilerParams(vmem_limit_bytes=48 * 1024 * 1024),
        cost_estimate=pl.CostEstimate(
            flops=7 * heads * length * length * HEAD_DIM,
            bytes_accessed=2 * length * 7 * span,
            transcendentals=heads * length * length // 2,
        ),
    )(place, qkv, grad_mixed, log_total)


EPS = 1e-05
GELU_A = math.sqrt(2.0 / math.pi)
GELU_B = 0.044715


def flip(axis, bit):
    return [(at, at ^ bit) for at in range(lax.axis_size(axis))]


def swap(value, axis, bit=1):
    return lax.ppermute(value, axis, flip(axis, bit))


def bits_of(axis):
    bits, bit = [], 1
    while bit < lax.axis_size(axis):
        bits.append(bit)
        bit *= 2
    return bits


def gathered(value, axis):
    pieces = {0: value}
    for bit in reversed(bits_of(axis)):
        for at in list(pieces):
            pieces[at | bit] = swap(pieces[at], axis, bit)
    return [pieces[at] for at in range(lax.axis_size(axis))]


def summed(pieces, axis):
    pieces = dict(enumerate(pieces))
    for bit in bits_of(axis):
        for at in sorted(pieces, reverse=True):
            if at & bit:
                came = swap(pieces.pop(at).astype(jnp.bfloat16), axis, bit)
                pieces[at ^ bit] = pieces[at ^ bit].astype(jnp.float32) + came.astype(jnp.float32)
    return pieces[0]


def exchanged(pieces, axis):
    return [swap(piece, axis, at) if at else piece for at, piece in enumerate(pieces)]


def by_owner(pieces, axis):
    here = lax.axis_index(axis)
    whole = jnp.zeros((len(pieces),) + pieces[0].shape, pieces[0].dtype)
    for at, piece in enumerate(pieces):
        whole = lax.dynamic_update_index_in_dim(whole, piece, here ^ at, 0)
    return whole


def over_wt(value, tiled=True):
    return lax.all_gather(value, "wt", axis=0, tiled=tiled)


def scatter_wt(value, tiled=True):
    return lax.psum_scatter(value, "wt", scatter_dimension=0, tiled=tiled)


def dot(left, right):
    return jnp.dot(left, right, preferred_element_type=jnp.float32)


def dot_nt(left, right):
    return lax.dot_general(left, right, (((1,), (1,)), ((), ())), preferred_element_type=jnp.float32)


def dot_tn(left, right):
    return lax.dot_general(left, right, (((0,), (0,)), ((), ())), preferred_element_type=jnp.float32)


def low(value):
    return value.astype(jnp.bfloat16)


def wide(value):
    return value.astype(jnp.float32)


def normed(values):
    center = values - jnp.mean(values, -1, keepdims=True)
    rate = lax.rsqrt(jnp.mean(center * center, -1, keepdims=True) + EPS)
    return center * rate, rate


def norm_back(grad, gain, values):
    unit, rate = normed(values)
    inner = grad * gain
    back = rate * (
        inner
        - jnp.mean(inner, -1, keepdims=True)
        - unit * jnp.mean(inner * unit, -1, keepdims=True)
    )
    return back, jnp.sum(grad * unit, 0), jnp.sum(grad, 0)


def gelu(value):
    return 0.5 * value * (1.0 + jnp.tanh(GELU_A * (value + GELU_B * value * value * value)))


def gelu_slope(value):
    square = value * value
    bend = jnp.tanh(GELU_A * (value + GELU_B * value * square))
    return 0.5 * (1.0 + bend) + 0.5 * value * (1.0 - bend * bend) * (
        GELU_A * (1.0 + 3.0 * GELU_B * square)
    )


class Plan:
    def __init__(self, width, hidden_rows):
        self.count = lax.axis_size("ctx")
        self.ci = lax.axis_index("ctx")
        self.first = lax.axis_index("section") == 0
        self.xi = lax.axis_index("section")
        self.wi = lax.axis_index("wt")
        self.width = width
        heads = width // HEAD_DIM
        stride = heads // self.count
        self.heads = heads - stride * (self.count - 1)
        self.step = stride * HEAD_DIM
        self.span = (self.heads + self.heads % 2) * HEAD_DIM
        self.padded = self.step * (self.count - 1) + self.span
        self.owned = jnp.where(self.ci == self.count - 1, self.heads, stride) * HEAD_DIM
        self.part = hidden_rows // self.count
        self.half = self.part // 2

    def padded_out(self, array):
        return jnp.pad(array, [(0, 0)] * (array.ndim - 1) + [(0, self.padded - array.shape[-1])])

    def window(self, padded, index):
        return lax.dynamic_slice_in_dim(padded, index * self.step, self.span, padded.ndim - 1)

    def joined(self, ordered):
        last = self.width - self.step * (self.count - 1)
        parts = [ordered[at, ..., : self.step] for at in range(self.count - 1)]
        return jnp.concatenate(parts + [ordered[self.count - 1, ..., :last]], -1)


def forward_layer(entering, weights, vectors, plan, place, block):
    w_qkv, w_proj, w_fc, w_out = weights
    attn_gain, attn_shift, bias_qkv, proj_bias, mlp_gain, mlp_shift, fc_bias, out_bias = vectors
    stream = wide(entering)
    first_norm = jnp.concatenate(gathered(low(normed(stream)[0] * attn_gain + attn_shift), "ctx"))
    qkv = low(dot(first_norm, w_qkv) + bias_qkv)
    mixed, log_total = attend(place, qkv, plan.heads, block)
    rows = entering.shape[0]
    pieces = [mixed[at * rows : (at + 1) * rows] for at in range(plan.count)]
    mixed_all = plan.joined(by_owner(exchanged(pieces, "ctx"), "ctx"))
    middle = stream + (dot(mixed_all, w_proj) + proj_bias)
    second_norm = jnp.concatenate(gathered(low(normed(middle)[0] * mlp_gain + mlp_shift), "ctx"))
    hidden = [dot(second_norm, part) + bias for part, bias in zip(w_fc, fc_bias)]
    active = [low(gelu(part)) for part in hidden]
    result = dot(active[0], w_out[0]) + dot(active[1], w_out[1])
    pieces = [result[at * rows : (at + 1) * rows] for at in range(plan.count)]
    final = middle + (summed(pieces, "ctx") + out_bias)
    kept = (stream, first_norm, qkv, log_total, mixed_all, middle, second_norm, hidden, active)
    return low(final), kept


def backward_layer(coming, kept, weights, vectors, plan, place, block):
    w_qkv, w_proj, w_fc, w_out = weights
    attn_gain, attn_shift, bias_qkv, proj_bias, mlp_gain, mlp_shift, fc_bias, out_bias = vectors
    stream, first_norm, qkv, log_total, mixed_all, middle, second_norm, hidden, active = kept
    rows = coming.shape[0]
    grad_final = wide(coming)
    g_out_bias = jnp.sum(grad_final, 0)
    coming_all = jnp.concatenate(gathered(coming, "ctx"))
    grad_hidden = [
        low(dot_nt(coming_all, part) * gelu_slope(at)) for part, at in zip(w_out, hidden)
    ]
    g_w_out = [low(dot_tn(part, coming_all)) for part in active]
    g_fc_bias = [jnp.sum(wide(part), 0) for part in grad_hidden]
    g_w_fc = [low(dot_tn(second_norm, part)) for part in grad_hidden]
    grad_second = dot_nt(grad_hidden[0], w_fc[0]) + dot_nt(grad_hidden[1], w_fc[1])
    pieces = [grad_second[at * rows : (at + 1) * rows] for at in range(plan.count)]
    back, g_mlp_gain, g_mlp_shift = norm_back(summed(pieces, "ctx"), mlp_gain, middle)
    grad_middle = grad_final + back
    branch = low(grad_middle)
    g_proj_bias = jnp.sum(wide(branch), 0)
    grad_mixed = plan.padded_out(low(dot_nt(branch, w_proj)))
    pieces = [plan.window(grad_mixed, plan.ci ^ at) for at in range(plan.count)]
    g_w_proj = low(dot_tn(mixed_all, branch))
    grad_heads = jnp.concatenate(exchanged(pieces, "ctx"))
    column = lax.broadcasted_iota(jnp.int32, grad_heads.shape, 1)
    grad_heads = jnp.where(column < plan.owned, grad_heads, 0)
    grad_qkv = attend_back(place, qkv, grad_heads, log_total, plan.heads, block)
    g_bias_qkv = jnp.sum(wide(grad_qkv), 0)
    g_w_qkv = low(dot_tn(first_norm, grad_qkv))
    grad_first = dot_nt(grad_qkv, w_qkv)
    pieces = [grad_first[at * rows : (at + 1) * rows] for at in range(plan.count)]
    back, g_attn_gain, g_attn_shift = norm_back(summed(pieces, "ctx"), attn_gain, stream)
    vectors_grad = (
        g_attn_gain,
        g_attn_shift,
        g_bias_qkv,
        g_proj_bias,
        g_mlp_gain,
        g_mlp_shift,
        g_fc_bias,
        g_out_bias,
    )
    return low(grad_middle + back), (g_w_qkv, g_w_proj, g_w_fc, g_w_out), vectors_grad


def body(
    feed,
    block_order,
    attn_gain,
    attn_shift,
    w_qkv,
    query_bias,
    value_bias,
    w_proj,
    proj_bias,
    mlp_gain,
    mlp_shift,
    w_fc,
    fc_bias,
    w_out,
    out_bias,
):
    width = w_proj.shape[2]
    shard = w_proj.shape[1]
    hidden_rows = w_out.shape[1]
    plan = Plan(width, hidden_rows)
    count, owners = plan.count, lax.axis_size("wt")
    first, xi, ci = plan.first, plan.xi, plan.ci
    part, half, span = plan.part, plan.half, plan.span
    rows = feed.shape[3]
    block = rows // 2

    def mine_other(mine, other):
        return (jnp.where(first, mine, other), jnp.where(first, other, mine))

    slots = jnp.arange(2 * count, dtype=jnp.int32)
    held = 2 * (ci ^ (slots // 2)) + slots % 2
    table = (held[:, None] == slots[None, :]).astype(jnp.int32)
    blocks_held = jnp.sum(table * block_order[None, :], 1)
    found = (blocks_held[None, :] == slots[:, None]).astype(jnp.int32)
    place = jnp.sum(found * slots[None, :], 1)

    local = feed[0, :, 0]
    own = lax.dynamic_index_in_dim(local, xi, 0, keepdims=False)
    came = swap(lax.dynamic_index_in_dim(local, 1 - xi, 0, keepdims=False), "section")
    entering, coming = mine_other(own, came)

    fc_part = lax.dynamic_slice_in_dim(fc_bias[0], ci * part, part, 0)
    small = jnp.concatenate(
        [
            vector[0]
            for vector in (
                attn_gain, attn_shift, query_bias, value_bias, proj_bias, mlp_gain, mlp_shift, out_bias
            )
        ]
        + [fc_part]
    )
    small = wide(lax.all_gather(small, ("section", "wt"))).reshape(2, owners, small.shape[0])

    def vectors_of(layer):
        full = jnp.swapaxes(small[layer, :, : 8 * shard].reshape(owners, 8, shard), 0, 1)
        full = full.reshape(8, owners * shard)
        hidden = small[layer, :, 8 * shard :]
        halves = [
            lax.dynamic_slice_in_dim(hidden, duty * half, half, 1).reshape(-1) for duty in (xi, 1 - xi)
        ]
        query = plan.window(plan.padded_out(full[2]), ci)
        value = plan.window(plan.padded_out(full[3]), ci)
        bias_qkv = jnp.concatenate([query, jnp.zeros_like(query), value])
        return (full[0], full[1], bias_qkv, full[4], full[5], full[6], halves, full[7])

    qkv_shard = jnp.concatenate(
        [
            plan.window(plan.padded_out(w_qkv[0][:, at * width : (at + 1) * width]), ci)
            for at in range(3)
        ],
        1,
    )
    proj_rows = shard // count
    proj_shard = lax.dynamic_slice_in_dim(w_proj[0], ci * proj_rows, proj_rows, 0)

    def fc_shard(duty):
        return jnp.concatenate(
            [
                lax.dynamic_slice_in_dim(
                    w_fc[0], owner * hidden_rows + ci * part + duty * half, half, 1
                )
                for owner in range(owners)
            ],
            1,
        )

    def out_shard(duty):
        return lax.dynamic_slice_in_dim(w_out[0], ci * part + duty * half, half, 0)

    qkv_shards = mine_other(qkv_shard, swap(qkv_shard, "section"))
    proj_shards = mine_other(proj_shard, swap(proj_shard, "section"))
    fc_shards = mine_other(fc_shard(xi), swap(fc_shard(1 - xi), "section"))
    out_shards = mine_other(out_shard(xi), swap(out_shard(1 - xi), "section"))

    def weights_of(layer):
        qkv_full = over_wt(qkv_shards[layer])
        proj_part = over_wt(proj_shards[layer], tiled=False)
        proj_full = jnp.swapaxes(by_owner(gathered(proj_part, "ctx"), "ctx"), 0, 1)
        proj_full = proj_full.reshape(width, width)
        fc_full = over_wt(fc_shards[layer])
        out_full = over_wt(out_shards[layer])
        return (
            qkv_full,
            proj_full,
            (fc_full, swap(fc_full, "section")),
            (out_full, swap(out_full, "section")),
        )

    weights = [weights_of(layer) for layer in range(2)]
    vectors = [vectors_of(layer) for layer in range(2)]
    kept = []
    state = entering
    for layer in range(2):
        state, kept_here = forward_layer(state, weights[layer], vectors[layer], plan, place, block)
        kept.append(kept_here)
    leaving = state

    def reduced(grads):
        g_w_qkv, g_w_proj, g_w_fc, g_w_out = grads
        fc_here = scatter_wt(g_w_fc[0] + swap(g_w_fc[1], "section"))
        out_here = scatter_wt(g_w_out[0] + swap(g_w_out[1], "section"))
        parts = g_w_proj.reshape(owners, count, proj_rows, width)
        parts = [lax.dynamic_index_in_dim(parts, ci ^ at, 1, keepdims=False) for at in range(count)]
        proj_here = scatter_wt(low(summed(parts, "ctx")), tiled=False)
        qkv_here = scatter_wt(g_w_qkv)
        return qkv_here, proj_here, fc_here, out_here

    def to_owner(late, early):
        there = swap(jnp.where(first, early, late), "section")
        return jnp.where(first, late, early), there

    weight_sums = [None, None]
    vector_grads = [None, None]
    for layer in (1, 0):
        coming, grads, vector_grads[layer] = backward_layer(
            coming, kept[layer], weights[layer], vectors[layer], plan, place, block
        )
        weight_sums[layer] = reduced(grads)

    def whole(value):
        return by_owner(gathered(value, "ctx"), "ctx")

    qkv_own, qkv_there = to_owner(weight_sums[0][0], weight_sums[1][0])
    proj_own, proj_there = to_owner(weight_sums[0][1], weight_sums[1][1])
    fc_own, fc_there = to_owner(weight_sums[0][2], weight_sums[1][2])
    out_own, out_there = to_owner(weight_sums[0][3], weight_sums[1][3])
    qkv_sum = wide(whole(low(wide(qkv_own) + wide(qkv_there)))).reshape(count, shard, 3, span)
    qkv_grad = jnp.concatenate([plan.joined(qkv_sum[:, :, at]) for at in range(3)], -1)
    proj_grad = wide(whole(low(wide(proj_own) + wide(proj_there)))).reshape(shard, width)
    fc_sum = jnp.where(first, jnp.stack([fc_own, fc_there]), jnp.stack([fc_there, fc_own]))
    fc_grad = wide(whole(fc_sum)).reshape(count, 2, shard, owners, half)
    fc_grad = fc_grad.transpose(2, 3, 0, 1, 4).reshape(shard, owners * hidden_rows)
    out_sum = jnp.where(
        first, jnp.concatenate([out_own, out_there]), jnp.concatenate([out_there, out_own])
    )
    out_grad = wide(whole(out_sum)).reshape(hidden_rows, width)

    def packed(grads):
        g_attn_gain, g_attn_shift, g_bias_qkv, g_proj_bias, g_mlp_gain, g_mlp_shift, g_fc, g_out = grads

        def placed(part):
            zeros = jnp.zeros((plan.padded,), jnp.float32)
            return lax.dynamic_update_slice_in_dim(zeros, part, ci * plan.step, 0)[:width]

        full = jnp.stack(
            [
                g_attn_gain,
                g_attn_shift,
                placed(g_bias_qkv[:span]),
                placed(g_bias_qkv[2 * span :]),
                g_proj_bias,
                g_mlp_gain,
                g_mlp_shift,
                g_out,
            ]
        )
        full = jnp.swapaxes(full.reshape(8, owners, shard), 0, 1).reshape(owners, 8 * shard)
        halves = [g.reshape(owners, half) for g in g_fc]
        halves = jnp.where(
            first, jnp.concatenate(halves, 1), jnp.concatenate(halves[::-1], 1)
        )
        zeros = jnp.zeros((owners, hidden_rows), jnp.float32)
        return jnp.concatenate(
            [full, lax.dynamic_update_slice_in_dim(zeros, halves, ci * part, 1)], 1
        )

    late, early = packed(vector_grads[0]), packed(vector_grads[1])
    total = jnp.where(first, late, early) + swap(jnp.where(first, early, late), "section")
    for bit in bits_of("ctx"):
        total = total + swap(total, "ctx", bit)
    pieces = {
        at: lax.dynamic_index_in_dim(total, plan.wi ^ at, 0, keepdims=False) for at in range(owners)
    }
    for bit in bits_of("wt"):
        for at in sorted(pieces, reverse=True):
            if at & bit:
                pieces[at ^ bit] = pieces[at ^ bit] + swap(pieces.pop(at), "wt", bit)
    total = pieces[0]
    vector_out = total[: 8 * shard].reshape(8, shard)
    fc_bias_out = total[8 * shard :]

    stays = jnp.where(first, coming, leaving)
    came = swap(jnp.where(first, leaving, coming), "section")
    result = jnp.where(first, jnp.stack([stays, came]), jnp.stack([came, stays]))
    result = result.reshape(1, 2, 1, rows, width)
    return (
        result,
        vector_out[0][None],
        vector_out[1][None],
        qkv_grad[None],
        vector_out[2][None],
        vector_out[3][None],
        proj_grad[None],
        vector_out[4][None],
        vector_out[5][None],
        vector_out[6][None],
        fc_grad[None],
        fc_bias_out[None],
        out_grad[None],
        vector_out[7][None],
    )


def solution(mesh):
    return jax.shard_map(
        body,
        mesh=mesh,
        in_specs=(
            P("section", None, "wt", "ctx", None),
            P(),
            P("section", "wt"),
            P("section", "wt"),
            P("section", "wt", None),
            P("section", "wt"),
            P("section", "wt"),
            P("section", "wt", None),
            P("section", "wt"),
            P("section", "wt"),
            P("section", "wt"),
            P("section", "wt", None),
            P("section", "wt"),
            P("section", "wt", None),
            P("section", "wt"),
        ),
        out_specs=(
            P("section", None, "wt", "ctx", None),
            P("section", "wt"),
            P("section", "wt"),
            P("section", "wt", None),
            P("section", "wt"),
            P("section", "wt"),
            P("section", "wt", None),
            P("section", "wt"),
            P("section", "wt"),
            P("section", "wt"),
            P("section", "wt", None),
            P("section", "wt"),
            P("section", "wt", None),
            P("section", "wt"),
        ),
        check_vma=False,
    )
```

time: 5680 us -> 1610 us (0.28)
  waiting for transfers between devices: 4610 us -> 771 us
  matrix products: 617 us -> 232 us
  other arithmetic: 182 us -> 87.1 us
  starting transfers between devices: 21.9 us -> 115 us
  local copies, waits for them, and re-layouts: 179 us -> 268 us
  Pallas kernels: 0 us -> 73.4 us
    reduce_scatter x15 -> x4, waiting for transfers between devices: 3170 us -> 0.01 us  [scatter_wt(): return lax.psum_scatter(value, 'wt', scatter_dimension=0, tiled=tiled)]
    all_gather x10 -> x8, waiting for transfers between devices: 1110 us -> 23.7 us  [over_wt(): return lax.all_gather(value, 'wt', axis=0, tiled=tiled)]
    ppermute x4 -> x96, waiting for transfers between devices: 62.8 us -> 747 us  [swap(): return lax.ppermute(value, axis, flip(axis, bit))]
    dot_general x141 -> x36, matrix products: 617 us -> 232 us  [the longest x12 82.5 us: dot_tn(): lax.dot_general(left, right, (((0,), (0,)), ((), ())), preferred_element_...]
    psum x1 -> x0, waiting for transfers between devices: 253 us -> none  [body(): lax.psum(shortened(totals), 'ctx')]
    ppermute x4 -> x96, starting transfers between devices: 9.04 us -> 113 us  [swap(): return lax.ppermute(value, axis, flip(axis, bit))]
    dynamic_slice x75 -> x16, local copies, waits for them, and re-layouts: 86.9 us -> 9.81 us  [the longest x9 4.44 us: window(): lax.dynamic_slice_in_dim(padded, index * self.step, self.span, padded.ndi...]
    pallas_call x0 -> x4, Pallas kernels: none -> 73.4 us  [the longest x2 42.1 us: attend_back(): pl.pallas_call(functools.partial(attend_back_kernel, block, tile, heads),...]
  transfers between devices with their start and end apart: 31 -> 112, of which waited for: 27 -> 50; matrix products, arithmetic and copies ran while one was open for 9% -> 27% of each run, Pallas kernels for 0% -> 3%
where the time goes in v1:
time: 1610 us; the launch traced here: 1600 us
  waiting for transfers between devices  771 us (48%)
  local copies, waits for them, and re-layouts  268 us (17%)
  matrix products  232 us (14%)
  starting transfers between devices  115 us (7%)
  other arithmetic  87.1 us (5%)
  Pallas kernels  73.4 us (5%)
  blocking collectives  31.3 us (2%)
  between operations  17.1 us (1%)
    ppermute x96, waiting for transfers between devices, swap(): return lax.ppermute(value, axis, flip(axis, bit))  747 us
    ppermute x96, starting transfers between devices, swap(): return lax.ppermute(value, axis, flip(axis, bit))  113 us
    dot_general x12, matrix products, dot_tn(): lax.dot_general(left, right, (((0,), (0,)), ((), ())), preferred_element_...  82.5 us
    dot_general x12, matrix products, dot(): return jnp.dot(left, right, preferred_element_type=jnp.float32)  76.5 us
    dot_general x12, matrix products, dot_nt(): lax.dot_general(left, right, (((1,), (1,)), ((), ())), preferred_element_...  73.3 us
    another operation x3, local copies, waits for them, and re-layouts, body(): fc_grad[None]  55 us
    pallas_call x2, Pallas kernels, attend_back(): pl.pallas_call(functools.partial(attend_back_kernel, block, tile, heads),...  42.1 us
    dynamic_update_slice x28, local copies, waits for them, and re-layouts, by_owner(): whole = lax.dynamic_update_index_in_dim(whole, piece, here ^ at, 0)  40.6 us
  transfers between devices with their start and end apart: 112, of which 50 were waited for; matrix products, arithmetic and copies ran while one was open for 27% of the time, Pallas kernels for 3%

profile of v1, /device:TPU:1, one launch (start us, length us, event | category | flops | bytes accessed | tf_op | source)
XLA Modules:
  0.0 1595.2 jit_solution(6426828455673447751)
XLA Ops:
  10.4 7.8 collective-permute-done.8
  24.5 15.2 collective-permute-done.15
  47.3 25.7 %collective-permute-done.4 = bf16[400,1536]{1,0:T(8,128)(2,1)S(1)} collective-permute-done((bf16[400,1536]{1,0:T(8,128)(2,1)S(1)}, bf16[400,1536]{1,0:T(8,128)(2,1)S(1)}, u32[]{:S(2)}, u32[]{:S(2)}) %collective-permute-start.4) | collective-permute-done | bytes 1228832 | tf_op jit(solution)/shard_map/ppermute | solution.py:197
  77.0 13.1 collective-permute-done.16
  95.1 31.3 %all-reduce.8 = bf16[28800]{0:T(1024)(128)(2,1)S(1)} all-reduce(bf16[28800]{0:T(1024)(128)(2,1)S(1)} %dynamic-update-slice), channel_id=2, replica_groups=mesh['section'=2,'ctx'=4,'wt'=4] {'section','wt'}, use_global_device_ids=true, to_apply=%add.8 | all-reduce | flops 28800 | bytes 115200
  138.9 11.7 collective-permute-start.9
  152.0 8.8 collective-permute-start.3
  164.8 17.4 %collective-permute-done.10 = bf16[4,100,1600]{2,0,1:T(4,128)(2,1)} collective-permute-done((bf16[4,100,1600]{2,0,1:T(4,128)(2,1)}, bf16[4,100,1600]{2,0,1:T(4,128)(2,1)}, u32[]{:S(2)}, u32[]{:S(2)}) %collective-permute-start.10) | collective-permute-done | bytes 1280032 | tf_op jit(solution)/shard_map/ppermute | solution.py:197
  197.8 13.6 all-gather.14.cloned.1.call-done
  211.4 8.6 add_convert_fusion.1.qkv
  220.0 15.6 shard_map.254
  239.5 8.0 reshape.476
  269.3 18.6 %collective-permute-done.13 = bf16[256,1600]{0,1:T(8,128)(2,1)S(1)} collective-permute-done((bf16[256,1600]{0,1:T(8,128)(2,1)S(1)}, bf16[256,1600]{0,1:T(8,128)(2,1)S(1)}, u32[]{:S(2)}, u32[]{:S(2)}) %collective-permute-start.13) | collective-permute-done | bytes 819232 | tf_op jit(solution)/shard_map/ppermute | solution.py:197
  302.2 45.9 %collective-permute-done.18 = bf16[800,1600]{1,0:T(8,128)(2,1)} collective-permute-done((bf16[800,1600]{1,0:T(8,128)(2,1)}, bf16[800,1600]{1,0:T(8,128)(2,1)}, u32[]{:S(2)}, u32[]{:S(2)}) %collective-permute-start.18) | collective-permute-done | bytes 2560032 | tf_op jit(solution)/shard_map/ppermute | solution.py:197
  370.5 14.5 collective-permute-done.21
  396.6 16.9 %collective-permute-done.29 = bf16[4,100,1600]{2,0,1:T(4,128)(2,1)} collective-permute-done((bf16[4,100,1600]{2,0,1:T(4,128)(2,1)}, bf16[4,100,1600]{2,0,1:T(4,128)(2,1)}, u32[]{:S(2)}, u32[]{:S(2)}) %collective-permute-start.29) | collective-permute-done | bytes 1280032 | tf_op jit(solution)/shard_map/ppermute | solution.py:197
  415.5 15.5 collective-permute-done.23
  443.6 10.1 all-gather.20.cloned.1.call-done
  454.9 9.1 add_convert_fusion.qkv
  464.0 15.6 shard_map.255
  483.5 8.4 reshape.477
  515.1 18.4 %collective-permute-done.35 = bf16[256,1600]{0,1:T(8,128)(2,1)} collective-permute-done((bf16[256,1600]{0,1:T(8,128)(2,1)}, bf16[256,1600]{0,1:T(8,128)(2,1)}, u32[]{:S(2)}, u32[]{:S(2)}) %collective-permute-start.35) | collective-permute-done | bytes 819232 | tf_op jit(solution)/shard_map/ppermute | solution.py:197
  535.9 15.2 collective-permute-done.32
  564.0 30.2 %collective-permute-done.37 = bf16[800,1600]{1,0:T(8,128)(2,1)} collective-permute-done((bf16[800,1600]{1,0:T(8,128)(2,1)}, bf16[800,1600]{1,0:T(8,128)(2,1)}, u32[]{:S(2)}, u32[]{:S(2)}) %collective-permute-start.37) | collective-permute-done | bytes 2560032 | tf_op jit(solution)/shard_map/ppermute | solution.py:197
  594.1 8.2 convert_reduce_fusion.2
  608.4 7.4 convert_reduce_fusion.3
  626.8 18.6 %collective-permute-done.41 = bf16[256,1600]{0,1:T(8,128)(2,1)} collective-permute-done((bf16[256,1600]{0,1:T(8,128)(2,1)}, bf16[256,1600]{0,1:T(8,128)(2,1)}, u32[]{:S(2)}, u32[]{:S(2)}) %collective-permute-start.41) | collective-permute-done | bytes 819232 | tf_op jit(solution)/shard_map/ppermute | solution.py:197
  673.6 21.2 %shard_map.256 = bf16[1024,1536]{1,0:T(8,128)(2,1)S(1)} custom-call(s32[8]{0:T(128)S(1)} %select_reduce_fusion.place, bf16[1024,1536]{1,0:T(8,128)(2,1)} %copy-done.7, bf16[1024,512]{1,0:T(8,128)(2,1)S(1)} %maximum_select_fusion.5.grad_mixed, f32[8,1024]{1,0:T(8,128)S(1)} %get-tuple-element.20.log_total), custom_call_target="tpu_custom_call" | custom-call | flops 3288334336 | bytes 7340032 | tf_op jit(solution)/shard_map/pallas_call | solution.py:163
  694.8 8.8 fusion.156
  707.7 18.3 %collective-permute-done.47 = bf16[256,1600]{0,1:T(8,128)(2,1)S(1)} collective-permute-done((bf16[256,1600]{0,1:T(8,128)(2,1)S(1)}, bf16[256,1600]{0,1:T(8,128)(2,1)S(1)}, u32[]{:S(2)}, u32[]{:S(2)}) %collective-permute-start.47) | collective-permute-done | bytes 819232 | tf_op jit(solution)/shard_map/ppermute | solution.py:197
  731.8 16.0 %collective-permute-done.49 = bf16[256,1600]{0,1:T(8,128)(2,1)S(1)} collective-permute-done((bf16[256,1600]{0,1:T(8,128)(2,1)S(1)}, bf16[256,1600]{0,1:T(8,128)(2,1)S(1)}, u32[]{:S(2)}, u32[]{:S(2)}) %collective-permute-start.49) | collective-permute-done | bytes 819232 | tf_op jit(solution)/shard_map/ppermute | solution.py:197
  751.8 6.9 convert_reduce_fusion.4
  782.6 7.6 reshape.487
  807.4 7.8 reshape.486
  830.4 23.6 %collective-permute-done.76 = bf16[4,100,1600]{2,0,1:T(4,128)(2,1)S(1)} collective-permute-done((bf16[4,100,1600]{2,0,1:T(4,128)(2,1)S(1)}, bf16[4,100,1600]{2,0,1:T(4,128)(2,1)S(1)}, u32[]{:S(2)}, u32[]{:S(2)}) %collective-permute-start.76) | collective-permute-done | bytes 1280032 | tf_op jit(solution)/shard_map/ppermute | solution.py:197
  855.5 8.0 convolution_convert_fusion.6
  864.8 17.8 %collective-permute-done.79 = bf16[4,100,1600]{2,0,1:T(4,128)(2,1)S(1)} collective-permute-done((bf16[4,100,1600]{2,0,1:T(4,128)(2,1)}, bf16[4,100,1600]{2,0,1:T(4,128)(2,1)S(1)}, u32[]{:S(2)}, u32[]{:S(2)}) %collective-permute-start.79) | collective-permute-done | bytes 1280032 | tf_op jit(solution)/shard_map/ppermute | solution.py:197
  886.3 34.8 %collective-permute-done.91 = bf16[800,1600]{1,0:T(8,128)(2,1)} collective-permute-done((bf16[800,1600]{1,0:T(8,128)(2,1)}, bf16[800,1600]{1,0:T(8,128)(2,1)}, u32[]{:S(2)}, u32[]{:S(2)}) %collective-permute-start.91) | collective-permute-done | bytes 2560032 | tf_op jit(solution)/shard_map/ppermute | solution.py:197
  921.1 8.9 fusion.35
  937.6 55.1 %collective-permute-done.90 = bf16[800,1600]{1,0:T(8,128)(2,1)S(1)} collective-permute-done((bf16[800,1600]{1,0:T(8,128)(2,1)S(1)}, bf16[800,1600]{1,0:T(8,128)(2,1)S(1)}, u32[]{:S(2)}, u32[]{:S(2)}) %collective-permute-start.90) | collective-permute-done | bytes 2560032 | tf_op jit(solution)/shard_map/ppermute | solution.py:197
  1005.3 54.3 %collective-permute-done.85 = bf16[1600,800]{0,1:T(8,128)(2,1)} collective-permute-done((bf16[1600,800]{0,1:T(8,128)(2,1)S(1)}, bf16[1600,800]{0,1:T(8,128)(2,1)}, u32[]{:S(2)}, u32[]{:S(2)}) %collective-permute-start.85) | collective-permute-done | bytes 2560032 | tf_op jit(solution)/shard_map/ppermute | solution.py:197
  1063.9 7.7 fusion.33
  1078.5 53.2 %collective-permute-done.84 = bf16[1600,800]{0,1:T(8,128)(2,1)S(1)} collective-permute-done((bf16[1600,800]{0,1:T(8,128)(2,1)S(1)}, bf16[1600,800]{0,1:T(8,128)(2,1)S(1)}, u32[]{:S(2)}, u32[]{:S(2)}) %collective-permute-start.84) | collective-permute-done | bytes 2560032 | tf_op jit(solution)/shard_map/ppermute | solution.py:197
  1135.2 8.6 fusion.32
  1144.1 8.9 convolution_convert_fusion
  1153.8 7.3 fusion.117
  1161.1 7.1 fusion.159
  1196.5 21.0 %shard_map.257 = bf16[1024,1536]{1,0:T(8,128)(2,1)S(1)} custom-call(s32[8]{0:T(128)S(1)} %select_reduce_fusion.place, bf16[1024,1536]{1,0:T(8,128)(2,1)} %copy-done.6, bf16[1024,512]{1,0:T(8,128)(2,1)S(1)} %maximum_select_fusion.6.grad_mixed, f32[8,1024]{1,0:T(8,128)S(1)} %get-tuple-element.21.log_total), custom_call_target="tpu_custom_call" | custom-call | flops 3288334336 | bytes 7340032 | tf_op jit(solution)/shard_map/pallas_call | solution.py:163
  1217.5 10.9 fusion.158
  1237.2 9.3 convolution_convert_fusion.1
  1269.4 15.0 collective-permute-done.66
  1303.4 13.8 collective-permute-done.63
  1328.7 12.3 collective-permute-done.92
  1347.6 8.7 collective-permute-done.86
  1378.5 29.6 %collective-permute-done.88 = bf16[2,400,800]{2,1,0:T(8,128)(2,1)} collective-permute-done((bf16[2,400,800]{2,1,0:T(8,128)(2,1)}, bf16[2,400,800]{2,1,0:T(8,128)(2,1)}, u32[]{:S(2)}, u32[]{:S(2)}) %collective-permute-start.88) | collective-permute-done | bytes 1280032 | tf_op jit(solution)/shard_map/ppermute | solution.py:197
  1421.9 22.1 %collective-permute-done.70 = bf16[400,1536]{1,0:T(8,128)(2,1)S(1)} collective-permute-done((bf16[400,1536]{1,0:T(8,128)(2,1)S(1)}, bf16[400,1536]{1,0:T(8,128)(2,1)S(1)}, u32[]{:S(2)}, u32[]{:S(2)}) %collective-permute-start.70) | collective-permute-done | bytes 1228832 | tf_op jit(solution)/shard_map/ppermute | solution.py:197
  1450.4 7.3 bitcast_convert_fusion
  1457.7 20.0 %collective-permute-done.72 = bf16[400,1536]{1,0:T(8,128)(2,1)} collective-permute-done((bf16[400,1536]{1,0:T(8,128)(2,1)S(1)}, bf16[400,1536]{1,0:T(8,128)(2,1)}, u32[]{:S(2)}, u32[]{:S(2)}) %collective-permute-start.72) | collective-permute-done | bytes 1228832 | tf_op jit(solution)/shard_map/ppermute | solution.py:197
  1479.7 16.2 %reshape.501 = f32[4,2,400,4,200]{4,3,2,1,0:T(4,128)} reshape(bf16[4,2,400,800]{3,2,1,0:T(8,128)(2,1)} %bitcast_dynamic-update-slice_fusion) | data formatting | bytes 15360000 | tf_op jit(solution)/shard_map/broadcast_in_dim;reshape | solution.py:608
  1495.9 19.6 %copy.196 = f32[400,4,4,2,200]{4,3,2,1,0:T(2,128)} copy(f32[400,4,4,2,200]{4,1,0,3,2:T(4,128)} %bitcast.243) | data formatting | bytes 20480000 | tf_op jit(solution)/shard_map/broadcast_in_dim;reshape | solution.py:608
  1515.4 19.2 %reshape.499 = f32[1,400,6400]{2,1,0:T(8,128)} reshape(f32[400,4,4,2,200]{4,3,2,1,0:T(2,128)} %copy.196) | data formatting | bytes 20480000 | tf_op jit(solution)/shard_map/broadcast_in_dim;reshape | solution.py:608
  1541.9 15.8 reshape.492
  1557.7 16.2 %fusion.139 = (f32[4,400,1,512]{3,2,1,0:T(1,128)S(1)}, f32[4,400,1,512]{3,2,1,0:T(1,128)S(1)}, f32[4,400,1,512]{3,2,1,0:T(1,128)S(1)}) fusion(f32[4,400,3,512]{3,2,1,0:T(4,128)} %reshape.492), kind=kLoop, calls=%fused_computation.387 | loop fusion | bytes 19660800 | tf_op jit(solution)/shard_map/slice | solution.py:539
  1579.1 9.3 concatenate.149
  (753 shorter events, 500.5 us)
Async XLA Ops:
  7.2 128.7 %all-gather.26.cloned.1.call-start = ((), (), s32[]{:S(2)}) async-start(), calls=%async_computation.18 | async-start | bytes 1730560 | tf_op jit(solution)/shard_map/all_gather | solution.py:239
  20.3 170.7 %all-gather.16.cloned.1.call-start = ((), (), s32[]{:S(2)}) async-start(), calls=%async_computation.9 | async-start | bytes 3584000 | tf_op jit(solution)/shard_map/all_gather | solution.py:239
  41.4 170.0 %all-gather.14.cloned.1.call-start = ((), (), s32[]{:S(2)}) async-start(), calls=%async_computation.8 | async-start | bytes 6144000 | tf_op jit(solution)/shard_map/all_gather | solution.py:239
  46.4 26.6 %collective-permute-start.4 = (bf16[400,1536]{1,0:T(8,128)(2,1)S(1)}, bf16[400,1536]{1,0:T(8,128)(2,1)S(1)}, u32[]{:S(2)}, u32[]{:S(2)}) collective-permute-start(bf16[400,1536]{1,0:T(8,128)(2,1)S(1)} %pad_maximum_fusion.6), channel_id=1, source_target_pairs={{0,16},{16,0},{1,17},{17,1},{2,18},{18,2},{3,19},{19,3},{4,20},{20... | collective-permute-start | bytes 3686408 | tf_op jit(solution)/shard_map/ppermute | solution.py:197
  75.1 213.4 %all-gather.18.cloned.1.call-start = ((), (), s32[]{:S(2)}) async-start(), calls=%async_computation.10 | async-start | bytes 3328000 | tf_op jit(solution)/shard_map/all_gather | solution.py:239
  92.6 274.1 %all-gather.28.cloned.1.call-start = ((), (), s32[]{:S(2)}) async-start(), calls=%async_computation.19 | async-start | bytes 1730560 | tf_op jit(solution)/shard_map/all_gather | solution.py:239
  92.7 38.0 %collective-permute-start = (bf16[256,1600]{0,1:T(8,128)(2,1)S(1)}, bf16[256,1600]{0,1:T(8,128)(2,1)S(1)}, u32[]{:S(2)}, u32[]{:S(2)}) collective-permute-start(bf16[256,1600]{0,1:T(8,128)(2,1)S(1)} %dynamic-slice_bitcast_fusion.4), channel_id=1, source_target_pairs={{0,16},{16,0},{1,17},{17,1},{2,18},{18,2},{3,19},{19,3},{4,20},{20... | collective-permute-start | bytes 2457608 | tf_op jit(solution)/shard_map/ppermute | solution.py:197
  130.6 306.7 %all-gather.24.cloned.1.call-start = ((), (), s32[]{:S(2)}) async-start(), calls=%async_computation.13 | async-start | bytes 3584000 | tf_op jit(solution)/shard_map/all_gather | solution.py:239
  138.9 47.1 %collective-permute-start.9 = (bf16[4,100,1600]{2,0,1:T(4,128)(2,1)}, bf16[4,100,1600]{2,0,1:T(4,128)(2,1)}, u32[]{:S(2)}, u32[]{:S(2)}) collective-permute-start(bf16[4,100,1600]{2,0,1:T(4,128)(2,1)} %copy.165), channel_id=1, source_target_pairs={{0,4},{4,0},{8,12},{12,8},{1,5},{5,1},{9,13},{13,9},{2,6},{6,2},{1... | collective-permute-start | bytes 3840008 | tf_op jit(solution)/shard_map/ppermute | solution.py:197
  150.6 31.6 %collective-permute-start.10 = (bf16[4,100,1600]{2,0,1:T(4,128)(2,1)}, bf16[4,100,1600]{2,0,1:T(4,128)(2,1)}, u32[]{:S(2)}, u32[]{:S(2)}) collective-permute-start(bf16[4,100,1600]{2,0,1:T(4,128)(2,1)} %copy.165), channel_id=1, source_target_pairs={{0,8},{4,12},{8,0},{12,4},{1,9},{5,13},{9,1},{13,5},{2,10},{6,14},... | collective-permute-start | bytes 3840008 | tf_op jit(solution)/shard_map/ppermute | solution.py:197
  151.6 302.2 %all-gather.20.cloned.1.call-start = ((), (), s32[]{:S(2)}) async-start(), calls=%async_computation.11 | async-start | bytes 6144000 | tf_op jit(solution)/shard_map/all_gather | solution.py:239
  151.6 46.2 %collective-permute-start.1 = (bf16[256,1600]{0,1:T(8,128)(2,1)S(1)}, bf16[256,1600]{0,1:T(8,128)(2,1)}, u32[]{:S(2)}, u32[]{:S(2)}) collective-permute-start(bf16[256,1600]{0,1:T(8,128)(2,1)S(1)} %fusion.66), channel_id=1, source_target_pairs={{0,4},{4,0},{8,12},{12,8},{1,5},{5,1},{9,13},{13,9},{2,6},{6,2},{1... | collective-permute-start | bytes 2457608 | tf_op jit(solution)/shard_map/ppermute | solution.py:197
  152.0 45.9 %collective-permute-start.3 = (bf16[256,1600]{0,1:T(8,128)(2,1)}, bf16[256,1600]{0,1:T(8,128)(2,1)}, u32[]{:S(2)}, u32[]{:S(2)}) collective-permute-start(bf16[256,1600]{0,1:T(8,128)(2,1)} %collective-permute-done.2), channel_id=1, source_target_pairs={{0,4},{4,0},{8,12},{12,8},{1,5},{5,1},{9,13},{13,9},{2,6},{6,2},{1... | collective-permute-start | bytes 2457608 | tf_op jit(solution)/shard_map/ppermute | solution.py:197
  182.2 54.8 %collective-permute-start.11 = (bf16[4,100,1600]{2,0,1:T(4,128)(2,1)}, bf16[4,100,1600]{2,0,1:T(4,128)(2,1)}, u32[]{:S(2)}, u32[]{:S(2)}) collective-permute-start(bf16[4,100,1600]{2,0,1:T(4,128)(2,1)} %collective-permute-done.10), channel_id=1, source_target_pairs={{0,4},{4,0},{8,12},{12,8},{1,5},{5,1},{9,13},{13,9},{2,6},{6,2},{1... | collective-permute-start | bytes 3840008 | tf_op jit(solution)/shard_map/ppermute | solution.py:197
  196.6 94.2 %collective-permute-start.17 = (bf16[1600,800]{0,1:T(8,128)(2,1)}, bf16[1600,800]{0,1:T(8,128)(2,1)}, u32[]{:S(2)}, u32[]{:S(2)}) collective-permute-start(bf16[1600,800]{0,1:T(8,128)(2,1)} %copy.170), channel_id=1, source_target_pairs={{0,16},{16,0},{1,17},{17,1},{2,18},{18,2},{3,19},{19,3},{4,20},{20... | collective-permute-start | bytes 7680008 | tf_op jit(solution)/shard_map/ppermute | solution.py:197
  267.8 20.1 %collective-permute-start.13 = (bf16[256,1600]{0,1:T(8,128)(2,1)S(1)}, bf16[256,1600]{0,1:T(8,128)(2,1)S(1)}, u32[]{:S(2)}, u32[]{:S(2)}) collective-permute-start(bf16[256,1600]{0,1:T(8,128)(2,1)S(1)} %add_convert_fusion.4), channel_id=1, source_target_pairs={{0,8},{4,12},{8,0},{12,4},{1,9},{5,13},{9,1},{13,5},{2,10},{6,14},... | collective-permute-start | bytes 2457608 | tf_op jit(solution)/shard_map/ppermute | solution.py:197
  269.1 21.7 %collective-permute-start.12 = (bf16[256,1600]{0,1:T(8,128)(2,1)S(1)}, bf16[256,1600]{0,1:T(8,128)(2,1)}, u32[]{:S(2)}, u32[]{:S(2)}) collective-permute-start(bf16[256,1600]{0,1:T(8,128)(2,1)S(1)} %add_convert_fusion.4), channel_id=1, source_target_pairs={{0,4},{4,0},{8,12},{12,8},{1,5},{5,1},{9,13},{13,9},{2,6},{6,2},{1... | collective-permute-start | bytes 2457608 | tf_op jit(solution)/shard_map/ppermute | solution.py:197
  288.5 59.6 %collective-permute-start.18 = (bf16[800,1600]{1,0:T(8,128)(2,1)}, bf16[800,1600]{1,0:T(8,128)(2,1)}, u32[]{:S(2)}, u32[]{:S(2)}) collective-permute-start(bf16[800,1600]{1,0:T(8,128)(2,1)} %all-gather.18.cloned.1.call-done), channel_id=1, source_target_pairs={{0,16},{16,0},{1,17},{17,1},{2,18},{18,2},{3,19},{19,3},{4,20},{20... | collective-permute-start | bytes 7680008 | tf_op jit(solution)/shard_map/ppermute | solution.py:197
  290.6 243.9 %all-gather.22.cloned.1.call-start = ((), (), s32[]{:S(2)}) async-start(), calls=%async_computation.12 | async-start | bytes 3328000 | tf_op jit(solution)/shard_map/all_gather | solution.py:239
  365.2 19.8 %collective-permute-start.21 = (bf16[256,1600]{0,1:T(8,128)(2,1)}, bf16[256,1600]{0,1:T(8,128)(2,1)S(1)}, u32[]{:S(2)}, u32[]{:S(2)}) collective-permute-start(bf16[256,1600]{0,1:T(8,128)(2,1)} %fusion.87), channel_id=1, source_target_pairs={{0,8},{4,12},{8,0},{12,4},{1,9},{5,13},{9,1},{13,5},{2,10},{6,14},... | collective-permute-start | bytes 2457608 | tf_op jit(solution)/shard_map/ppermute | solution.py:197
  369.7 62.5 %collective-permute-start.28 = (bf16[4,100,1600]{2,0,1:T(4,128)(2,1)}, bf16[4,100,1600]{2,0,1:T(4,128)(2,1)}, u32[]{:S(2)}, u32[]{:S(2)}) collective-permute-start(bf16[4,100,1600]{2,0,1:T(4,128)(2,1)} %copy.172), channel_id=1, source_target_pairs={{0,4},{4,0},{8,12},{12,8},{1,5},{5,1},{9,13},{13,9},{2,6},{6,2},{1... | collective-permute-start | bytes 3840008 | tf_op jit(solution)/shard_map/ppermute | solution.py:197
  370.4 43.1 %collective-permute-start.29 = (bf16[4,100,1600]{2,0,1:T(4,128)(2,1)}, bf16[4,100,1600]{2,0,1:T(4,128)(2,1)}, u32[]{:S(2)}, u32[]{:S(2)}) collective-permute-start(bf16[4,100,1600]{2,0,1:T(4,128)(2,1)} %copy.172), channel_id=1, source_target_pairs={{0,8},{4,12},{8,0},{12,4},{1,9},{5,13},{9,1},{13,5},{2,10},{6,14},... | collective-permute-start | bytes 3840008 | tf_op jit(solution)/shard_map/ppermute | solution.py:197
  389.2 41.8 %collective-permute-start.23 = (bf16[256,1600]{0,1:T(8,128)(2,1)}, bf16[256,1600]{0,1:T(8,128)(2,1)}, u32[]{:S(2)}, u32[]{:S(2)}) collective-permute-start(bf16[256,1600]{0,1:T(8,128)(2,1)} %fusion.57), channel_id=1, source_target_pairs={{0,8},{4,12},{8,0},{12,4},{1,9},{5,13},{9,1},{13,5},{2,10},{6,14},... | collective-permute-start | bytes 2457608 | tf_op jit(solution)/shard_map/ppermute | solution.py:197
  392.5 899.2 %reduce-scatter.25.cloned.1.call-start = ((), (), s32[]{:S(2)}) async-start(), calls=%async_computation.20 | async-start | bytes 1730560
  413.5 67.5 %collective-permute-start.30 = (bf16[4,100,1600]{2,0,1:T(4,128)(2,1)}, bf16[4,100,1600]{2,0,1:T(4,128)(2,1)}, u32[]{:S(2)}, u32[]{:S(2)}) collective-permute-start(bf16[4,100,1600]{2,0,1:T(4,128)(2,1)} %collective-permute-done.29), channel_id=1, source_target_pairs={{0,4},{4,0},{8,12},{12,8},{1,5},{5,1},{9,13},{13,9},{2,6},{6,2},{1... | collective-permute-start | bytes 3840008 | tf_op jit(solution)/shard_map/ppermute | solution.py:197
  415.5 38.2 %collective-permute-start.22 = (bf16[256,1600]{0,1:T(8,128)(2,1)}, bf16[256,1600]{0,1:T(8,128)(2,1)S(1)}, u32[]{:S(2)}, u32[]{:S(2)}) collective-permute-start(bf16[256,1600]{0,1:T(8,128)(2,1)} %fusion.57), channel_id=1, source_target_pairs={{0,4},{4,0},{8,12},{12,8},{1,5},{5,1},{9,13},{13,9},{2,6},{6,2},{1... | collective-permute-start | bytes 2457608 | tf_op jit(solution)/shard_map/ppermute | solution.py:197
  431.0 22.7 %collective-permute-start.24 = (bf16[256,1600]{0,1:T(8,128)(2,1)}, bf16[256,1600]{0,1:T(8,128)(2,1)S(1)}, u32[]{:S(2)}, u32[]{:S(2)}) collective-permute-start(bf16[256,1600]{0,1:T(8,128)(2,1)} %collective-permute-done.23), channel_id=1, source_target_pairs={{0,4},{4,0},{8,12},{12,8},{1,5},{5,1},{9,13},{13,9},{2,6},{6,2},{1... | collective-permute-start | bytes 2457608 | tf_op jit(solution)/shard_map/ppermute | solution.py:197
  442.4 109.3 %collective-permute-start.38 = (bf16[1600,800]{0,1:T(8,128)(2,1)}, bf16[1600,800]{0,1:T(8,128)(2,1)}, u32[]{:S(2)}, u32[]{:S(2)}) collective-permute-start(bf16[1600,800]{0,1:T(8,128)(2,1)} %copy.177), channel_id=1, source_target_pairs={{0,16},{16,0},{1,17},{17,1},{2,18},{18,2},{3,19},{19,3},{4,20},{20... | collective-permute-start | bytes 7680008 | tf_op jit(solution)/shard_map/ppermute | solution.py:197
  513.2 20.3 %collective-permute-start.35 = (bf16[256,1600]{0,1:T(8,128)(2,1)}, bf16[256,1600]{0,1:T(8,128)(2,1)}, u32[]{:S(2)}, u32[]{:S(2)}) collective-permute-start(bf16[256,1600]{0,1:T(8,128)(2,1)} %add_convert_fusion.3), channel_id=1, source_target_pairs={{0,8},{4,12},{8,0},{12,4},{1,9},{5,13},{9,1},{13,5},{2,10},{6,14},... | collective-permute-start | bytes 2457608 | tf_op jit(solution)/shard_map/ppermute | solution.py:197
  514.4 36.6 %collective-permute-start.32 = (bf16[256,1600]{0,1:T(8,128)(2,1)}, bf16[256,1600]{0,1:T(8,128)(2,1)}, u32[]{:S(2)}, u32[]{:S(2)}) collective-permute-start(bf16[256,1600]{0,1:T(8,128)(2,1)} %get-tuple-element.67), channel_id=1, source_target_pairs={{0,8},{4,12},{8,0},{12,4},{1,9},{5,13},{9,1},{13,5},{2,10},{6,14},... | collective-permute-start | bytes 2457608 | tf_op jit(solution)/shard_map/ppermute | solution.py:197
  514.7 37.1 %collective-permute-start.34 = (bf16[256,1600]{0,1:T(8,128)(2,1)}, bf16[256,1600]{0,1:T(8,128)(2,1)}, u32[]{:S(2)}, u32[]{:S(2)}) collective-permute-start(bf16[256,1600]{0,1:T(8,128)(2,1)} %add_convert_fusion.3), channel_id=1, source_target_pairs={{0,4},{4,0},{8,12},{12,8},{1,5},{5,1},{9,13},{13,9},{2,6},{6,2},{1... | collective-permute-start | bytes 2457608 | tf_op jit(solution)/shard_map/ppermute | solution.py:197
  534.5 59.7 %collective-permute-start.37 = (bf16[800,1600]{1,0:T(8,128)(2,1)}, bf16[800,1600]{1,0:T(8,128)(2,1)}, u32[]{:S(2)}, u32[]{:S(2)}) collective-permute-start(bf16[800,1600]{1,0:T(8,128)(2,1)} %all-gather.22.cloned.1.call-done), channel_id=1, source_target_pairs={{0,16},{16,0},{1,17},{17,1},{2,18},{18,2},{3,19},{19,3},{4,20},{20... | collective-permute-start | bytes 7680008 | tf_op jit(solution)/shard_map/ppermute | solution.py:197
  823.5 30.5 %collective-permute-start.76 = (bf16[4,100,1600]{2,0,1:T(4,128)(2,1)S(1)}, bf16[4,100,1600]{2,0,1:T(4,128)(2,1)S(1)}, u32[]{:S(2)}, u32[]{:S(2)}) collective-permute-start(bf16[4,100,1600]{2,0,1:T(4,128)(2,1)S(1)} %copy.186), channel_id=1, source_target_pairs={{0,8},{4,12},{8,0},{12,4},{1,9},{5,13},{9,1},{13,5},{2,10},{6,14},... | collective-permute-start | bytes 3840008 | tf_op jit(solution)/shard_map/ppermute | solution.py:197
  826.3 38.5 %collective-permute-start.77 = (bf16[4,100,1600]{2,0,1:T(4,128)(2,1)}, bf16[4,100,1600]{2,0,1:T(4,128)(2,1)}, u32[]{:S(2)}, u32[]{:S(2)}) collective-permute-start(bf16[4,100,1600]{2,0,1:T(4,128)(2,1)} %copy.188), channel_id=1, source_target_pairs={{0,4},{4,0},{8,12},{12,8},{1,5},{5,1},{9,13},{13,9},{2,6},{6,2},{1... | collective-permute-start | bytes 3840008 | tf_op jit(solution)/shard_map/ppermute | solution.py:197
  830.2 52.4 %collective-permute-start.79 = (bf16[4,100,1600]{2,0,1:T(4,128)(2,1)}, bf16[4,100,1600]{2,0,1:T(4,128)(2,1)S(1)}, u32[]{:S(2)}, u32[]{:S(2)}) collective-permute-start(bf16[4,100,1600]{2,0,1:T(4,128)(2,1)} %copy.192), channel_id=1, source_target_pairs={{0,8},{4,12},{8,0},{12,4},{1,9},{5,13},{9,1},{13,5},{2,10},{6,14},... | collective-permute-start | bytes 3840008 | tf_op jit(solution)/shard_map/ppermute | solution.py:197
  855.5 436.2 %reduce-scatter.27.cloned.1.call-start = ((), (), s32[]{:S(2)}) async-start(), calls=%async_computation.21 | async-start | bytes 1730560
  863.6 57.5 %collective-permute-start.91 = (bf16[800,1600]{1,0:T(8,128)(2,1)}, bf16[800,1600]{1,0:T(8,128)(2,1)}, u32[]{:S(2)}, u32[]{:S(2)}) collective-permute-start(bf16[800,1600]{1,0:T(8,128)(2,1)} %convolution_convert_fusion.6), channel_id=1, source_target_pairs={{0,16},{16,0},{1,17},{17,1},{2,18},{18,2},{3,19},{19,3},{4,20},{20... | collective-permute-start | bytes 7680008 | tf_op jit(solution)/shard_map/ppermute | solution.py:197
  885.9 436.5 %reduce-scatter.31.cloned.1.call-start = ((), (), s32[]{:S(2)}) async-start(), calls=%async_computation.23 | async-start | bytes 3328000
  930.1 392.3 %reduce-scatter.29.cloned.1.call-start = ((), (), s32[]{:S(2)}) async-start(), calls=%async_computation.22 | async-start | bytes 3328000
  936.4 56.4 %collective-permute-start.90 = (bf16[800,1600]{1,0:T(8,128)(2,1)S(1)}, bf16[800,1600]{1,0:T(8,128)(2,1)S(1)}, u32[]{:S(2)}, u32[]{:S(2)}) collective-permute-start(bf16[800,1600]{1,0:T(8,128)(2,1)S(1)} %convolution_convert_fusion.8), channel_id=1, source_target_pairs={{0,16},{16,0},{1,17},{17,1},{2,18},{18,2},{3,19},{19,3},{4,20},{20... | collective-permute-start | bytes 7680008 | tf_op jit(solution)/shard_map/ppermute | solution.py:197
  998.2 326.7 %reduce-scatter.23.cloned.1.call-start = ((), (), s32[]{:S(2)}) async-start(), calls=%async_computation.17 | async-start | bytes 3584000 | tf_op jit(solution)/shard_map/reduce_scatter | solution.py:243
  1004.1 55.6 %collective-permute-start.85 = (bf16[1600,800]{0,1:T(8,128)(2,1)S(1)}, bf16[1600,800]{0,1:T(8,128)(2,1)}, u32[]{:S(2)}, u32[]{:S(2)}) collective-permute-start(bf16[1600,800]{0,1:T(8,128)(2,1)S(1)} %convolution_convert_fusion.10), channel_id=1, source_target_pairs={{0,16},{16,0},{1,17},{17,1},{2,18},{18,2},{3,19},{19,3},{4,20},{20... | collective-permute-start | bytes 7680008 | tf_op jit(solution)/shard_map/ppermute | solution.py:197
  1071.6 253.4 %reduce-scatter.21.cloned.1.call-start = ((), (), s32[]{:S(2)}) async-start(), calls=%async_computation.16 | async-start | bytes 3584000 | tf_op jit(solution)/shard_map/reduce_scatter | solution.py:243
  1077.2 54.5 %collective-permute-start.84 = (bf16[1600,800]{0,1:T(8,128)(2,1)S(1)}, bf16[1600,800]{0,1:T(8,128)(2,1)S(1)}, u32[]{:S(2)}, u32[]{:S(2)}) collective-permute-start(bf16[1600,800]{0,1:T(8,128)(2,1)S(1)} %convolution_convert_fusion.11), channel_id=1, source_target_pairs={{0,16},{16,0},{1,17},{17,1},{2,18},{18,2},{3,19},{19,3},{4,20},{20... | collective-permute-start | bytes 7680008 | tf_op jit(solution)/shard_map/ppermute | solution.py:197
  1143.8 270.1 %reduce-scatter.19.cloned.1.call-start = ((), (), s32[]{:S(2)}) async-start(), calls=%async_computation.15 | async-start | bytes 6144000 | tf_op jit(solution)/shard_map/reduce_scatter | solution.py:243
  1153.0 260.9 %reduce-scatter.17.cloned.1.call-start = ((), (), s32[]{:S(2)}) async-start(), calls=%async_computation.14 | async-start | bytes 6144000 | tf_op jit(solution)/shard_map/reduce_scatter | solution.py:243
  1185.4 76.4 %collective-permute-start.61 = (bf16[256,1600]{0,1:T(8,128)(2,1)}, bf16[256,1600]{0,1:T(8,128)(2,1)}, u32[]{:S(2)}, u32[]{:S(2)}) collective-permute-start(bf16[256,1600]{0,1:T(8,128)(2,1)} %get-tuple-element.110), channel_id=1, source_target_pairs={{0,4},{4,0},{8,12},{12,8},{1,5},{5,1},{9,13},{13,9},{2,6},{6,2},{1... | collective-permute-start | bytes 2457608 | tf_op jit(solution)/shard_map/ppermute | solution.py:197
  1185.7 99.1 %collective-permute-start.60 = (bf16[256,1600]{0,1:T(8,128)(2,1)}, bf16[256,1600]{0,1:T(8,128)(2,1)}, u32[]{:S(2)}, u32[]{:S(2)}) collective-permute-start(bf16[256,1600]{0,1:T(8,128)(2,1)} %get-tuple-element.109), channel_id=1, source_target_pairs={{0,4},{4,0},{8,12},{12,8},{1,5},{5,1},{9,13},{13,9},{2,6},{6,2},{1... | collective-permute-start | bytes 2457608 | tf_op jit(solution)/shard_map/ppermute | solution.py:197
  1235.7 20.0 %collective-permute-start.59 = (bf16[256,1600]{0,1:T(8,128)(2,1)}, bf16[256,1600]{0,1:T(8,128)(2,1)}, u32[]{:S(2)}, u32[]{:S(2)}) collective-permute-start(bf16[256,1600]{0,1:T(8,128)(2,1)} %fusion.79), channel_id=1, source_target_pairs={{0,8},{4,12},{8,0},{12,4},{1,9},{5,13},{9,1},{13,5},{2,10},{6,14},... | collective-permute-start | bytes 2457608 | tf_op jit(solution)/shard_map/ppermute | solution.py:197
  1263.6 21.1 %collective-permute-start.62 = (bf16[256,1600]{0,1:T(8,128)(2,1)S(1)}, bf16[256,1600]{0,1:T(8,128)(2,1)}, u32[]{:S(2)}, u32[]{:S(2)}) collective-permute-start(bf16[256,1600]{0,1:T(8,128)(2,1)S(1)} %fusion.74), channel_id=1, source_target_pairs={{0,8},{4,12},{8,0},{12,4},{1,9},{5,13},{9,1},{13,5},{2,10},{6,14},... | collective-permute-start | bytes 2457608 | tf_op jit(solution)/shard_map/ppermute | solution.py:197
  1294.4 22.8 %collective-permute-start.63 = (bf16[256,1600]{0,1:T(8,128)(2,1)S(1)}, bf16[256,1600]{0,1:T(8,128)(2,1)S(1)}, u32[]{:S(2)}, u32[]{:S(2)}) collective-permute-start(bf16[256,1600]{0,1:T(8,128)(2,1)S(1)} %broadcast_select_fusion.3), channel_id=1, source_target_pairs={{0,16},{16,0},{1,17},{17,1},{2,18},{18,2},{3,19},{19,3},{4,20},{20... | collective-permute-start | bytes 2457608 | tf_op jit(solution)/shard_map/ppermute | solution.py:197
  1300.6 21.8 %collective-permute-start.82 = (bf16[100,1600]{1,0:T(8,128)(2,1)}, bf16[100,1600]{1,0:T(8,128)(2,1)}, u32[]{:S(2)}, u32[]{:S(2)}) collective-permute-start(bf16[100,1600]{1,0:T(8,128)(2,1)} %get-tuple-element.59), channel_id=1, source_target_pairs={{0,8},{4,12},{8,0},{12,4},{1,9},{5,13},{9,1},{13,5},{2,10},{6,14},... | collective-permute-start | bytes 960008 | tf_op jit(solution)/shard_map/ppermute | solution.py:197
  1322.4 39.3 %collective-permute-start.83 = (bf16[100,1600]{1,0:T(8,128)(2,1)}, bf16[100,1600]{1,0:T(8,128)(2,1)}, u32[]{:S(2)}, u32[]{:S(2)}) collective-permute-start(bf16[100,1600]{1,0:T(8,128)(2,1)} %collective-permute-done.82), channel_id=1, source_target_pairs={{0,4},{4,0},{8,12},{12,8},{1,5},{5,1},{9,13},{13,9},{2,6},{6,2},{1... | collective-permute-start | bytes 960008 | tf_op jit(solution)/shard_map/ppermute | solution.py:197
  1326.5 29.9 %collective-permute-start.86 = (bf16[400,800]{1,0:T(8,128)(2,1)S(1)}, bf16[400,800]{1,0:T(8,128)(2,1)S(1)}, u32[]{:S(2)}, u32[]{:S(2)}) collective-permute-start(bf16[400,800]{1,0:T(8,128)(2,1)S(1)} %get-tuple-element.128), channel_id=1, source_target_pairs={{0,16},{16,0},{1,17},{17,1},{2,18},{18,2},{3,19},{19,3},{4,20},{20... | collective-permute-start | bytes 1920008 | tf_op jit(solution)/shard_map/ppermute | solution.py:197
  1343.9 67.5 %collective-permute-start.93 = (bf16[400,1600]{1,0:T(8,128)(2,1)}, bf16[400,1600]{1,0:T(8,128)(2,1)}, u32[]{:S(2)}, u32[]{:S(2)}) collective-permute-start(bf16[400,1600]{1,0:T(8,128)(2,1)} %maximum_select_fusion.4), channel_id=1, source_target_pairs={{0,4},{4,0},{8,12},{12,8},{1,5},{5,1},{9,13},{13,9},{2,6},{6,2},{1... | collective-permute-start | bytes 3840008 | tf_op jit(solution)/shard_map/ppermute | solution.py:197
  1346.1 31.2 %collective-permute-start.94 = (bf16[400,1600]{1,0:T(8,128)(2,1)}, bf16[400,1600]{1,0:T(8,128)(2,1)}, u32[]{:S(2)}, u32[]{:S(2)}) collective-permute-start(bf16[400,1600]{1,0:T(8,128)(2,1)} %maximum_select_fusion.4), channel_id=1, source_target_pairs={{0,8},{4,12},{8,0},{12,4},{1,9},{5,13},{9,1},{13,5},{2,10},{6,14},... | collective-permute-start | bytes 3840008 | tf_op jit(solution)/shard_map/ppermute | solution.py:197
  1358.0 50.9 %collective-permute-start.87 = (bf16[2,400,800]{2,1,0:T(8,128)(2,1)}, bf16[2,400,800]{2,1,0:T(8,128)(2,1)}, u32[]{:S(2)}, u32[]{:S(2)}) collective-permute-start(bf16[2,400,800]{2,1,0:T(8,128)(2,1)} %maximum_select_fusion.2), channel_id=1, source_target_pairs={{0,4},{4,0},{8,12},{12,8},{1,5},{5,1},{9,13},{13,9},{2,6},{6,2},{1... | collective-permute-start | bytes 3840008 | tf_op jit(solution)/shard_map/ppermute | solution.py:197
  1359.2 48.9 %collective-permute-start.88 = (bf16[2,400,800]{2,1,0:T(8,128)(2,1)}, bf16[2,400,800]{2,1,0:T(8,128)(2,1)}, u32[]{:S(2)}, u32[]{:S(2)}) collective-permute-start(bf16[2,400,800]{2,1,0:T(8,128)(2,1)} %maximum_select_fusion.2), channel_id=1, source_target_pairs={{0,8},{4,12},{8,0},{12,4},{1,9},{5,13},{9,1},{13,5},{2,10},{6,14},... | collective-permute-start | bytes 3840008 | tf_op jit(solution)/shard_map/ppermute | solution.py:197
  1377.4 43.4 %collective-permute-start.95 = (bf16[400,1600]{1,0:T(8,128)(2,1)}, bf16[400,1600]{1,0:T(8,128)(2,1)S(1)}, u32[]{:S(2)}, u32[]{:S(2)}) collective-permute-start(bf16[400,1600]{1,0:T(8,128)(2,1)} %collective-permute-done.94), channel_id=1, source_target_pairs={{0,4},{4,0},{8,12},{12,8},{1,5},{5,1},{9,13},{13,9},{2,6},{6,2},{1... | collective-permute-start | bytes 3840008 | tf_op jit(solution)/shard_map/ppermute | solution.py:197
  1408.1 70.4 %collective-permute-start.89 = (bf16[2,400,800]{2,1,0:T(8,128)(2,1)}, bf16[2,400,800]{2,1,0:T(8,128)(2,1)S(1)}, u32[]{:S(2)}, u32[]{:S(2)}) collective-permute-start(bf16[2,400,800]{2,1,0:T(8,128)(2,1)} %collective-permute-done.88), channel_id=1, source_target_pairs={{0,4},{4,0},{8,12},{12,8},{1,5},{5,1},{9,13},{13,9},{2,6},{6,2},{1... | collective-permute-start | bytes 3840008 | tf_op jit(solution)/shard_map/ppermute | solution.py:197
  1415.3 28.7 %collective-permute-start.70 = (bf16[400,1536]{1,0:T(8,128)(2,1)S(1)}, bf16[400,1536]{1,0:T(8,128)(2,1)S(1)}, u32[]{:S(2)}, u32[]{:S(2)}) collective-permute-start(bf16[400,1536]{1,0:T(8,128)(2,1)S(1)} %broadcast_select_fusion), channel_id=1, source_target_pairs={{0,16},{16,0},{1,17},{17,1},{2,18},{18,2},{3,19},{19,3},{4,20},{20... | collective-permute-start | bytes 3686408 | tf_op jit(solution)/shard_map/ppermute | solution.py:197
  1448.1 86.5 %collective-permute-start.71 = (bf16[400,1536]{1,0:T(8,128)(2,1)S(1)}, bf16[400,1536]{1,0:T(8,128)(2,1)}, u32[]{:S(2)}, u32[]{:S(2)}) collective-permute-start(bf16[400,1536]{1,0:T(8,128)(2,1)S(1)} %get-tuple-element.61), channel_id=1, source_target_pairs={{0,4},{4,0},{8,12},{12,8},{1,5},{5,1},{9,13},{13,9},{2,6},{6,2},{1... | collective-permute-start | bytes 3686408 | tf_op jit(solution)/shard_map/ppermute | solution.py:197
  1448.9 28.8 %collective-permute-start.72 = (bf16[400,1536]{1,0:T(8,128)(2,1)S(1)}, bf16[400,1536]{1,0:T(8,128)(2,1)}, u32[]{:S(2)}, u32[]{:S(2)}) collective-permute-start(bf16[400,1536]{1,0:T(8,128)(2,1)S(1)} %get-tuple-element.61), channel_id=1, source_target_pairs={{0,8},{4,12},{8,0},{12,4},{1,9},{5,13},{9,1},{13,5},{2,10},{6,14},... | collective-permute-start | bytes 3686408 | tf_op jit(solution)/shard_map/ppermute | solution.py:197
  1477.7 61.8 %collective-permute-start.73 = (bf16[400,1536]{1,0:T(8,128)(2,1)}, bf16[400,1536]{1,0:T(8,128)(2,1)}, u32[]{:S(2)}, u32[]{:S(2)}) collective-permute-start(bf16[400,1536]{1,0:T(8,128)(2,1)} %collective-permute-done.72), channel_id=1, source_target_pairs={{0,4},{4,0},{8,12},{12,8},{1,5},{5,1},{9,13},{13,9},{2,6},{6,2},{1... | collective-permute-start | bytes 3686408 | tf_op jit(solution)/shard_map/ppermute | solution.py:197
  (186 other events, 3101.0 us)
Sparse Core Ops, SparseCore 0:
  20.4 35.2 all-gather.25
  57.9 59.7 all-gather.15
  119.9 91.4 all-gather.13
  212.8 53.7 all-gather.17
  268.0 32.0 all-gather.27
  301.5 58.4 all-gather.23
  362.2 91.4 all-gather.19
  455.3 53.8 all-gather.21
  855.6 31.5 reduce-scatter.24
  889.5 31.7 reduce-scatter.26
  930.2 53.1 reduce-scatter.30
  998.4 54.1 reduce-scatter.28
  1071.7 58.6 reduce-scatter.22
  1144.0 59.6 reduce-scatter.20
  1205.8 89.1 reduce-scatter.18
  1297.8 89.3 reduce-scatter.16

commit v2 on v1

v2 whole, which is shorter than its diff:
```python
import functools
import math

import jax
import jax.numpy as jnp
from jax import lax
from jax.experimental import pallas as pl
from jax.experimental.pallas import tpu as pltpu
from jax.sharding import PartitionSpec as P

SECTION, CTX, WT = "section", "ctx", "wt"
QKV, PROJ, FC, OUT = range(4)
OWN, NORM, SCORES, MIXED, GATHERED, ACTIVE, RESULT = range(7)
START, HIDDEN, SECOND, SUM, HEADS, BACK, THERE, FIRST, END = range(9)
FULL, MOVED, SEND, CAME, REDUCE, DONE, HOP, OWNED, TOKEN = range(9)

HEAD_DIM = 64
NEG = -1000000000.0
LANES = 128


def nt_dot(left, right):
    return lax.dot_general(left, right, (((1,), (1,)), ((), ())), preferred_element_type=jnp.float32)


def nn_dot(left, right):
    return jnp.dot(left, right, preferred_element_type=jnp.float32)


def causal_scores(keys, query, tile):
    scores = nt_dot(keys, query)
    edge = scores.shape[0] - tile
    key_at = lax.broadcasted_iota(jnp.int32, (tile, tile), 0)
    query_at = lax.broadcasted_iota(jnp.int32, (tile, tile), 1)
    last = jnp.where(key_at <= query_at, scores[edge:], NEG)
    return jnp.concatenate([scores[:edge], last], 0) if edge else last


def attend_kernel(block, tile, heads, place, qkv, out, log_total, query, keyed, valued, mixed):
    length, three = qkv.shape
    span = three // 3
    lane = lax.broadcasted_iota(jnp.int32, (tile, LANES), 1)

    def pair(index, carry):
        start = pl.multiple_of(index * LANES, LANES)
        for at in range(length // block):
            rows = pl.ds(pl.multiple_of(place[at] * block, block), block)
            here = pl.ds(at * block, block)
            query[here, :] = qkv[rows, pl.ds(start, LANES)] * (HEAD_DIM ** (-0.5))
            keyed[here, :] = qkv[rows, pl.ds(span + start, LANES)]
            valued[:, here] = qkv[rows, pl.ds(2 * span + start, LANES)].T

        for half in range(2):

            @pl.when(2 * index + half < heads)
            def _():
                mine = (lane < HEAD_DIM) if half == 0 else (lane >= HEAD_DIM)
                features = slice(half * HEAD_DIM, (half + 1) * HEAD_DIM)
                for at in range(length // tile):
                    seen = (at + 1) * tile
                    cols = slice(at * tile, seen)
                    part = jnp.where(mine, query[cols, :], 0)
                    scores = causal_scores(keyed[:seen, :], part, tile)
                    highest = jnp.max(scores, 0, keepdims=True)
                    exponent = jnp.exp(scores - highest)
                    total = jnp.sum(exponent, 0, keepdims=True)
                    result = nn_dot(valued[features, :seen], exponent.astype(jnp.bfloat16))
                    mixed[features, cols] = result * (1.0 / total)
                    log_total[pl.ds(2 * index + half, 1), cols] = highest + jnp.log(total)

        for at in range(length // block):
            rows = pl.ds(pl.multiple_of(place[at] * block, block), block)
            out[rows, pl.ds(start, LANES)] = mixed[:, at * block : (at + 1) * block].T.astype(out.dtype)
        return carry

    mixed[...] = jnp.zeros_like(mixed)
    lax.fori_loop(0, span // LANES, pair, 0)


def attend(place, qkv, heads, block):
    length, three = qkv.shape
    span = three // 3
    tile = min(256, length)
    rows = -(-span // HEAD_DIM // 8) * 8
    vmem = pl.BlockSpec(memory_space=pltpu.VMEM)
    return pl.pallas_call(
        functools.partial(attend_kernel, block, tile, heads),
        out_shape=(
            jax.ShapeDtypeStruct((length, span), jnp.bfloat16),
            jax.ShapeDtypeStruct((rows, length), jnp.float32),
        ),
        in_specs=[pl.BlockSpec(memory_space=pltpu.SMEM), vmem],
        out_specs=(vmem, vmem),
        scratch_shapes=[
            pltpu.VMEM((length, LANES), jnp.bfloat16),
            pltpu.VMEM((length, LANES), jnp.bfloat16),
            pltpu.VMEM((LANES, length), jnp.bfloat16),
            pltpu.VMEM((LANES, length), jnp.float32),
        ],
        compiler_params=pltpu.CompilerParams(vmem_limit_bytes=40 * 1024 * 1024),
        cost_estimate=pl.CostEstimate(
            flops=0, bytes_accessed=0, transcendentals=0
        ),
    )(place, qkv)


def attend_back_kernel(
    block, tile, heads, place, qkv, grad_mixed, log_total, out,
    query, keyed, keyed_t, valued, grad, grad_query, grad_key, grad_value,
):
    length, three = qkv.shape
    span = three // 3
    scale = HEAD_DIM ** (-0.5)
    lane = lax.broadcasted_iota(jnp.int32, (tile, LANES), 1)

    def pair(index, carry):
        start = pl.multiple_of(index * LANES, LANES)
        for at in range(length // block):
            rows = pl.ds(pl.multiple_of(place[at] * block, block), block)
            here = pl.ds(at * block, block)
            query[here, :] = qkv[rows, pl.ds(start, LANES)] * scale
            key_part = qkv[rows, pl.ds(span + start, LANES)]
            keyed[here, :] = key_part
            keyed_t[:, here] = key_part.T
            valued[here, :] = qkv[rows, pl.ds(2 * span + start, LANES)]
            grad[here, :] = grad_mixed[rows, pl.ds(start, LANES)]
        grad_query[...] = jnp.zeros_like(grad_query)
        grad_key[...] = jnp.zeros_like(grad_key)
        grad_value[...] = jnp.zeros_like(grad_value)

        for half in range(2):

            @pl.when(2 * index + half < heads)
            def _():
                mine = (lane < HEAD_DIM) if half == 0 else (lane >= HEAD_DIM)
                features = slice(half * HEAD_DIM, (half + 1) * HEAD_DIM)
                for at in range(length // tile):
                    seen = (at + 1) * tile
                    cols = slice(at * tile, seen)
                    part = jnp.where(mine, query[cols, :], 0)
                    grad_part = jnp.where(mine, grad[cols, :], 0)
                    scores = causal_scores(keyed[:seen, :], part, tile)
                    chance = jnp.exp(scores - log_total[pl.ds(2 * index + half, 1), cols])
                    grad_chance = nt_dot(valued[:seen, :], grad_part)
                    inner = jnp.sum(chance * grad_chance, 0, keepdims=True)
                    grad_scores = (chance * (grad_chance - inner)).astype(jnp.bfloat16)
                    grad_value[:seen, :] += nn_dot(chance.astype(jnp.bfloat16), grad_part)
                    grad_key[:seen, :] += nn_dot(grad_scores, part)
                    grad_query[features, cols] = nn_dot(keyed_t[features, :seen], grad_scores) * scale

        for at in range(length // block):
            rows = pl.ds(pl.multiple_of(place[at] * block, block), block)
            here = slice(at * block, (at + 1) * block)
            out[rows, pl.ds(start, LANES)] = grad_query[:, here].T.astype(out.dtype)
            out[rows, pl.ds(span + start, LANES)] = grad_key[here, :].astype(out.dtype)
            out[rows, pl.ds(2 * span + start, LANES)] = grad_value[here, :].astype(out.dtype)
        return carry

    lax.fori_loop(0, span // LANES, pair, 0)


def attend_back(place, qkv, grad_mixed, log_total, heads, block):
    length, three = qkv.shape
    span = three // 3
    tile = min(256, length)
    vmem = pl.BlockSpec(memory_space=pltpu.VMEM)
    return pl.pallas_call(
        functools.partial(attend_back_kernel, block, tile, heads),
        out_shape=jax.ShapeDtypeStruct((length, three), jnp.bfloat16),
        in_specs=[pl.BlockSpec(memory_space=pltpu.SMEM), vmem, vmem, vmem],
        out_specs=vmem,
        scratch_shapes=[
            pltpu.VMEM((length, LANES), jnp.bfloat16),
            pltpu.VMEM((length, LANES), jnp.bfloat16),
            pltpu.VMEM((LANES, length), jnp.bfloat16),
            pltpu.VMEM((length, LANES), jnp.bfloat16),
            pltpu.VMEM((length, LANES), jnp.bfloat16),
            pltpu.VMEM((LANES, length), jnp.float32),
            pltpu.VMEM((length, LANES), jnp.float32),
            pltpu.VMEM((length, LANES), jnp.float32),
        ],
        compiler_params=pltpu.CompilerParams(vmem_limit_bytes=48 * 1024 * 1024),
        cost_estimate=pl.CostEstimate(
            flops=0, bytes_accessed=0, transcendentals=0
        ),
    )(place, qkv, grad_mixed, log_total)


EPS = 1e-05
GELU_A = math.sqrt(2.0 / math.pi)
GELU_B = 0.044715


def flip(axis, bit):
    return [(at, at ^ bit) for at in range(lax.axis_size(axis))]


def swap(value, axis, bit=1):
    return lax.ppermute(value, axis, flip(axis, bit))


def bits_of(axis):
    bits, bit = [], 1
    while bit < lax.axis_size(axis):
        bits.append(bit)
        bit *= 2
    return bits


def gathered(value, axis):
    pieces = {0: value}
    for bit in reversed(bits_of(axis)):
        for at in list(pieces):
            pieces[at | bit] = swap(pieces[at], axis, bit)
    return [pieces[at] for at in range(lax.axis_size(axis))]


def gathered_whole(value, axis):
    pieces = {0: value}
    for bit in reversed(bits_of(axis)):
        held = list(pieces)
        for at, came in zip(held, together([pieces[at] for at in held], axis, bit)):
            pieces[at | bit] = came
    return [pieces[at] for at in range(lax.axis_size(axis))]


def together(pieces, axis, bit):
    if len(pieces) == 1:
        return [swap(pieces[0], axis, bit)]
    came = swap(jnp.concatenate(pieces), axis, bit)
    rows = pieces[0].shape[0]
    return [came[at * rows : (at + 1) * rows] for at in range(len(pieces))]


def summed(pieces, axis, bits=None):
    pieces = dict(pieces) if isinstance(pieces, dict) else dict(enumerate(pieces))
    for bit in bits_of(axis) if bits is None else bits:
        for at in sorted(pieces, reverse=True):
            if at & bit:
                came = swap(pieces.pop(at).astype(jnp.bfloat16), axis, bit)
                pieces[at ^ bit] = pieces[at ^ bit].astype(jnp.float32) + came.astype(jnp.float32)
    return pieces[0] if len(pieces) == 1 else pieces


def exchanged(pieces, axis):
    return [swap(piece, axis, at) if at else piece for at, piece in enumerate(pieces)]


def at_once(go, step, operands, aside=None):
    aside = aside or []
    counts = [len(inputs) for unused, inputs in aside]

    def both(operands, inputs):
        results, at = [], 0
        for (work, unused), count in zip(aside, counts):
            results.append(work(*inputs[at : at + count]))
            at += count
        return step(*operands), results

    inputs = [value for unused, values in aside for value in values]
    shapes = jax.eval_shape(both, operands, inputs)

    def nothing(*unused):
        return jax.tree.map(lambda shape: jnp.zeros(shape.shape, shape.dtype), shapes)

    return lax.cond(go, both, nothing, operands, inputs)


def by_owner(pieces, axis):
    here = lax.axis_index(axis)
    whole = jnp.zeros((len(pieces),) + pieces[0].shape, pieces[0].dtype)
    for at, piece in enumerate(pieces):
        whole = lax.dynamic_update_index_in_dim(whole, piece, here ^ at, 0)
    return whole


def after(value, *marks):
    return lax.optimization_barrier(marks + (value,))[-1]


def tied(*values):
    return lax.optimization_barrier(values)


def over_wt(value, tiled=True):
    return lax.all_gather(value, WT, axis=0, tiled=tiled)


def scatter_wt(value, tiled=True):
    return lax.psum_scatter(value, WT, scatter_dimension=0, tiled=tiled)


def dot(left, right):
    return jnp.dot(left, right, preferred_element_type=jnp.float32)


def dot_nt(left, right):
    return lax.dot_general(left, right, (((1,), (1,)), ((), ())), preferred_element_type=jnp.float32)


def dot_tn(left, right):
    return lax.dot_general(left, right, (((0,), (0,)), ((), ())), preferred_element_type=jnp.float32)


def low(value):
    return value.astype(jnp.bfloat16)


def wide(value):
    return value.astype(jnp.float32)


def normed(values):
    center = values - jnp.mean(values, -1, keepdims=True)
    rate = lax.rsqrt(jnp.mean(center * center, -1, keepdims=True) + EPS)
    return center * rate, rate


def norm_back(grad, gain, values):
    unit, rate = normed(values)
    inner = grad * gain
    back = (
        inner
        - jnp.mean(inner, -1, keepdims=True)
        - unit * jnp.mean(inner * unit, -1, keepdims=True)
    ) * rate
    return back, jnp.sum(grad * unit, 0), jnp.sum(grad, 0)


def gelu(value):
    return 0.5 * value * (1.0 + jnp.tanh(GELU_A * (value + GELU_B * value * value * value)))


def gelu_slope(value):
    square = value * value
    bend = jnp.tanh(GELU_A * (value + GELU_B * value * square))
    return 0.5 * (1.0 + bend) + 0.5 * value * (1.0 - bend * bend) * (
        GELU_A * (1.0 + 3.0 * GELU_B * square)
    )


def joined_kernel(count, segments, at, *refs):
    out, pieces = refs[-1], refs[:-1]
    kinds = len(pieces) // count
    picked = {}
    for kind, owner, source, target, columns in segments:
        if (kind, owner) not in picked:
            value = pieces[kind * count][...].astype(jnp.float32)
            for step in range(1, count):
                other = pieces[kind * count + step][...].astype(jnp.float32)
                value = jnp.where((at[0] ^ owner) == step, other, value)
            picked[kind, owner] = value
        out[:, target : target + columns] = picked[kind, owner][:, source : source + columns]
    assert kinds * count == len(pieces)


def joined_columns(pieces, segments, ci, columns):
    flat = [piece for kind in pieces for piece in kind]
    rows = flat[0].shape[0]
    tile = 80 if rows % 80 == 0 else rows
    return pl.pallas_call(
        functools.partial(joined_kernel, len(pieces[0]), segments),
        out_shape=jax.ShapeDtypeStruct((rows, columns), jnp.float32),
        grid=(rows // tile,),
        in_specs=[pl.BlockSpec(memory_space=pltpu.SMEM)]
        + [pl.BlockSpec((tile, piece.shape[1]), lambda at: (at, 0)) for piece in flat],
        out_specs=pl.BlockSpec((tile, columns), lambda at: (at, 0)),
        compiler_params=pltpu.CompilerParams(vmem_limit_bytes=48 * 1024 * 1024),
        cost_estimate=pl.CostEstimate(
            flops=0, bytes_accessed=6 * rows * columns, transcendentals=0
        ),
    )(ci.reshape(1), *flat)


class Plan:
    def __init__(self, width, hidden_rows, go):
        self.go = go
        self.count = lax.axis_size(CTX)
        self.ci = lax.axis_index(CTX)
        self.first = lax.axis_index(SECTION) == 0
        self.xi = lax.axis_index(SECTION)
        self.wi = lax.axis_index(WT)
        self.width = width
        heads = width // HEAD_DIM
        stride = heads // self.count
        self.heads = heads - stride * (self.count - 1)
        self.step = stride * HEAD_DIM
        self.span = (self.heads + self.heads % 2) * HEAD_DIM
        self.padded = self.step * (self.count - 1) + self.span
        self.owned = jnp.where(self.ci == self.count - 1, self.heads, stride) * HEAD_DIM
        self.part = hidden_rows // self.count
        self.half = self.part // 2
        self.shard = width // lax.axis_size(WT)
        self.proj_rows = -(-self.shard // self.count // 16) * 16

    def proj_start(self, index):
        return jnp.minimum(index * self.proj_rows, self.shard - self.proj_rows)

    def gathered(self, value):
        def step(value):
            return gathered(value, CTX)[1:]

        return [value] + at_once(self.go, step, [value])[0]

    def exchanged(self, pieces, aside=None):
        def step(*pieces):
            return [swap(piece, CTX, at + 1) for at, piece in enumerate(pieces)]

        came, extra = at_once(self.go, step, pieces[1:], aside)
        return pieces[:1] + came, extra

    def summed(self, value, aside=None):
        def step(value):
            return wide(summed(cut(value, self.count), CTX))

        return at_once(self.go, step, [value], aside)

    def proj_parts(self, left, right):
        parts = grad_dot(left, right).reshape(-1, self.shard, self.width)
        return [
            lax.dynamic_slice_in_dim(parts, self.proj_start(self.ci ^ at), self.proj_rows, 1)
            for at in range(self.count)
        ]

    def padded_out(self, array):
        return jnp.pad(array, [(0, 0)] * (array.ndim - 1) + [(0, self.padded - array.shape[-1])])

    def window(self, padded, index):
        return lax.dynamic_slice_in_dim(padded, index * self.step, self.span, padded.ndim - 1)

    def joined(self, ordered):
        last = self.width - self.step * (self.count - 1)
        parts = [ordered[at, ..., : self.step] for at in range(self.count - 1)]
        return jnp.concatenate(parts + [ordered[self.count - 1, ..., :last]], -1)


def joined_rows_kernel(at, *refs):
    out, pieces = refs[-1], refs[:-1]
    step = pl.program_id(0)
    for index, piece in enumerate(pieces):

        @pl.when(step == index)
        def _():
            out[...] = piece[...].astype(jnp.float32)


def joined_rows(pieces, ci):
    rows, columns = pieces[0].shape
    count = len(pieces)
    if rows % 8:
        return wide(by_owner(pieces, CTX)).reshape(count * rows, columns)
    return pl.pallas_call(
        joined_rows_kernel,
        out_shape=jax.ShapeDtypeStruct((count * rows, columns), jnp.float32),
        grid_spec=pltpu.PrefetchScalarGridSpec(
            num_scalar_prefetch=1,
            grid=(count,),
            in_specs=[pl.BlockSpec((rows, columns), lambda step, at: (0, 0))] * count,
            out_specs=pl.BlockSpec((rows, columns), lambda step, at: (at[0] ^ step, 0)),
        ),
        compiler_params=pltpu.CompilerParams(vmem_limit_bytes=48 * 1024 * 1024),
        cost_estimate=pl.CostEstimate(
            flops=0, bytes_accessed=6 * count * rows * columns, transcendentals=0
        ),
    )(ci.reshape(1), *pieces)


def placed_kernel(owners, start, *refs):
    out, pieces = refs[-1], refs[:-1]
    rows = pieces[0].shape[0] // owners
    shard = out.shape[0] // owners
    for at, piece in enumerate(pieces):
        for owner in range(owners):
            here = pl.ds(pl.multiple_of(owner * shard + start[at], 16), rows)
            out[here, :] = piece[owner * rows : (owner + 1) * rows, :].astype(out.dtype)


def placed_rows(pieces, starts, owners, shard, dtype):
    columns = pieces[0].shape[1]
    vmem = pl.BlockSpec(memory_space=pltpu.VMEM)
    return pl.pallas_call(
        functools.partial(placed_kernel, owners),
        out_shape=jax.ShapeDtypeStruct((owners * shard, columns), dtype),
        in_specs=[pl.BlockSpec(memory_space=pltpu.SMEM)] + [vmem] * len(pieces),
        out_specs=vmem,
        compiler_params=pltpu.CompilerParams(vmem_limit_bytes=48 * 1024 * 1024),
        cost_estimate=pl.CostEstimate(
            flops=0, bytes_accessed=4 * owners * shard * columns, transcendentals=0
        ),
    )(jnp.stack(starts), *pieces)


def cut(value, count):
    rows = value.shape[0] // count
    return [value[at * rows : (at + 1) * rows] for at in range(count)]


def forward_layer(entering, weight, vectors, plan, place, block, pin):
    attn_gain, attn_shift, bias_qkv, proj_bias, mlp_gain, mlp_shift, fc_bias, out_bias = vectors
    stream = wide(entering)
    first_norm = pin(OWN, low(normed(stream)[0] * attn_gain + attn_shift))
    first_norm = jnp.concatenate(pin(NORM, plan.gathered(first_norm)))
    qkv = pin(SCORES, low(dot(first_norm, weight(QKV)) + bias_qkv))
    mixed, log_total = attend(place, qkv, plan.heads, block)
    mixed = pin(MIXED, mixed)
    mixed_all = plan.joined(by_owner(plan.exchanged(cut(mixed, plan.count))[0], CTX))
    middle = (dot(mixed_all, weight(PROJ)) + proj_bias) + stream
    second_norm = low(normed(middle)[0] * mlp_gain + mlp_shift)
    second_norm = jnp.concatenate(pin(GATHERED, plan.gathered(second_norm)))
    hidden = [dot(second_norm, part) + bias for part, bias in zip(weight(FC), fc_bias)]
    active = pin(ACTIVE, [low(gelu(part)) for part in hidden])

    def final(first_marks=(), last_marks=()):
        parts = after(active, *first_marks)
        w_out = weight(OUT)
        result = pin(RESULT, low(dot(parts[0], w_out[0]) + dot(parts[1], w_out[1])))
        return low((plan.summed(after(result, *last_marks))[0] + out_bias) + middle)

    kept = (stream, first_norm, qkv, log_total, mixed_all, middle, second_norm, hidden, active)
    return final, kept


def grad_dot(left, right):
    return low(dot_tn(left, right))


def grad_dot_all(left, *right):
    return low(dot_tn(left, jnp.concatenate(right)))


def backward_layer(coming, coming_all, kept, weight, vectors, plan, place, block, pin, aside):
    attn_gain, attn_shift, bias_qkv, proj_bias, mlp_gain, mlp_shift, fc_bias, out_bias = vectors
    stream, first_norm, qkv, log_total, mixed_all, middle, second_norm, hidden, active = kept
    grads, sums = {}, {}
    w_fc, w_out = weight(FC), weight(OUT)
    grads[OUT] = [(grad_dot_all, [part] + coming_all) for part in active]
    coming_all = pin(START, coming_all, grads)
    grads[OUT] = [(grad_dot_all, [part] + coming_all) for part in active]
    coming_whole = jnp.concatenate(coming_all)
    grad_hidden = [
        low(dot_nt(coming_whole, part) * gelu_slope(at)) for part, at in zip(w_out, hidden)
    ]
    grads[FC] = [(grad_dot, [second_norm, part]) for part in grad_hidden]
    grad_hidden = pin(HIDDEN, grad_hidden, grads)
    grads[FC] = [(grad_dot, [second_norm, part]) for part in grad_hidden]
    grad_second = low(dot_nt(grad_hidden[0], w_fc[0]) + dot_nt(grad_hidden[1], w_fc[1]))
    grad_second = pin(SECOND, grad_second, grads)
    grad_norm = aside(SUM, lambda extra: plan.summed(grad_second, extra), grads)
    grad_norm = pin(SUM, grad_norm, grads)
    back, sums["mlp_gain"], sums["mlp_shift"] = norm_back(grad_norm, mlp_gain, middle)
    grad_final = wide(coming)
    grad_middle = back + grad_final
    branch = low(grad_middle)
    grad_mixed = plan.padded_out(low(dot_nt(branch, weight(PROJ))))
    pieces = [plan.window(grad_mixed, plan.ci ^ at) for at in range(plan.count)]
    grads[PROJ] = [(plan.proj_parts, [mixed_all, branch])]
    grad_heads = aside(HEADS, lambda extra: plan.exchanged(pieces, extra), grads)
    grad_heads = jnp.concatenate(grad_heads)
    column = lax.broadcasted_iota(jnp.int32, grad_heads.shape, 1)
    grad_heads = pin(HEADS, jnp.where(column < plan.owned, grad_heads, 0), grads)
    grad_qkv = attend_back(place, qkv, grad_heads, log_total, plan.heads, block)
    grad_qkv = pin(BACK, grad_qkv, grads)
    grads[QKV] = [(grad_dot, [first_norm, grad_qkv])]
    grad_qkv = pin(THERE, grad_qkv, grads)
    grad_first = pin(FIRST, low(dot_nt(grad_qkv, weight(QKV))), grads)
    grad_norm = aside(END, lambda extra: plan.summed(grad_first, extra), grads)
    grad_norm = pin(END, grad_norm, grads)
    back, sums["attn_gain"], sums["attn_shift"] = norm_back(grad_norm, attn_gain, stream)
    leaving = low(back + grad_middle)
    sums["fc"] = [jnp.sum(wide(part), 0) for part in grad_hidden]
    sums["out"] = jnp.sum(grad_final, 0)
    sums["proj"] = jnp.sum(wide(branch), 0)
    sums["qkv"] = jnp.sum(wide(grad_qkv), 0)
    return leaving, sums


def body(
    feed,
    block_order,
    attn_gain,
    attn_shift,
    w_qkv,
    query_bias,
    value_bias,
    w_proj,
    proj_bias,
    mlp_gain,
    mlp_shift,
    w_fc,
    fc_bias,
    w_out,
    out_bias,
):
    width = w_proj.shape[2]
    shard = w_proj.shape[1]
    hidden_rows = w_out.shape[1]
    plan = Plan(width, hidden_rows, block_order[0] >= 0)
    count, owners = plan.count, lax.axis_size(WT)
    first, xi, ci = plan.first, plan.xi, plan.ci
    part, half, span = plan.part, plan.half, plan.span
    rows = feed.shape[3]
    block = rows // 2

    def mine_other(mine, other):
        return (jnp.where(first, mine, other), jnp.where(first, other, mine))

    slots = jnp.arange(2 * count, dtype=jnp.int32)
    held = 2 * (ci ^ (slots // 2)) + slots % 2
    table = (held[:, None] == slots[None, :]).astype(jnp.int32)
    blocks_held = jnp.sum(table * block_order[None, :], 1)
    found = (blocks_held[None, :] == slots[:, None]).astype(jnp.int32)
    place = jnp.sum(found * slots[None, :], 1)

    fc_part = lax.dynamic_slice_in_dim(fc_bias[0], ci * part, part, 0)
    names = (attn_gain, attn_shift, query_bias, value_bias, proj_bias, mlp_gain, mlp_shift, out_bias)
    small = jnp.concatenate([vector[0] for vector in names] + [fc_part])
    local = feed[0, :, 0]
    feed_own = lax.dynamic_index_in_dim(local, xi, 0, keepdims=False)
    feed_gone = lax.dynamic_index_in_dim(local, 1 - xi, 0, keepdims=False)

    def fc_shard(duty):
        return jnp.concatenate(
            [
                lax.dynamic_slice_in_dim(
                    w_fc[0], owner * hidden_rows + ci * part + duty * half, half, 1
                )
                for owner in range(owners)
            ],
            1,
        )

    def out_shard(duty):
        return lax.dynamic_slice_in_dim(w_out[0], ci * part + duty * half, half, 0)

    qkv_shard = jnp.concatenate(
        [
            plan.window(plan.padded_out(w_qkv[0][:, at * width : (at + 1) * width]), ci)
            for at in range(3)
        ],
        1,
    )
    proj_shard = lax.dynamic_slice_in_dim(w_proj[0], plan.proj_start(ci), plan.proj_rows, 0)

    def qkv_half(duty):
        return lax.dynamic_slice_in_dim(qkv_shard, duty * (shard // 2), shard // 2, 0)

    whole_here = {(OUT, 1)}
    own_shards = {QKV: qkv_half(xi), PROJ: proj_shard, FC: fc_shard(xi), OUT: out_shard(xi)}
    gone = {QKV: qkv_half(1 - xi), PROJ: proj_shard, FC: fc_shard(1 - xi), OUT: out_shard(1 - xi)}
    came = {QKV: swap(gone[QKV], SECTION)}
    started = [came[QKV]]
    feed_gone = after(feed_gone, gone[QKV])
    feed_came = swap(feed_gone, SECTION)
    small_came = swap(after(small, feed_gone), SECTION)
    started += [feed_came, small_came]
    before = feed_gone
    for name in (PROJ, FC, OUT):
        before = after(gone[name], before)
        came[name] = swap(before, SECTION)
        started.append(came[name])
    shards = {name: mine_other(own_shards[name], came[name]) for name in (QKV, PROJ)}
    last_gone = after(own_shards[OUT], before)
    last_came = swap(last_gone, SECTION)

    entering, coming = mine_other(feed_own, feed_came)
    small = jnp.stack(mine_other(small, small_came))
    small = wide(by_owner(gathered(small, WT), WT))

    def vectors_of(layer):
        full = jnp.swapaxes(small[:, layer, : 8 * shard].reshape(owners, 8, shard), 0, 1)
        full = full.reshape(8, owners * shard)
        hidden = small[:, layer, 8 * shard :]
        halves = [
            lax.dynamic_slice_in_dim(hidden, duty * half, half, 1).reshape(-1) for duty in (xi, 1 - xi)
        ]
        query = plan.window(plan.padded_out(full[2]), ci)
        value = plan.window(plan.padded_out(full[3]), ci)
        bias_qkv = jnp.concatenate([query, jnp.zeros_like(query), value])
        return (full[0], full[1], bias_qkv, full[4], full[5], full[6], halves, full[7])

    vectors = [vectors_of(layer) for layer in range(2)]
    full, operands = {}, []
    tiny = small_came[:128]

    def gather_over_wt(keys, *marks):
        for key in keys:
            name, layer = key
            piece = after(shards[name][layer], *operands[-1:], *marks)
            operands.append(piece)
            full[key] = over_wt(piece)
            started.append(full[key])

    gather_over_wt([(QKV, 0)])
    gather_over_wt([(PROJ, 0)], feed_came, small_came)

    made, moved = {}, {}

    def move(key):
        if key not in moved:
            value = full[key]
            if key[0] == PROJ:
                moved[key] = gathered(value, CTX)
            elif key in whole_here:
                moved[key] = None
            else:
                moved[key] = swap(value, SECTION)
            started.append(moved[key])
        return moved[key]

    def weight(layer, name):
        key = (name, layer)
        if key in made:
            return made[key]
        other, value = move(key), full[key]
        if name == QKV:
            halves = [part.reshape(owners, shard // 2, 3 * span) for part in mine_other(value, other)]
            result = jnp.stack(halves, 1).reshape(width, 3 * span)
        elif name == PROJ:
            starts = [plan.proj_start(ci ^ at) for at in range(count)]
            result = placed_rows(other, starts, owners, shard, jnp.bfloat16)
        elif key in whole_here:
            result = tuple(value[:, at].reshape(-1, value.shape[-1]) for at in range(2))
        else:
            result = (value, other)
        made[key] = result
        return result

    front = {
        (0, OWN): ((FULL, QKV, 0),),
        (0, NORM): ((FULL, PROJ, 0),),
        (0, MIXED): ((MOVED, PROJ, 0), (FULL, FC, 0)),
        (0, GATHERED): ((MOVED, FC, 0), (FULL, OUT, 0)),
        (0, ACTIVE): ((FULL, PROJ, 1),),
        (0, RESULT): ((MOVED, PROJ, 1), (FULL, QKV, 1)),
        (1, NORM): ((MOVED, QKV, 1), (FULL, FC, 1)),
        (1, GATHERED): ((MOVED, FC, 1),),
    }

    def forward_pin(layer):
        def pin(point, value):
            if (layer, point) == (0, OWN):
                for name in (FC, OUT):
                    shards[name] = mine_other(own_shards[name], after(came[name], value))
                keys = [(FC, 0), (OUT, 0), (PROJ, 1), (QKV, 1), (FC, 1)]
                gather_over_wt(keys, value)
            if (layer, point) == (0, MIXED):
                last, value = tied(last_came, value)
                shards[OUT, 1] = jnp.stack([shards[OUT][1], mine_other(gone[OUT], last)[1]])
            if (layer, point) == (0, ACTIVE):
                piece, value = tied(shards[OUT, 1], value)
                full[OUT, 1] = over_wt(after(piece, operands[-1]), tiled=False)
                started.append(full[OUT, 1])
            for kind, *key in front.get((layer, point), ()):
                key = tuple(key)
                if kind == FULL:
                    full[key], value = tied(full[key], value)
                    move(key)
                else:
                    moved[key], value = tied(moved[key], value)
            return value

        return pin

    kept = []
    state = entering
    for layer in range(2):
        state, kept_here = forward_layer(
            state,
            functools.partial(weight, layer),
            vectors[layer],
            plan,
            place,
            block,
            forward_pin(layer),
        )
        kept.append(kept_here)
        if layer == 0:
            state = state()

    whole_sums = {(OUT, 1)}
    dots, sent, ready, sums, hops, order = {}, {}, {}, {}, {}, []

    def grad_of(key, at, grads):
        if (key, at) not in dots:
            work, inputs = grads[key[0]][at]
            dots[key, at] = work(*inputs)
        return dots[key, at]

    def prepared(key, grads):
        if key[0] == QKV:
            parts = grad_of(key, 0, grads).reshape(owners, 2, shard // 2, 3 * span)
            mine, away = (
                lax.dynamic_index_in_dim(parts, at, 1, keepdims=False).reshape(-1, 3 * span)
                for at in (xi, 1 - xi)
            )
            dots[key, QKV] = mine
            return away
        if key[0] == PROJ:
            return grad_of(key, 0, grads)
        if key in whole_sums:
            halves = [grad_of(key, at, grads).reshape(owners, half, width) for at in range(2)]
            return jnp.stack(halves, 1).reshape(-1, width)
        return grad_of(key, 1, grads)

    def core(*parts):
        return summed(parts, CTX, bits_of(CTX)[:-1])

    def start(key, away):
        if key[0] == PROJ:
            sent[key] = summed(away, CTX, bits_of(CTX)[-1:])
        elif key in whole_sums:
            sent[key] = away
        else:
            sent[key] = swap(away, SECTION)
        started.append(sent[key])

    def add(key, grads):
        came = sent[key]
        if key[0] == PROJ:
            return low(came).reshape(-1, width)
        if key in whole_sums:
            return came
        mine = dots[key, QKV] if key[0] == QKV else grad_of(key, 0, grads)
        return low(wide(came) + wide(mine))

    def hop(key):
        if key not in hops:
            hops[key] = lax.ppermute(sums[key], SECTION, [(1 - key[1], key[1])])
            started.append(hops[key])
        return hops[key]

    def both_halves(key):
        value, came = sums[key], hop(key)
        rows = value.shape[0]
        if key in whole_sums:
            rows = rows // 2
            own = low(wide(value[:rows]) + wide(came[rows:]))
            came = low(wide(value[rows:]) + wide(came[:rows]))
            value = own
        return (value, came) if key[1] == 0 else (came, value)

    def ordered(name):
        late, early = both_halves((name, 0)), both_halves((name, 1))
        return tuple(jnp.where(first, a, b) for a, b in zip(late, early))

    owned = {}
    back = {
        (1, START): ((SEND, OUT, 1), (CAME, OUT, 1), (REDUCE, OUT, 1)),
        (1, HIDDEN): ((SEND, FC, 1),),
        (1, HEADS): ((CAME, FC, 1), (SEND, PROJ, 1), (TOKEN,)),
        (1, BACK): ((DONE, OUT, 1), (REDUCE, FC, 1)),
        (1, FIRST): ((CAME, PROJ, 1),),
        (1, END): ((HOP, OUT, 1), (REDUCE, PROJ, 1), (SEND, QKV, 1), (TOKEN,)),
        (0, START): ((DONE, FC, 1), (SEND, OUT, 0)),
        (0, HIDDEN): ((CAME, QKV, 1),),
        (0, SECOND): ((REDUCE, QKV, 1),),
        (0, SUM): ((CAME, OUT, 0), (SEND, FC, 0), (TOKEN,), (DONE, PROJ, 1)),
        (0, HEADS): ((REDUCE, OUT, 0), (SEND, PROJ, 0), (TOKEN,)),
        (0, BACK): ((DONE, QKV, 1), (DONE, OUT, 0), (CAME, FC, 0), (REDUCE, FC, 0)),
        (0, THERE): ((SEND, QKV, 0), (TOKEN,), (HOP, OUT, 0)),
        (0, FIRST): ((CAME, PROJ, 0), (OWNED, OUT, 0)),
    }
    beside = {
        (1, HEADS): ((PROJ, 0),),
        (1, END): ((QKV, 0),),
        (0, SUM): ((OUT, 0),),
        (0, HEADS): ((PROJ, 0),),
    }

    def backward_pin(layer):
        def pin(point, value, grads):
            for kind, *key in back.get((layer, point), ()):
                key = tuple(key)
                if kind == SEND:
                    away = prepared(key, grads)
                    if key[0] == PROJ:
                        away = at_once(plan.go, core, away)[0]
                    away, value = tied(away, value)
                    start(key, away)
                elif kind == CAME:
                    sent[key], value = tied(sent[key], value)
                    ready[key] = add(key, grads if key[1] == layer else all_grads[key[1]])
                elif kind == TOKEN:
                    token, value = tied(tiny, value)
                    token, value = tied(swap(token, CTX), value)
                    started.append(token)
                elif kind == OWNED:
                    whole, value = tied(jnp.concatenate(ordered(key[0])), value)
                    owned[key[0]] = gathered_whole(whole, CTX)
                elif kind == HOP:
                    hops[key], value = tied(hop(key), value)
                elif kind == DONE:
                    sums[key], value = tied(sums[key], value)
                elif kind == REDUCE:
                    if order:
                        ready[key] = after(ready[key], ready[order[-1]])
                    order.append(key)
                    sums[key] = scatter_wt(ready[key])
                    started.append(sums[key])
            all_grads[layer] = grads
            return value

        return pin

    def beside_of(layer):
        def aside(point, step, grads):
            wanted = beside.get((layer, point), ())
            value, extra = step([grads[name][at] for name, at in wanted])
            for (name, at), result in zip(wanted, extra):
                dots[(name, layer), at] = result
            return value

        return aside

    all_grads = {}
    vector_grads = [None, None]
    for layer in (1, 0):
        coming, vector_grads[layer] = backward_layer(
            coming,
            plan.gathered(coming),
            kept[layer],
            functools.partial(weight, layer),
            vectors[layer],
            plan,
            place,
            block,
            backward_pin(layer),
            beside_of(layer),
        )

    def to_owner(name):
        there = swap(jnp.where(first, sums[name, 1], sums[name, 0]), SECTION)
        return jnp.where(first, sums[name, 0], sums[name, 1]), there

    sent[QKV, 0], coming = tied(sent[QKV, 0], coming)
    ready[QKV, 0] = add((QKV, 0), None)
    sums[QKV, 0] = scatter_wt(after(ready[QKV, 0], sums[FC, 0]))
    fc_own, fc_there = to_owner(FC)
    fc_halves = (jnp.where(first, fc_own, fc_there), jnp.where(first, fc_there, fc_own))
    fc_parts = [gathered(value, CTX) for value in fc_halves]
    leaving = state([coming], [fc_there])
    sums[PROJ, 0] = scatter_wt(after(ready[PROJ, 0], sums[QKV, 0]))

    def packed(grads):
        def placed(piece):
            zeros = jnp.zeros((plan.padded,), jnp.float32)
            return lax.dynamic_update_slice_in_dim(zeros, piece, ci * plan.step, 0)[:width]

        full = jnp.stack(
            [
                grads["attn_gain"],
                grads["attn_shift"],
                placed(grads["qkv"][:span]),
                placed(grads["qkv"][2 * span :]),
                grads["proj"],
                grads["mlp_gain"],
                grads["mlp_shift"],
                grads["out"],
            ]
        )
        full = jnp.swapaxes(full.reshape(8, owners, shard), 0, 1).reshape(owners, 8 * shard)
        halves = [piece.reshape(owners, half) for piece in grads["fc"]]
        halves = jnp.where(
            first, jnp.concatenate(halves, 1), jnp.concatenate(halves[::-1], 1)
        )
        zeros = jnp.zeros((owners, hidden_rows), jnp.float32)
        return jnp.concatenate(
            [full, lax.dynamic_update_slice_in_dim(zeros, halves, ci * part, 1)], 1
        )

    late, early = packed(vector_grads[0]), packed(vector_grads[1])
    early = after(early, leaving)
    total = jnp.where(first, late, early) + swap(jnp.where(first, early, late), SECTION)
    for bit in bits_of(CTX):
        total = total + swap(total, CTX, bit)
    pieces = {
        at: lax.dynamic_index_in_dim(total, plan.wi ^ at, 0, keepdims=False) for at in range(owners)
    }
    for bit in bits_of(WT):
        for at in sorted(pieces, reverse=True):
            if at & bit:
                pieces[at ^ bit] = pieces[at ^ bit] + swap(pieces.pop(at), WT, bit)
    total = pieces[0]
    vector_out = total[: 8 * shard].reshape(8, shard)
    fc_bias_out = total[8 * shard :]

    stays = jnp.where(first, coming, leaving)
    came = swap(jnp.where(first, leaving, coming), SECTION)
    result = jnp.where(first, jnp.stack([stays, came]), jnp.stack([came, stays]))
    result = result.reshape(1, 2, 1, rows, width)
    result = after(result, *jax.tree.leaves(started))
    out_grad = joined_rows(owned[OUT], ci)
    segments = [
        (kind, owner, at * half, at * hidden_rows + owner * part + kind * half, half)
        for at in range(owners)
        for owner in range(count)
        for kind in range(2)
    ]
    fc_grad = joined_columns(fc_parts, segments, ci, owners * hidden_rows)
    qkv_own, qkv_there = to_owner(QKV)
    qkv_halves = [jnp.where(first, qkv_own, qkv_there), jnp.where(first, qkv_there, qkv_own)]
    qkv_parts = gathered(jnp.concatenate(qkv_halves), CTX)
    segments = [
        (
            0,
            owner,
            at * span,
            at * width + owner * plan.step,
            plan.step if owner < count - 1 else width - plan.step * (count - 1),
        )
        for at in range(3)
        for owner in range(count)
    ]
    qkv_grad = joined_columns([qkv_parts], segments, ci, 3 * width)
    proj_own, proj_there = to_owner(PROJ)
    proj_parts = gathered(low(wide(proj_own) + wide(proj_there)), CTX)
    starts = [plan.proj_start(ci ^ at) for at in range(count)]
    proj_grad = placed_rows(proj_parts, starts, 1, shard, jnp.float32)

    return (
        result,
        vector_out[0][None],
        vector_out[1][None],
        qkv_grad[None],
        vector_out[2][None],
        vector_out[3][None],
        proj_grad[None],
        vector_out[4][None],
        vector_out[5][None],
        vector_out[6][None],
        fc_grad[None],
        fc_bias_out[None],
        out_grad[None],
        vector_out[7][None],
    )


def solution(mesh):
    return jax.shard_map(
        body,
        mesh=mesh,
        in_specs=(
            P(SECTION, None, WT, CTX, None),
            P(),
            P(SECTION, WT),
            P(SECTION, WT),
            P(SECTION, WT, None),
            P(SECTION, WT),
            P(SECTION, WT),
            P(SECTION, WT, None),
            P(SECTION, WT),
            P(SECTION, WT),
            P(SECTION, WT),
            P(SECTION, WT, None),
            P(SECTION, WT),
            P(SECTION, WT, None),
            P(SECTION, WT),
        ),
        out_specs=(
            P(SECTION, None, WT, CTX, None),
            P(SECTION, WT),
            P(SECTION, WT),
            P(SECTION, WT, None),
            P(SECTION, WT),
            P(SECTION, WT),
            P(SECTION, WT, None),
            P(SECTION, WT),
            P(SECTION, WT),
            P(SECTION, WT),
            P(SECTION, WT, None),
            P(SECTION, WT),
            P(SECTION, WT, None),
            P(SECTION, WT),
        ),
        check_vma=False,
    )
```

time: 1610 us -> 1220 us (0.76)
  waiting for transfers between devices: 771 us -> 473 us
  local copies, waits for them, and re-layouts: 268 us -> 159 us
  blocking collectives: 31.3 us -> 0 us
  other arithmetic: 87.1 us -> 118 us
  Pallas kernels: 73.4 us -> 103 us
    ppermute x96 -> x104, waiting for transfers between devices: 747 us -> 449 us  [swap(): return lax.ppermute(value, axis, flip(axis, bit))]
    another operation x36 -> x35, local copies, waits for them, and re-layouts: 66.6 us -> 10.3 us  [the longest x3 55 us: body(): fc_grad[None]]
    reshape x10 -> x4, local copies, waits for them, and re-layouts: 48 us -> 0.32 us  [packed(): halves = [piece.reshape(owners, half) for piece in grads['fc']]]
    unnamed x280 -> x326, local copies, waits for them, and re-layouts: 8.44 us -> 44.8 us
    unnamed x1 -> x0, blocking collectives: 31.3 us -> none
    pallas_call x0 -> x6, Pallas kernels: none -> 28.6 us  [the longest x2 12.8 us: joined_columns(): pl.pallas_call(functools.partial(joined_kernel, len(pieces[0]), segments)...]
    dynamic_update_slice x28 -> x11, local copies, waits for them, and re-layouts: 40.6 us -> 12.6 us  [by_owner(): whole = lax.dynamic_update_index_in_dim(whole, piece, here ^ at, 0)]
    optimization_barrier x0 -> x4, local copies, waits for them, and re-layouts: none -> 20.9 us  [tied(): return lax.optimization_barrier(values)]
  transfers between devices with their start and end apart: 112 -> 122, of which waited for: 50 -> 62; matrix products, arithmetic and copies ran while one was open for 27% -> 38% of each run, Pallas kernels for 3% -> 8%
where the time goes in v2:
time: 1220 us; the launch traced here: 1210 us
  waiting for transfers between devices  473 us (39%)
  matrix products  216 us (18%)
  local copies, waits for them, and re-layouts  159 us (13%)
  starting transfers between devices  120 us (10%)
  other arithmetic  118 us (10%)
  Pallas kernels  103 us (8%)
  between operations  16.8 us (1%)
    ppermute x104, waiting for transfers between devices, swap(): return lax.ppermute(value, axis, flip(axis, bit))  449 us
    ppermute x104, starting transfers between devices, swap(): return lax.ppermute(value, axis, flip(axis, bit))  113 us
    dot_general x12, matrix products, dot_tn(): lax.dot_general(left, right, (((0,), (0,)), ((), ())), preferred_element_...  75.6 us
    dot_general x12, matrix products, dot(): return jnp.dot(left, right, preferred_element_type=jnp.float32)  71.9 us
    dot_general x12, matrix products, dot_nt(): lax.dot_general(left, right, (((1,), (1,)), ((), ())), preferred_element_...  68 us
    unnamed x326, local copies, waits for them, and re-layouts  44.8 us
    pallas_call x2, Pallas kernels, attend_back(): pl.pallas_call(functools.partial(attend_back_kernel, block, tile, heads),...  42.3 us
    pallas_call x2, Pallas kernels, attend(): pl.pallas_call(functools.partial(attend_kernel, block, tile, heads), out_...  32.2 us
  transfers between devices with their start and end apart: 122, of which 62 were waited for; matrix products, arithmetic and copies ran while one was open for 38% of the time, Pallas kernels for 8%

profile of v2, /device:TPU:1, one launch (start us, length us, event | category | flops | bytes accessed | tf_op | source)
XLA Modules:
  0.0 1208.2 jit_solution(14696866987528670217)
XLA Ops:
  17.2 13.8 %collective-permute-done.52 = bf16[200,1536]{1,0:T(8,128)(2,1)S(1)} collective-permute-done((bf16[200,1536]{1,0:T(8,128)(2,1)}, bf16[200,1536]{1,0:T(8,128)(2,1)S(1)}, u32[]{:S(2)}, u32[]{:S(2)}) %collective-permute-start.52) | collective-permute-done | bytes 614432 | tf_op jit(solution)/shard_map/ppermute | solution.py:199
  40.8 11.5 collective-permute-done.54
  79.1 11.5 collective-permute-done.57
  98.8 23.1 %conditional.18 = (bf16[256,1600]{0,1:T(8,128)(2,1)}, bf16[256,1600]{0,1:T(8,128)(2,1)}, bf16[256,1600]{0,1:T(8,128)(2,1)}) conditional(s32[]{:T(128)} %bitcast.29, () %tuple.255, bf16[256,1600]{0,1:T(8,128)(2,1)S(1)} %fusion.73), branch_computations={%region_2.3_spmd, %region_3.4_spmd} | conditional | bytes 9830544 | solution.py:266
  105.5 8.1 collective-permute-done.1
  133.2 22.6 %collective-permute-done.63.refs_2_ = bf16[448,1600]{1,0:T(8,128)(2,1)S(1)} collective-permute-done((bf16[448,1600]{1,0:T(8,128)(2,1)}, bf16[448,1600]{1,0:T(8,128)(2,1)S(1)}, u32[]{:S(2)}, u32[]{:S(2)}) %collective-permute-start.63) | collective-permute-done | bytes 1433632 | tf_op jit(solution)/shard_map/ppermute | solution.py:199
  160.6 6.4 add_convert_fusion.11.qkv
  167.1 16.6 %shard_map.254 = (bf16[1024,512]{1,0:T(8,128)(2,1)}, f32[8,1024]{1,0:T(8,128)S(1)}) custom-call(s32[8]{0:T(128)S(1)} %select_reduce_fusion.place, bf16[1024,1536]{1,0:T(8,128)(2,1)S(1)} %add_convert_fusion.11.qkv), custom_call_target="tpu_custom_call" | custom-call | tf_op jit(solution)/shard_map/pallas_call | solution.py:86
  198.1 15.4 %conditional.19 = (bf16[1,256,512]{2,1,0:T(8,128)(2,1)}, bf16[1,256,512]{2,1,0:T(8,128)(2,1)}, bf16[1,256,512]{2,1,0:T(8,128)(2,1)}) conditional(s32[]{:T(128)} %bitcast.29, () %tuple.261, bf16[1024,512]{1,0:T(8,128)(2,1)} %get-tuple-element.392), branch_computations={%region_6.7_spmd, %region_7.8_spmd} | conditional | bytes 4718736 | solution.py:266
  201.5 6.8 collective-permute-done.24
  232.8 23.1 %conditional.20 = (bf16[256,1600]{0,1:T(8,128)(2,1)}, bf16[256,1600]{0,1:T(8,128)(2,1)}, bf16[256,1600]{0,1:T(8,128)(2,1)}) conditional(s32[]{:T(128)} %bitcast.29, () %tuple.262, bf16[256,1600]{0,1:T(8,128)(2,1)S(1)} %add_convert_fusion.18), branch_computations={%region_10.11_spmd, %region_11.12_spmd} | conditional | bytes 9830544 | solution.py:266
  235.0 17.0 %collective-permute-done.4 = bf16[256,1600]{0,1:T(8,128)(2,1)} collective-permute-done((bf16[256,1600]{0,1:T(8,128)(2,1)S(1)}, bf16[256,1600]{0,1:T(8,128)(2,1)}, u32[]{:S(2)}, u32[]{:S(2)}) %collective-permute-start.4) | collective-permute-done | bytes 819232 | tf_op jit(solution)/shard_map/cond/branch_1_fun/ppermute | solution.py:199
  265.9 7.2 fusion.31
  277.9 29.5 %collective-permute-done.69.refs_2_ = bf16[448,1600]{1,0:T(8,128)(2,1)S(1)} collective-permute-done((bf16[448,1600]{1,0:T(8,128)(2,1)}, bf16[448,1600]{1,0:T(8,128)(2,1)S(1)}, u32[]{:S(2)}, u32[]{:S(2)}) %collective-permute-start.69) | collective-permute-done | bytes 1433632 | tf_op jit(solution)/shard_map/ppermute | solution.py:199
  315.7 6.9 add_convert_fusion.9
  329.5 23.3 %conditional.25 = (bf16[256,1600]{0,1:T(8,128)(2,1)}, bf16[256,1600]{0,1:T(8,128)(2,1)}, bf16[256,1600]{0,1:T(8,128)(2,1)}) conditional(s32[]{:T(128)} %bitcast.29, () %tuple.278, bf16[256,1600]{0,1:T(8,128)(2,1)} %get-tuple-element.459), branch_computations={%region_24.25_spmd, %region_25.26_spmd} | conditional | bytes 9830544 | solution.py:266
  332.0 16.6 %collective-permute-done.13 = bf16[256,1600]{0,1:T(8,128)(2,1)} collective-permute-done((bf16[256,1600]{0,1:T(8,128)(2,1)}, bf16[256,1600]{0,1:T(8,128)(2,1)}, u32[]{:S(2)}, u32[]{:S(2)}) %collective-permute-start.13) | collective-permute-done | bytes 819232 | tf_op jit(solution)/shard_map/cond/branch_1_fun/ppermute | solution.py:199
  352.9 25.5 %conditional.21 = (f32[256,1600]{0,1:T(8,128)}) conditional(s32[]{:T(128)} %bitcast.29, () %tuple.271, bf16[1024,1600]{0,1:T(8,128)(2,1)} %add_convert_fusion.9), branch_computations={%region_12.13_spmd, %region_13.14_spmd} | conditional | flops 3686400 | bytes 32768156 | solution.py:266
  358.6 18.4 %collective-permute-done.30 = bf16[256,1600]{0,1:T(8,128)(2,1)S(1)} collective-permute-done((bf16[256,1600]{0,1:T(8,128)(2,1)S(1)}, bf16[256,1600]{0,1:T(8,128)(2,1)S(1)}, u32[]{:S(2)}, u32[]{:S(2)}) %collective-permute-start.30) | collective-permute-done | bytes 819232 | tf_op jit(solution)/shard_map/cond/branch_1_fun/ppermute | solution.py:199
  382.5 23.2 %conditional.22 = (bf16[256,1600]{0,1:T(8,128)(2,1)}, bf16[256,1600]{0,1:T(8,128)(2,1)}, bf16[256,1600]{0,1:T(8,128)(2,1)}) conditional(s32[]{:T(128)} %bitcast.29, () %tuple.272, bf16[256,1600]{0,1:T(8,128)(2,1)S(1)} %fusion.64), branch_computations={%region_16.17_spmd, %region_17.18_spmd} | conditional | bytes 9830544 | solution.py:266
  385.0 16.2 %collective-permute-done.7 = bf16[256,1600]{0,1:T(8,128)(2,1)} collective-permute-done((bf16[256,1600]{0,1:T(8,128)(2,1)S(1)}, bf16[256,1600]{0,1:T(8,128)(2,1)}, u32[]{:S(2)}, u32[]{:S(2)}) %collective-permute-start.7) | collective-permute-done | bytes 819232 | tf_op jit(solution)/shard_map/cond/branch_1_fun/ppermute | solution.py:199
  427.3 6.4 add_convert_fusion.10.qkv
  433.8 15.6 %shard_map.256 = (bf16[1024,512]{1,0:T(8,128)(2,1)S(1)}, f32[8,1024]{1,0:T(8,128)S(1)}) custom-call(s32[8]{0:T(128)S(1)} %select_reduce_fusion.place, bf16[1024,1536]{1,0:T(8,128)(2,1)S(1)} %add_convert_fusion.10.qkv), custom_call_target="tpu_custom_call" | custom-call | tf_op jit(solution)/shard_map/pallas_call | solution.py:86
  451.2 14.6 %conditional.23 = (bf16[1,256,512]{2,1,0:T(8,128)(2,1)}, bf16[1,256,512]{2,1,0:T(8,128)(2,1)}, bf16[1,256,512]{2,1,0:T(8,128)(2,1)}) conditional(s32[]{:T(128)} %bitcast.29, () %tuple.275, bf16[1024,512]{1,0:T(8,128)(2,1)S(1)} %get-tuple-element.439), branch_computations={%region_18.19_spmd, %region_19.20_spmd} | conditional | bytes 4718736 | solution.py:266
  453.5 6.8 collective-permute-done.27
  479.9 23.5 %conditional.24 = (bf16[256,1600]{0,1:T(8,128)(2,1)}, bf16[256,1600]{0,1:T(8,128)(2,1)}, bf16[256,1600]{0,1:T(8,128)(2,1)}) conditional(s32[]{:T(128)} %bitcast.29, () %tuple.276, bf16[256,1600]{0,1:T(8,128)(2,1)S(1)} %add_convert_fusion.16), branch_computations={%region_22.23_spmd, %region_23.24_spmd} | conditional | bytes 9830544 | solution.py:266
  482.3 17.5 %collective-permute-done.10 = bf16[256,1600]{0,1:T(8,128)(2,1)} collective-permute-done((bf16[256,1600]{0,1:T(8,128)(2,1)S(1)}, bf16[256,1600]{0,1:T(8,128)(2,1)}, u32[]{:S(2)}, u32[]{:S(2)}) %collective-permute-start.10) | collective-permute-done | bytes 819232 | tf_op jit(solution)/shard_map/cond/branch_1_fun/ppermute | solution.py:199
  508.5 8.4 fusion.41
  571.8 24.7 %conditional.26 = (f32[256,1600]{0,1:T(8,128)}, f32[1,4,400]{2,1,0:T(4,128)S(1)}) conditional(s32[]{:T(128)} %bitcast.29, () %tuple.283, bf16[1024,1600]{0,1:T(8,128)(2,1)S(1)} %add_convert_fusion.8), branch_computations={%region_27.28_spmd, %region_28.30_spmd} | conditional | flops 4094400 | bytes 19680136 | solution.py:266
  576.1 18.4 %collective-permute-done.36 = bf16[256,1600]{0,1:T(8,128)(2,1)S(1)} collective-permute-done((bf16[256,1600]{0,1:T(8,128)(2,1)S(1)}, bf16[256,1600]{0,1:T(8,128)(2,1)S(1)}, u32[]{:S(2)}, u32[]{:S(2)}) %collective-permute-start.36) | collective-permute-done | bytes 819232 | tf_op jit(solution)/shard_map/cond/branch_1_fun/ppermute | solution.py:199
  611.1 16.4 %conditional.27 = (bf16[256,512]{1,0:T(8,128)(2,1)}, bf16[256,512]{1,0:T(8,128)(2,1)}, bf16[256,512]{1,0:T(8,128)(2,1)}, bf16[4,112,1600]{2,1,0:T(8,128)(2,1)}, ...) conditional(s32[]{:T(128)} %bitcast.29, () %tuple.282, ...), branch_computations={%region_32.33_spmd, %region_33.34_spmd} | conditional | flops 1313280000 | bytes 22946264 | solution.py:266
  636.0 8.5 add_convert_fusion.13
  644.5 7.6 conditional.28
  654.6 21.3 %shard_map.258 = bf16[1024,1536]{1,0:T(8,128)(2,1)} custom-call(s32[8]{0:T(128)S(1)} %select_reduce_fusion.place, bf16[1024,1536]{1,0:T(8,128)(2,1)S(1)} %add_convert_fusion.10.qkv, bf16[1024,512]{1,0:T(8,128)(2,1)S(1)} %copy-done.3, f32[8,1024]{1,0:T(8,128)S(1)} %get-tuple-element.483.log_total), custom_call_target="tpu_custom_call" | custom-call | tf_op jit(solution)/shard_map/pallas_call | solution.py:167
  675.9 11.8 collective-permute-done.74
  693.1 9.1 convolution_convert_fusion.6
  702.2 25.4 %conditional.29 = (f32[256,1600]{0,1:T(8,128)S(1)}, bf16[4,2,200,1536]{3,2,1,0:T(8,128)(2,1)}) conditional(s32[]{:T(128)} %bitcast.29, () %tuple.293, (bf16[1024,1600]{0,1:T(8,128)(2,1)}, bf16[1024,1600]{0,1:T(8,128)(2,1)}, bf16[1024,1536]{1,0:T(8,128)(2,1)S(1)}) %tuple.531), branch_computations={%region_38.39_spmd, %region_39.40_spmd} | conditional | flops 5039308800 | bytes 44105892 | solution.py:266
  708.7 8.9 convolution_convert_fusion.1
  717.5 9.8 collective-permute-done.48
  737.3 23.4 %conditional.30 = (bf16[256,1600]{0,1:T(8,128)(2,1)}, bf16[256,1600]{0,1:T(8,128)(2,1)}, bf16[256,1600]{0,1:T(8,128)(2,1)}) conditional(s32[]{:T(128)} %bitcast.29, () %tuple.298, bf16[256,1600]{0,1:T(8,128)(2,1)S(1)} %get-tuple-element.503), branch_computations={%region_42.43_spmd, %region_43.44_spmd} | conditional | bytes 9830544 | solution.py:266
  739.7 16.4 %collective-permute-done.16 = bf16[256,1600]{0,1:T(8,128)(2,1)} collective-permute-done((bf16[256,1600]{0,1:T(8,128)(2,1)S(1)}, bf16[256,1600]{0,1:T(8,128)(2,1)}, u32[]{:S(2)}, u32[]{:S(2)}) %collective-permute-start.16) | collective-permute-done | bytes 819232 | tf_op jit(solution)/shard_map/cond/branch_1_fun/ppermute | solution.py:199
  760.7 6.8 convolution_convert_fusion.10
  777.9 7.6 multiply_convert_fusion
  810.4 33.9 %conditional.31 = (f32[256,1600]{0,1:T(8,128)S(1)}, f32[800,1600]{1,0:T(8,128)}) conditional(s32[]{:T(128)} %bitcast.29, () %tuple.303, (bf16[1024,1600]{0,1:T(8,128)(2,1)S(1)}, bf16[256,1600]{0,1:T(8,128)(2,1)S(1)}, bf16[256,1600]{0,1:T(8,128)(2,1)}, bf16[256,1600]{0,1:T(8,128)(2,1)}, bf16[256,1600]{0,1:T(8,128)(2,1)}, ...), branch_computations={%region_45.46_spmd, %region_46.47_spmd} | conditional | flops 2640793600 | bytes 49356964 | solution.py:266
  824.2 7.5 convert_bitcast_fusion
  831.7 10.9 collective-permute-done.42
  844.3 9.4 collective-permute-done.77
  859.4 7.2 convolution_convert_fusion.9
  875.6 17.1 %conditional.32 = (bf16[256,512]{1,0:T(8,128)(2,1)}, bf16[256,512]{1,0:T(8,128)(2,1)}, bf16[256,512]{1,0:T(8,128)(2,1)}, bf16[4,112,1600]{2,1,0:T(8,128)(2,1)}, ...) conditional(s32[]{:T(128)} %bitcast.29, () %tuple.309, ...), branch_computations={%region_50.51_spmd, %region_51.52_spmd} | conditional | flops 1313280000 | bytes 22946264 | solution.py:266
  892.7 7.5 conditional.33
  910.2 21.1 %shard_map.259 = bf16[1024,1536]{1,0:T(8,128)(2,1)S(1)} custom-call(s32[8]{0:T(128)S(1)} %select_reduce_fusion.place, bf16[1024,1536]{1,0:T(8,128)(2,1)} %copy-done.2, bf16[1024,512]{1,0:T(8,128)(2,1)S(1)} %copy-done.4, f32[8,1024]{1,0:T(8,128)S(1)} %get-tuple-element.533.log_total), custom_call_target="tpu_custom_call" | custom-call | tf_op jit(solution)/shard_map/pallas_call | solution.py:167
  931.2 8.2 collective-permute-done.79
  948.8 8.5 add_convert_fusion.12
  957.8 7.4 convolution_convert_fusion.4
  970.9 8.0 convolution_convert_fusion.5
  982.8 48.0 %conditional.34 = (f32[256,1600]{0,1:T(8,128)}, f32[1,4,400]{2,1,0:T(4,128)S(1)}) conditional(s32[]{:T(128)} %bitcast.29, () %tuple.321, bf16[1024,1600]{0,1:T(8,128)(2,1)S(1)} %convolution_convert_fusion.5), branch_computations={%region_55.56_spmd, %region_56.58_spmd} | conditional | flops 4094400 | bytes 19680136 | solution.py:266
  988.0 41.2 %collective-permute-done.39 = bf16[256,1600]{0,1:T(8,128)(2,1)S(1)} collective-permute-done((bf16[256,1600]{0,1:T(8,128)(2,1)S(1)}, bf16[256,1600]{0,1:T(8,128)(2,1)S(1)}, u32[]{:S(2)}, u32[]{:S(2)}) %collective-permute-start.39) | collective-permute-done | bytes 819232 | tf_op jit(solution)/shard_map/cond/branch_1_fun/ppermute | solution.py:199
  1056.9 12.6 %collective-permute-done.82 = bf16[400,800]{1,0:T(8,128)(2,1)S(1)} collective-permute-done((bf16[400,800]{1,0:T(8,128)(2,1)S(1)}, bf16[400,800]{1,0:T(8,128)(2,1)S(1)}, u32[]{:S(2)}, u32[]{:S(2)}) %collective-permute-start.82) | collective-permute-done | bytes 640032 | tf_op jit(solution)/shard_map/ppermute | solution.py:199
  1070.4 25.9 %conditional.35 = (f32[256,1600]{0,1:T(8,128)}) conditional(s32[]{:T(128)} %bitcast.29, () %tuple.327, bf16[1024,1600]{0,1:T(8,128)(2,1)} %add_convert_fusion.6), branch_computations={%region_60.61_spmd, %region_61.62_spmd} | conditional | flops 3686400 | bytes 32768156 | solution.py:266
  1076.0 18.6 %collective-permute-done.33 = bf16[256,1600]{0,1:T(8,128)(2,1)S(1)} collective-permute-done((bf16[256,1600]{0,1:T(8,128)(2,1)S(1)}, bf16[256,1600]{0,1:T(8,128)(2,1)S(1)}, u32[]{:S(2)}, u32[]{:S(2)}) %collective-permute-start.33) | collective-permute-done | bytes 819232 | tf_op jit(solution)/shard_map/cond/branch_1_fun/ppermute | solution.py:199
  1117.2 17.8 %reduce-scatter.23.cloned.1.call-done = bf16[112,1600]{1,0:T(8,128)(2,1)} async-done(((bf16[448,1600]{1,0:T(8,128)(2,1)}), bf16[112,1600]{1,0:T(8,128)(2,1)}) %reduce-scatter.23.cloned.1.call-update) | async-done | bytes 358416 | tf_op jit(solution)/shard_map/reduce_scatter | solution.py:290
  1142.0 6.9 collective-permute-done.94
  1151.5 19.1 %collective-permute-done.99.refs_2_ = bf16[400,800]{1,0:T(8,128)(2,1)S(1)} collective-permute-done((bf16[400,800]{1,0:T(8,128)(2,1)S(1)}, bf16[400,800]{1,0:T(8,128)(2,1)S(1)}, u32[]{:S(2)}, u32[]{:S(2)}) %collective-permute-start.99) | collective-permute-done | bytes 640032 | tf_op jit(solution)/shard_map/ppermute | solution.py:199
  1186.4 6.6 shard_map.262
  (859 shorter events, 595.4 us)
Async XLA Ops:
  7.2 88.5 %all-gather.10.cloned.1.call-start = ((), (), s32[]{:S(2)}) async-start(), calls=%async_computation.8 | async-start | bytes 3072000 | tf_op jit(solution)/shard_map/all_gather | solution.py:286
  32.3 90.5 %all-gather.12.cloned.1.call-start = ((), (), s32[]{:S(2)}) async-start(), calls=%async_computation.9 | async-start | bytes 1863680 | tf_op jit(solution)/shard_map/all_gather | solution.py:286
  33.3 29.2 %collective-permute-start.53 = (bf16[256,1600]{0,1:T(8,128)(2,1)}, bf16[256,1600]{0,1:T(8,128)(2,1)}, u32[]{:S(2)}, u32[]{:S(2)}) collective-permute-start(bf16[256,1600]{0,1:T(8,128)(2,1)} %dynamic-slice_bitcast_fusion), channel_id=1, source_target_pairs={{0,16},{16,0},{1,17},{17,1},{2,18},{18,2},{3,19},{19,3},{4,20},{20... | collective-permute-start | bytes 2457608 | tf_op jit(solution)/shard_map/ppermute | solution.py:199
  37.1 23.2 %collective-permute-start.55 = (bf16[112,1600]{1,0:T(8,128)(2,1)}, bf16[112,1600]{1,0:T(8,128)(2,1)}, u32[]{:S(2)}, u32[]{:S(2)}) collective-permute-start(bf16[112,1600]{1,0:T(8,128)(2,1)} %dynamic-slice_bitcast_fusion.3), channel_id=1, source_target_pairs={{0,16},{16,0},{1,17},{17,1},{2,18},{18,2},{3,19},{19,3},{4,20},{20... | collective-permute-start | bytes 1075208 | tf_op jit(solution)/shard_map/ppermute | solution.py:199
  62.5 126.7 %all-gather.14.cloned.1.call-start = ((), (), s32[]{:S(2)}) async-start(), calls=%async_computation.10 | async-start | bytes 3584000 | tf_op jit(solution)/shard_map/all_gather | solution.py:286
  76.7 179.1 %all-gather.16.cloned.1.call-start = ((), (), s32[]{:S(2)}) async-start(), calls=%async_computation.11 | async-start | bytes 3328000 | tf_op jit(solution)/shard_map/all_gather | solution.py:286
  95.0 179.4 %all-gather.18.cloned.1.call-start = ((), (), s32[]{:S(2)}) async-start(), calls=%async_computation.12 | async-start | bytes 1863680 | tf_op jit(solution)/shard_map/all_gather | solution.py:286
  95.6 232.0 %all-gather.20.cloned.1.call-start = ((), (), s32[]{:S(2)}) async-start(), calls=%async_computation.13 | async-start | bytes 3072000 | tf_op jit(solution)/shard_map/all_gather | solution.py:286
  95.7 62.4 %collective-permute-start.61 = (bf16[800,1536]{1,0:T(8,128)(2,1)}, bf16[800,1536]{1,0:T(8,128)(2,1)}, u32[]{:S(2)}, u32[]{:S(2)}) collective-permute-start(bf16[800,1536]{1,0:T(8,128)(2,1)} %all-gather.10.cloned.1.call-done), channel_id=1, source_target_pairs={{0,16},{16,0},{1,17},{17,1},{2,18},{18,2},{3,19},{19,3},{4,20},{20... | collective-permute-start | bytes 7372808 | tf_op jit(solution)/shard_map/ppermute | solution.py:199
  100.0 19.6 %collective-permute-start = (bf16[256,1600]{0,1:T(8,128)(2,1)S(1)}, bf16[256,1600]{0,1:T(8,128)(2,1)}, u32[]{:S(2)}, u32[]{:S(2)}) collective-permute-start(bf16[256,1600]{0,1:T(8,128)(2,1)S(1)} %param.1), channel_id=1, source_target_pairs={{0,4},{4,0},{8,12},{12,8},{1,5},{5,1},{9,13},{13,9},{2,6},{6,2},{1... | collective-permute-start | bytes 2457608 | tf_op jit(solution)/shard_map/cond/branch_1_fun/ppermute | solution.py:199
  122.8 33.0 %collective-permute-start.63 = (bf16[448,1600]{1,0:T(8,128)(2,1)}, bf16[448,1600]{1,0:T(8,128)(2,1)S(1)}, u32[]{:S(2)}, u32[]{:S(2)}) collective-permute-start(bf16[448,1600]{1,0:T(8,128)(2,1)} %all-gather.12.cloned.1.call-done.refs_0_), channel_id=1, source_target_pairs={{0,8},{4,12},{8,0},{12,4},{1,9},{5,13},{9,1},{13,5},{2,10},{6,14},... | collective-permute-start | bytes 4300808 | tf_op jit(solution)/shard_map/ppermute | solution.py:199
  124.3 61.1 %collective-permute-start.65 = (bf16[200,1600]{1,0:T(8,128)(2,1)}, bf16[200,1600]{1,0:T(8,128)(2,1)}, u32[]{:S(2)}, u32[]{:S(2)}) collective-permute-start(bf16[200,1600]{1,0:T(8,128)(2,1)} %get-tuple-element.383), channel_id=1, source_target_pairs={{0,16},{16,0},{1,17},{17,1},{2,18},{18,2},{3,19},{19,3},{4,20},{20... | collective-permute-start | bytes 1920008 | tf_op jit(solution)/shard_map/ppermute | solution.py:199
  125.6 286.3 %all-gather.22.cloned.1.call-start = ((), (), s32[]{:S(2)}) async-start(), calls=%async_computation.14 | async-start | bytes 3584000 | tf_op jit(solution)/shard_map/all_gather | solution.py:286
  125.8 62.3 %collective-permute-start.62 = (bf16[448,1600]{1,0:T(8,128)(2,1)}, bf16[448,1600]{1,0:T(8,128)(2,1)S(1)}, u32[]{:S(2)}, u32[]{:S(2)}) collective-permute-start(bf16[448,1600]{1,0:T(8,128)(2,1)} %all-gather.12.cloned.1.call-done.refs_0_), channel_id=1, source_target_pairs={{0,4},{4,0},{8,12},{12,8},{1,5},{5,1},{9,13},{13,9},{2,6},{6,2},{1... | collective-permute-start | bytes 4300808 | tf_op jit(solution)/shard_map/ppermute | solution.py:199
  155.9 33.4 %collective-permute-start.64 = (bf16[448,1600]{1,0:T(8,128)(2,1)S(1)}, bf16[448,1600]{1,0:T(8,128)(2,1)}, u32[]{:S(2)}, u32[]{:S(2)}) collective-permute-start(bf16[448,1600]{1,0:T(8,128)(2,1)S(1)} %collective-permute-done.63.refs_2_), channel_id=1, source_target_pairs={{0,4},{4,0},{8,12},{12,8},{1,5},{5,1},{9,13},{13,9},{2,6},{6,2},{1... | collective-permute-start | bytes 4300808 | tf_op jit(solution)/shard_map/ppermute | solution.py:199
  194.4 61.5 %collective-permute-start.66 = (bf16[1600,800]{0,1:T(8,128)(2,1)}, bf16[1600,800]{0,1:T(8,128)(2,1)}, u32[]{:S(2)}, u32[]{:S(2)}) collective-permute-start(bf16[1600,800]{0,1:T(8,128)(2,1)} %copy.211), channel_id=1, source_target_pairs={{0,16},{16,0},{1,17},{17,1},{2,18},{18,2},{3,19},{19,3},{4,20},{20... | collective-permute-start | bytes 7680008 | tf_op jit(solution)/shard_map/ppermute | solution.py:199
  232.8 19.2 %collective-permute-start.4 = (bf16[256,1600]{0,1:T(8,128)(2,1)S(1)}, bf16[256,1600]{0,1:T(8,128)(2,1)}, u32[]{:S(2)}, u32[]{:S(2)}) collective-permute-start(bf16[256,1600]{0,1:T(8,128)(2,1)S(1)} %param.5), channel_id=1, source_target_pairs={{0,8},{4,12},{8,0},{12,4},{1,9},{5,13},{9,1},{13,5},{2,10},{6,14},... | collective-permute-start | bytes 2457608 | tf_op jit(solution)/shard_map/cond/branch_1_fun/ppermute | solution.py:199
  234.0 19.6 %collective-permute-start.3 = (bf16[256,1600]{0,1:T(8,128)(2,1)S(1)}, bf16[256,1600]{0,1:T(8,128)(2,1)}, u32[]{:S(2)}, u32[]{:S(2)}) collective-permute-start(bf16[256,1600]{0,1:T(8,128)(2,1)S(1)} %param.5), channel_id=1, source_target_pairs={{0,4},{4,0},{8,12},{12,8},{1,5},{5,1},{9,13},{13,9},{2,6},{6,2},{1... | collective-permute-start | bytes 2457608 | tf_op jit(solution)/shard_map/cond/branch_1_fun/ppermute | solution.py:199
  255.9 59.8 %collective-permute-start.67 = (bf16[800,1600]{1,0:T(8,128)(2,1)}, bf16[800,1600]{1,0:T(8,128)(2,1)}, u32[]{:S(2)}, u32[]{:S(2)}) collective-permute-start(bf16[800,1600]{1,0:T(8,128)(2,1)} %all-gather.16.cloned.1.call-done), channel_id=1, source_target_pairs={{0,16},{16,0},{1,17},{17,1},{2,18},{18,2},{3,19},{19,3},{4,20},{20... | collective-permute-start | bytes 7680008 | tf_op jit(solution)/shard_map/ppermute | solution.py:199
  274.4 33.0 %collective-permute-start.69 = (bf16[448,1600]{1,0:T(8,128)(2,1)}, bf16[448,1600]{1,0:T(8,128)(2,1)S(1)}, u32[]{:S(2)}, u32[]{:S(2)}) collective-permute-start(bf16[448,1600]{1,0:T(8,128)(2,1)} %all-gather.18.cloned.1.call-done.refs_0_), channel_id=1, source_target_pairs={{0,8},{4,12},{8,0},{12,4},{1,9},{5,13},{9,1},{13,5},{2,10},{6,14},... | collective-permute-start | bytes 4300808 | tf_op jit(solution)/shard_map/ppermute | solution.py:199
  275.6 262.8 %all-gather.24.cloned.1.call-start = ((), (), s32[]{:S(2)}) async-start(), calls=%async_computation.22 | async-start | bytes 6656000 | tf_op jit(solution)/shard_map/all_gather | solution.py:286
  276.1 46.4 %collective-permute-start.68 = (bf16[448,1600]{1,0:T(8,128)(2,1)}, bf16[448,1600]{1,0:T(8,128)(2,1)S(1)}, u32[]{:S(2)}, u32[]{:S(2)}) collective-permute-start(bf16[448,1600]{1,0:T(8,128)(2,1)} %all-gather.18.cloned.1.call-done.refs_0_), channel_id=1, source_target_pairs={{0,4},{4,0},{8,12},{12,8},{1,5},{5,1},{9,13},{13,9},{2,6},{6,2},{1... | collective-permute-start | bytes 4300808 | tf_op jit(solution)/shard_map/ppermute | solution.py:199
  327.6 84.2 %collective-permute-start.71 = (bf16[800,1536]{1,0:T(8,128)(2,1)}, bf16[800,1536]{1,0:T(8,128)(2,1)}, u32[]{:S(2)}, u32[]{:S(2)}) collective-permute-start(bf16[800,1536]{1,0:T(8,128)(2,1)} %all-gather.20.cloned.1.call-done), channel_id=1, source_target_pairs={{0,16},{16,0},{1,17},{17,1},{2,18},{18,2},{3,19},{19,3},{4,20},{20... | collective-permute-start | bytes 7372808 | tf_op jit(solution)/shard_map/ppermute | solution.py:199
  330.8 19.8 %collective-permute-start.12 = (bf16[256,1600]{0,1:T(8,128)(2,1)}, bf16[256,1600]{0,1:T(8,128)(2,1)}, u32[]{:S(2)}, u32[]{:S(2)}) collective-permute-start(bf16[256,1600]{0,1:T(8,128)(2,1)} %param.15), channel_id=1, source_target_pairs={{0,4},{4,0},{8,12},{12,8},{1,5},{5,1},{9,13},{13,9},{2,6},{6,2},{1... | collective-permute-start | bytes 2457608 | tf_op jit(solution)/shard_map/cond/branch_1_fun/ppermute | solution.py:199
  352.9 336.3 %reduce-scatter.11.cloned.1.call-start = ((), (), s32[]{:S(2)}) async-start(), calls=%async_computation.15 | async-start | bytes 6656000 | tf_op jit(solution)/shard_map/reduce_scatter | solution.py:290
  357.3 19.6 %collective-permute-start.30 = (bf16[256,1600]{0,1:T(8,128)(2,1)S(1)}, bf16[256,1600]{0,1:T(8,128)(2,1)S(1)}, u32[]{:S(2)}, u32[]{:S(2)}) collective-permute-start(bf16[256,1600]{0,1:T(8,128)(2,1)S(1)} %add_convert_fusion), channel_id=1, source_target_pairs={{0,8},{4,12},{8,0},{12,4},{1,9},{5,13},{9,1},{13,5},{2,10},{6,14},... | collective-permute-start | bytes 2457608 | tf_op jit(solution)/shard_map/cond/branch_1_fun/ppermute | solution.py:199
  383.7 19.6 %collective-permute-start.6 = (bf16[256,1600]{0,1:T(8,128)(2,1)S(1)}, bf16[256,1600]{0,1:T(8,128)(2,1)}, u32[]{:S(2)}, u32[]{:S(2)}) collective-permute-start(bf16[256,1600]{0,1:T(8,128)(2,1)S(1)} %param.9), channel_id=1, source_target_pairs={{0,4},{4,0},{8,12},{12,8},{1,5},{5,1},{9,13},{13,9},{2,6},{6,2},{1... | collective-permute-start | bytes 2457608 | tf_op jit(solution)/shard_map/cond/branch_1_fun/ppermute | solution.py:199
  419.2 84.2 %collective-permute-start.72 = (bf16[1600,800]{0,1:T(8,128)(2,1)}, bf16[1600,800]{0,1:T(8,128)(2,1)}, u32[]{:S(2)}, u32[]{:S(2)}) collective-permute-start(bf16[1600,800]{0,1:T(8,128)(2,1)} %copy.212), channel_id=1, source_target_pairs={{0,16},{16,0},{1,17},{17,1},{2,18},{18,2},{3,19},{19,3},{4,20},{20... | collective-permute-start | bytes 7680008 | tf_op jit(solution)/shard_map/ppermute | solution.py:199
  480.3 19.5 %collective-permute-start.10 = (bf16[256,1600]{0,1:T(8,128)(2,1)S(1)}, bf16[256,1600]{0,1:T(8,128)(2,1)}, u32[]{:S(2)}, u32[]{:S(2)}) collective-permute-start(bf16[256,1600]{0,1:T(8,128)(2,1)S(1)} %param.13), channel_id=1, source_target_pairs={{0,8},{4,12},{8,0},{12,4},{1,9},{5,13},{9,1},{13,5},{2,10},{6,14},... | collective-permute-start | bytes 2457608 | tf_op jit(solution)/shard_map/cond/branch_1_fun/ppermute | solution.py:199
  481.6 19.6 %collective-permute-start.9 = (bf16[256,1600]{0,1:T(8,128)(2,1)S(1)}, bf16[256,1600]{0,1:T(8,128)(2,1)}, u32[]{:S(2)}, u32[]{:S(2)}) collective-permute-start(bf16[256,1600]{0,1:T(8,128)(2,1)S(1)} %param.13), channel_id=1, source_target_pairs={{0,4},{4,0},{8,12},{12,8},{1,5},{5,1},{9,13},{13,9},{2,6},{6,2},{1... | collective-permute-start | bytes 2457608 | tf_op jit(solution)/shard_map/cond/branch_1_fun/ppermute | solution.py:199
  536.0 231.5 %reduce-scatter.13.cloned.1.call-start = ((), (), s32[]{:S(2)}) async-start(), calls=%async_computation.16 | async-start | bytes 3584000 | tf_op jit(solution)/shard_map/reduce_scatter | solution.py:290
  561.2 69.6 %collective-permute-start.73 = (bf16[1600,800]{0,1:T(8,128)(2,1)}, bf16[1600,800]{0,1:T(8,128)(2,1)}, u32[]{:S(2)}, u32[]{:S(2)}) collective-permute-start(bf16[1600,800]{0,1:T(8,128)(2,1)} %convolution_convert_fusion.11), channel_id=1, source_target_pairs={{0,16},{16,0},{1,17},{17,1},{2,18},{18,2},{3,19},{19,3},{4,20},{20... | collective-permute-start | bytes 7680008 | tf_op jit(solution)/shard_map/ppermute | solution.py:199
  574.9 19.6 %collective-permute-start.36 = (bf16[256,1600]{0,1:T(8,128)(2,1)S(1)}, bf16[256,1600]{0,1:T(8,128)(2,1)S(1)}, u32[]{:S(2)}, u32[]{:S(2)}) collective-permute-start(bf16[256,1600]{0,1:T(8,128)(2,1)S(1)} %add_convert_fusion.1), channel_id=1, source_target_pairs={{0,8},{4,12},{8,0},{12,4},{1,9},{5,13},{9,1},{13,5},{2,10},{6,14},... | collective-permute-start | bytes 2457608 | tf_op jit(solution)/shard_map/cond/branch_1_fun/ppermute | solution.py:199
  644.5 222.1 %reduce-scatter.15.cloned.1.call-start = ((), (), s32[]{:S(2)}) async-start(), calls=%async_computation.17 | async-start | bytes 1863680 | tf_op jit(solution)/shard_map/reduce_scatter | solution.py:290
  653.8 34.0 %collective-permute-start.74 = (bf16[4,112,1600]{2,1,0:T(8,128)(2,1)S(1)}, bf16[4,112,1600]{2,1,0:T(8,128)(2,1)S(1)}, u32[]{:S(2)}, u32[]{:S(2)}) collective-permute-start(bf16[4,112,1600]{2,1,0:T(8,128)(2,1)S(1)} %convert_element_type.475), channel_id=1, source_target_pairs={{0,8},{4,12},{8,0},{12,4},{1,9},{5,13},{9,1},{13,5},{2,10},{6,14},... | collective-permute-start | bytes 4300808 | tf_op jit(solution)/shard_map/ppermute | solution.py:199
  689.1 43.7 %collective-permute-start.75 = (bf16[400,1600]{1,0:T(8,128)(2,1)}, bf16[400,1600]{1,0:T(8,128)(2,1)}, u32[]{:S(2)}, u32[]{:S(2)}) collective-permute-start(bf16[400,1600]{1,0:T(8,128)(2,1)} %reduce-scatter.11.cloned.1.call-done), channel_id=1, source_target_pairs={{0,16},{1,17},{2,18},{3,19},{4,20},{5,21},{6,22},{7,23},{8,24},{9,... | collective-permute-start | bytes 3840008 | tf_op jit(solution)/shard_map/ppermute | solution.py:828
  707.8 19.5 %collective-permute-start.48 = (bf16[256,1600]{0,1:T(8,128)(2,1)S(1)}, bf16[256,1600]{0,1:T(8,128)(2,1)S(1)}, u32[]{:S(2)}, u32[]{:S(2)}) collective-permute-start(bf16[256,1600]{0,1:T(8,128)(2,1)S(1)} %add_convert_fusion.2), channel_id=1, source_target_pairs={{0,8},{4,12},{8,0},{12,4},{1,9},{5,13},{9,1},{13,5},{2,10},{6,14},... | collective-permute-start | bytes 2457608 | tf_op jit(solution)/shard_map/cond/branch_1_fun/ppermute | solution.py:199
  727.7 214.6 %reduce-scatter.17.cloned.1.call-start = ((), (), s32[]{:S(2)}) async-start(), calls=%async_computation.18 | async-start | bytes 3072000 | tf_op jit(solution)/shard_map/reduce_scatter | solution.py:290
  733.9 54.0 %collective-permute-start.76 = (bf16[800,1536]{1,0:T(8,128)(2,1)}, bf16[800,1536]{1,0:T(8,128)(2,1)}, u32[]{:S(2)}, u32[]{:S(2)}) collective-permute-start(bf16[800,1536]{1,0:T(8,128)(2,1)} %bitcast.66), channel_id=1, source_target_pairs={{0,16},{16,0},{1,17},{17,1},{2,18},{18,2},{3,19},{19,3},{4,20},{20... | collective-permute-start | bytes 7372808 | tf_op jit(solution)/shard_map/ppermute | solution.py:199
  738.4 19.8 %collective-permute-start.15 = (bf16[256,1600]{0,1:T(8,128)(2,1)S(1)}, bf16[256,1600]{0,1:T(8,128)(2,1)}, u32[]{:S(2)}, u32[]{:S(2)}) collective-permute-start(bf16[256,1600]{0,1:T(8,128)(2,1)S(1)} %param.25), channel_id=1, source_target_pairs={{0,4},{4,0},{8,12},{12,8},{1,5},{5,1},{9,13},{13,9},{2,6},{6,2},{1... | collective-permute-start | bytes 2457608 | tf_op jit(solution)/shard_map/cond/branch_1_fun/ppermute | solution.py:199
  791.9 150.4 %reduce-scatter.25.cloned.1.call-start = ((), (), s32[]{:S(2)}) async-start(), calls=%async_computation.23 | async-start | bytes 3328000
  796.3 57.5 %collective-permute-start.77 = (bf16[800,1600]{1,0:T(8,128)(2,1)}, bf16[800,1600]{1,0:T(8,128)(2,1)}, u32[]{:S(2)}, u32[]{:S(2)}) collective-permute-start(bf16[800,1600]{1,0:T(8,128)(2,1)} %convolution_convert_fusion.10), channel_id=1, source_target_pairs={{0,16},{16,0},{1,17},{17,1},{2,18},{18,2},{3,19},{19,3},{4,20},{20... | collective-permute-start | bytes 7680008 | tf_op jit(solution)/shard_map/ppermute | solution.py:199
  823.2 19.5 %collective-permute-start.42 = (bf16[256,1600]{0,1:T(8,128)(2,1)S(1)}, bf16[256,1600]{0,1:T(8,128)(2,1)S(1)}, u32[]{:S(2)}, u32[]{:S(2)}) collective-permute-start(bf16[256,1600]{0,1:T(8,128)(2,1)S(1)} %add_convert_fusion.3), channel_id=1, source_target_pairs={{0,8},{4,12},{8,0},{12,4},{1,9},{5,13},{9,1},{13,5},{2,10},{6,14},... | collective-permute-start | bytes 2457608 | tf_op jit(solution)/shard_map/cond/branch_1_fun/ppermute | solution.py:199
  859.1 181.8 %reduce-scatter.19.cloned.1.call-start = ((), (), s32[]{:S(2)}) async-start(), calls=%async_computation.19 | async-start | bytes 3584000 | tf_op jit(solution)/shard_map/reduce_scatter | solution.py:290
  866.6 75.7 %collective-permute-start.78 = (bf16[1600,800]{0,1:T(8,128)(2,1)}, bf16[1600,800]{0,1:T(8,128)(2,1)}, u32[]{:S(2)}, u32[]{:S(2)}) collective-permute-start(bf16[1600,800]{0,1:T(8,128)(2,1)} %convolution_convert_fusion.9), channel_id=1, source_target_pairs={{0,16},{16,0},{1,17},{17,1},{2,18},{18,2},{3,19},{19,3},{4,20},{20... | collective-permute-start | bytes 7680008 | tf_op jit(solution)/shard_map/ppermute | solution.py:199
  905.0 34.4 %collective-permute-start.79 = (bf16[4,112,1600]{2,1,0:T(8,128)(2,1)}, bf16[4,112,1600]{2,1,0:T(8,128)(2,1)}, u32[]{:S(2)}, u32[]{:S(2)}) collective-permute-start(bf16[4,112,1600]{2,1,0:T(8,128)(2,1)} %convert_element_type.498), channel_id=1, source_target_pairs={{0,8},{4,12},{8,0},{12,4},{1,9},{5,13},{9,1},{13,5},{2,10},{6,14},... | collective-permute-start | bytes 4300808 | tf_op jit(solution)/shard_map/ppermute | solution.py:199
  942.3 28.6 %collective-permute-start.81 = (bf16[200,1600]{1,0:T(8,128)(2,1)}, bf16[200,1600]{1,0:T(8,128)(2,1)}, u32[]{:S(2)}, u32[]{:S(2)}) collective-permute-start(bf16[200,1600]{1,0:T(8,128)(2,1)} %reduce-scatter.25.cloned.1.call-done), channel_id=1, source_target_pairs={{16,0},{17,1},{18,2},{19,3},{20,4},{21,5},{22,6},{23,7},{24,8},{25... | collective-permute-start | bytes 1920008 | tf_op jit(solution)/shard_map/ppermute | solution.py:828
  957.3 142.1 %reduce-scatter.21.cloned.1.call-start = ((), (), s32[]{:S(2)}) async-start(), calls=%async_computation.20 | async-start | bytes 3072000 | tf_op jit(solution)/shard_map/reduce_scatter | solution.py:290
  968.0 68.9 %collective-permute-start.80 = (bf16[800,1536]{1,0:T(8,128)(2,1)}, bf16[800,1536]{1,0:T(8,128)(2,1)}, u32[]{:S(2)}, u32[]{:S(2)}) collective-permute-start(bf16[800,1536]{1,0:T(8,128)(2,1)} %bitcast.69), channel_id=1, source_target_pairs={{0,16},{16,0},{1,17},{17,1},{2,18},{18,2},{3,19},{19,3},{4,20},{20... | collective-permute-start | bytes 7372808 | tf_op jit(solution)/shard_map/ppermute | solution.py:199
  982.3 59.5 %collective-permute-start.104 = (bf16[400,1600]{1,0:T(8,128)(2,1)}, bf16[400,1600]{1,0:T(8,128)(2,1)}, u32[]{:S(2)}, u32[]{:S(2)}) collective-permute-start(bf16[400,1600]{1,0:T(8,128)(2,1)} %pad_maximum_fusion.6.refs_0_), channel_id=1, source_target_pairs={{0,8},{4,12},{8,0},{12,4},{1,9},{5,13},{9,1},{13,5},{2,10},{6,14},... | collective-permute-start | bytes 3840008 | tf_op jit(solution)/shard_map/ppermute | solution.py:199
  987.1 42.1 %collective-permute-start.39 = (bf16[256,1600]{0,1:T(8,128)(2,1)S(1)}, bf16[256,1600]{0,1:T(8,128)(2,1)S(1)}, u32[]{:S(2)}, u32[]{:S(2)}) collective-permute-start(bf16[256,1600]{0,1:T(8,128)(2,1)S(1)} %add_convert_fusion.4), channel_id=1, source_target_pairs={{0,8},{4,12},{8,0},{12,4},{1,9},{5,13},{9,1},{13,5},{2,10},{6,14},... | collective-permute-start | bytes 2457608 | tf_op jit(solution)/shard_map/cond/branch_1_fun/ppermute | solution.py:199
  1040.9 94.1 %reduce-scatter.23.cloned.1.call-start = ((), (), s32[]{:S(2)}) async-start(), calls=%async_computation.21 | async-start | bytes 1863680 | tf_op jit(solution)/shard_map/reduce_scatter | solution.py:290
  1045.4 90.8 %collective-permute-start.105 = (bf16[800,1600]{1,0:T(8,128)(2,1)}, bf16[800,1600]{1,0:T(8,128)(2,1)}, u32[]{:S(2)}, u32[]{:S(2)}) collective-permute-start(bf16[800,1600]{1,0:T(8,128)(2,1)} %pad_maximum_fusion.4), channel_id=1, source_target_pairs={{0,4},{4,0},{8,12},{12,8},{1,5},{5,1},{9,13},{13,9},{2,6},{6,2},{1... | collective-permute-start | bytes 7680008 | tf_op jit(solution)/shard_map/ppermute | solution.py:199
  1075.1 19.5 %collective-permute-start.33 = (bf16[256,1600]{0,1:T(8,128)(2,1)S(1)}, bf16[256,1600]{0,1:T(8,128)(2,1)S(1)}, u32[]{:S(2)}, u32[]{:S(2)}) collective-permute-start(bf16[256,1600]{0,1:T(8,128)(2,1)S(1)} %add_convert_fusion.5), channel_id=1, source_target_pairs={{0,8},{4,12},{8,0},{12,4},{1,9},{5,13},{9,1},{13,5},{2,10},{6,14},... | collective-permute-start | bytes 2457608 | tf_op jit(solution)/shard_map/cond/branch_1_fun/ppermute | solution.py:199
  1112.3 26.3 %collective-permute-start.102 = (bf16[400,800]{1,0:T(8,128)(2,1)S(1)}, bf16[400,800]{1,0:T(8,128)(2,1)S(1)}, u32[]{:S(2)}, u32[]{:S(2)}) collective-permute-start(bf16[400,800]{1,0:T(8,128)(2,1)S(1)} %get-tuple-element.800.refs_4_), channel_id=1, source_target_pairs={{0,8},{4,12},{8,0},{12,4},{1,9},{5,13},{9,1},{13,5},{2,10},{6,14},... | collective-permute-start | bytes 1920008 | tf_op jit(solution)/shard_map/ppermute | solution.py:199
  1112.9 24.2 %collective-permute-start.87 = (f32[4800]{0:T(1024)S(1)}, f32[4800]{0:T(1024)S(1)}, u32[]{:S(2)}, u32[]{:S(2)}) collective-permute-start(f32[4800]{0:T(1024)S(1)} %get-tuple-element.696), channel_id=1, source_target_pairs={{0,1},{1,0},{2,3},{3,2},{4,5},{5,4},{6,7},{7,6},{8,9},{9,8},{10,11... | collective-permute-start | bytes 57608 | tf_op jit(solution)/shard_map/ppermute | solution.py:199
  1115.4 22.9 %collective-permute-start.89 = (f32[4800]{0:T(1024)S(1)}, f32[4800]{0:T(1024)S(1)}, u32[]{:S(2)}, u32[]{:S(2)}) collective-permute-start(f32[4800]{0:T(1024)S(1)} %add.765), channel_id=1, source_target_pairs={{0,2},{1,3},{2,0},{3,1},{4,6},{5,7},{6,4},{7,5},{8,10},{9,11},{10,... | collective-permute-start | bytes 57608 | tf_op jit(solution)/shard_map/ppermute | solution.py:199
  1116.6 55.9 %collective-permute-start.92 = (bf16[400,1536]{1,0:T(8,128)(2,1)S(1)}, bf16[400,1536]{1,0:T(8,128)(2,1)}, u32[]{:S(2)}, u32[]{:S(2)}) collective-permute-start(bf16[400,1536]{1,0:T(8,128)(2,1)S(1)} %pad_maximum_fusion.8.refs_0_), channel_id=1, source_target_pairs={{0,8},{4,12},{8,0},{12,4},{1,9},{5,13},{9,1},{13,5},{2,10},{6,14},... | collective-permute-start | bytes 3686408 | tf_op jit(solution)/shard_map/ppermute | solution.py:199
  1137.1 33.4 %collective-permute-start.99 = (bf16[400,800]{1,0:T(8,128)(2,1)S(1)}, bf16[400,800]{1,0:T(8,128)(2,1)S(1)}, u32[]{:S(2)}, u32[]{:S(2)}) collective-permute-start(bf16[400,800]{1,0:T(8,128)(2,1)S(1)} %get-tuple-element.801.refs_0_), channel_id=1, source_target_pairs={{0,8},{4,12},{8,0},{12,4},{1,9},{5,13},{9,1},{13,5},{2,10},{6,14},... | collective-permute-start | bytes 1920008 | tf_op jit(solution)/shard_map/ppermute | solution.py:199
  1138.3 34.2 %collective-permute-start.98 = (bf16[400,800]{1,0:T(8,128)(2,1)S(1)}, bf16[400,800]{1,0:T(8,128)(2,1)S(1)}, u32[]{:S(2)}, u32[]{:S(2)}) collective-permute-start(bf16[400,800]{1,0:T(8,128)(2,1)S(1)} %get-tuple-element.801.refs_0_), channel_id=1, source_target_pairs={{0,4},{4,0},{8,12},{12,8},{1,5},{5,1},{9,13},{13,9},{2,6},{6,2},{1... | collective-permute-start | bytes 1920008 | tf_op jit(solution)/shard_map/ppermute | solution.py:199
  1148.9 32.3 %collective-permute-start.83 = (bf16[256,1600]{0,1:T(8,128)(2,1)}, bf16[256,1600]{0,1:T(8,128)(2,1)S(1)}, u32[]{:S(2)}, u32[]{:S(2)}) collective-permute-start(bf16[256,1600]{0,1:T(8,128)(2,1)} %broadcast_select_fusion.4), channel_id=1, source_target_pairs={{0,16},{16,0},{1,17},{17,1},{2,18},{18,2},{3,19},{19,3},{4,20},{20... | collective-permute-start | bytes 2457608 | tf_op jit(solution)/shard_map/ppermute | solution.py:199
  1150.3 31.6 %collective-permute-start.103 = (bf16[400,800]{1,0:T(8,128)(2,1)S(1)}, bf16[400,800]{1,0:T(8,128)(2,1)S(1)}, u32[]{:S(2)}, u32[]{:S(2)}) collective-permute-start(bf16[400,800]{1,0:T(8,128)(2,1)S(1)} %collective-permute-done.102.refs_6_), channel_id=1, source_target_pairs={{0,4},{4,0},{8,12},{12,8},{1,5},{5,1},{9,13},{13,9},{2,6},{6,2},{1... | collective-permute-start | bytes 1920008 | tf_op jit(solution)/shard_map/ppermute | solution.py:199
  1170.5 22.5 %collective-permute-start.91 = (bf16[400,1536]{1,0:T(8,128)(2,1)S(1)}, bf16[400,1536]{1,0:T(8,128)(2,1)S(1)}, u32[]{:S(2)}, u32[]{:S(2)}) collective-permute-start(bf16[400,1536]{1,0:T(8,128)(2,1)S(1)} %pad_maximum_fusion.8.refs_0_), channel_id=1, source_target_pairs={{0,4},{4,0},{8,12},{12,8},{1,5},{5,1},{9,13},{13,9},{2,6},{6,2},{1... | collective-permute-start | bytes 3686408 | tf_op jit(solution)/shard_map/ppermute | solution.py:199
  1172.6 20.5 %collective-permute-start.93 = (bf16[400,1536]{1,0:T(8,128)(2,1)}, bf16[400,1536]{1,0:T(8,128)(2,1)S(1)}, u32[]{:S(2)}, u32[]{:S(2)}) collective-permute-start(bf16[400,1536]{1,0:T(8,128)(2,1)} %collective-permute-done.92.refs_2_), channel_id=1, source_target_pairs={{0,4},{4,0},{8,12},{12,8},{1,5},{5,1},{9,13},{13,9},{2,6},{6,2},{1... | collective-permute-start | bytes 3686408 | tf_op jit(solution)/shard_map/ppermute | solution.py:199
  (210 other events, 3034.8 us)
Sparse Core Ops, SparseCore 0:
  32.4 54.7 all-gather.9
  88.8 33.9 all-gather.11
  125.0 58.4 all-gather.13
  185.0 54.1 all-gather.15
  240.6 33.7 all-gather.17
  275.8 51.6 all-gather.19
  329.1 57.6 all-gather.21
  388.4 98.2 all-gather.23
  536.1 94.2 reduce-scatter.10
  644.6 54.2 reduce-scatter.12
  727.8 32.7 reduce-scatter.14
  792.0 49.0 reduce-scatter.16
  859.2 53.0 reduce-scatter.24
  957.5 57.3 reduce-scatter.18
  1041.0 49.3 reduce-scatter.20
  1099.6 35.4 reduce-scatter.22

commit v3 on v2

--- a/solution.py
+++ b/solution.py
@@ -732,9 +732,11 @@
         (0, GATHERED): ((MOVED, FC, 0), (FULL, OUT, 0)),
         (0, ACTIVE): ((FULL, PROJ, 1),),
         (0, RESULT): ((MOVED, PROJ, 1), (FULL, QKV, 1)),
-        (1, NORM): ((MOVED, QKV, 1), (FULL, FC, 1)),
+        (1, NORM): ((MOVED, QKV, 1), (FULL, FC, 1), (TOKEN,)),
         (1, GATHERED): ((MOVED, FC, 1),),
     }
+
+    coming_parts = []
 
     def forward_pin(layer):
         def pin(point, value):
@@ -752,11 +754,17 @@
                 started.append(full[OUT, 1])
             for kind, *key in front.get((layer, point), ()):
                 key = tuple(key)
-                if kind == FULL:
+                if kind == TOKEN:
+                    token, value = tied(tiny, value)
+                    token, value = tied(swap(token, CTX), value)
+                    started.append(token)
+                elif kind == FULL:
                     full[key], value = tied(full[key], value)
                     move(key)
                 else:
                     moved[key], value = tied(moved[key], value)
+            if (layer, point) == (1, GATHERED):
+                coming_parts.extend(gathered(after(coming, *value), CTX))
             return value
 
         return pin
@@ -917,7 +925,7 @@
     for layer in (1, 0):
         coming, vector_grads[layer] = backward_layer(
             coming,
-            plan.gathered(coming),
+            coming_parts if layer else plan.gathered(coming),
             kept[layer],
             functools.partial(weight, layer),
             vectors[layer],
@@ -932,10 +940,11 @@
         there = swap(jnp.where(first, sums[name, 1], sums[name, 0]), SECTION)
         return jnp.where(first, sums[name, 0], sums[name, 1]), there
 
+    fc_away, coming = tied(jnp.where(first, sums[FC, 1], sums[FC, 0]), coming)
+    fc_own, fc_there = jnp.where(first, sums[FC, 0], sums[FC, 1]), swap(fc_away, SECTION)
     sent[QKV, 0], coming = tied(sent[QKV, 0], coming)
     ready[QKV, 0] = add((QKV, 0), None)
     sums[QKV, 0] = scatter_wt(after(ready[QKV, 0], sums[FC, 0]))
-    fc_own, fc_there = to_owner(FC)
     fc_halves = (jnp.where(first, fc_own, fc_there), jnp.where(first, fc_there, fc_own))
     fc_parts = [gathered(value, CTX) for value in fc_halves]
     leaving = state([coming], [fc_there])

time: 1220 us -> 1200 us (0.984)
  waiting for transfers between devices: 473 us -> 458 us
    ppermute x104, waiting for transfers between devices: 449 us -> 434 us  [swap(): return lax.ppermute(value, axis, flip(axis, bit))]
    unnamed x326 -> x335, local copies, waits for them, and re-layouts: 44.8 us -> 46.8 us
  transfers between devices with their start and end apart: 122 -> 122, of which waited for: 62 -> 61; matrix products, arithmetic and copies ran while one was open for 38% -> 38% of each run, Pallas kernels for 8% -> 8%
where the time goes in v3:
time: 1200 us; the launch traced here: 1190 us
  waiting for transfers between devices  458 us (38%)
  matrix products  211 us (18%)
  local copies, waits for them, and re-layouts  159 us (13%)
  other arithmetic  120 us (10%)
  starting transfers between devices  119 us (10%)
  Pallas kernels  103 us (9%)
  between operations  16.8 us (1%)
    ppermute x104, waiting for transfers between devices, swap(): return lax.ppermute(value, axis, flip(axis, bit))  434 us
    ppermute x104, starting transfers between devices, swap(): return lax.ppermute(value, axis, flip(axis, bit))  112 us
    dot_general x12, matrix products, dot_tn(): lax.dot_general(left, right, (((0,), (0,)), ((), ())), preferred_element_...  72.1 us
    dot_general x12, matrix products, dot(): return jnp.dot(left, right, preferred_element_type=jnp.float32)  70.7 us
    dot_general x12, matrix products, dot_nt(): lax.dot_general(left, right, (((1,), (1,)), ((), ())), preferred_element_...  68.5 us
    unnamed x335, local copies, waits for them, and re-layouts  46.8 us
    pallas_call x2, Pallas kernels, attend_back(): pl.pallas_call(functools.partial(attend_back_kernel, block, tile, heads),...  42.3 us
    pallas_call x2, Pallas kernels, attend(): pl.pallas_call(functools.partial(attend_kernel, block, tile, heads), out_...  32.2 us
  transfers between devices with their start and end apart: 122, of which 61 were waited for; matrix products, arithmetic and copies ran while one was open for 38% of the time, Pallas kernels for 8%

profile of v3, /device:TPU:1, one launch (start us, length us, event | category | flops | bytes accessed | tf_op | source)
XLA Modules:
  0.0 1189.5 jit_solution(12073723902983543259)
XLA Ops:
  17.2 13.8 %collective-permute-done.49 = bf16[200,1536]{1,0:T(8,128)(2,1)S(1)} collective-permute-done((bf16[200,1536]{1,0:T(8,128)(2,1)}, bf16[200,1536]{1,0:T(8,128)(2,1)S(1)}, u32[]{:S(2)}, u32[]{:S(2)}) %collective-permute-start.49) | collective-permute-done | bytes 614432 | tf_op jit(solution)/shard_map/ppermute | solution.py:199
  40.8 11.5 collective-permute-done.51
  79.1 11.4 collective-permute-done.54
  97.9 23.1 %conditional.17 = (bf16[256,1600]{0,1:T(8,128)(2,1)}, bf16[256,1600]{0,1:T(8,128)(2,1)}, bf16[256,1600]{0,1:T(8,128)(2,1)}) conditional(s32[]{:T(128)} %bitcast.29, () %tuple.252, bf16[256,1600]{0,1:T(8,128)(2,1)S(1)} %fusion.73), branch_computations={%region_2.3_spmd, %region_3.4_spmd} | conditional | bytes 9830544 | solution.py:266
  104.6 8.0 collective-permute-done.1
  133.2 22.6 %collective-permute-done.60.refs_2_ = bf16[448,1600]{1,0:T(8,128)(2,1)S(1)} collective-permute-done((bf16[448,1600]{1,0:T(8,128)(2,1)}, bf16[448,1600]{1,0:T(8,128)(2,1)S(1)}, u32[]{:S(2)}, u32[]{:S(2)}) %collective-permute-start.60) | collective-permute-done | bytes 1433632 | tf_op jit(solution)/shard_map/ppermute | solution.py:199
  160.6 6.5 add_convert_fusion.11.qkv
  167.1 16.6 %shard_map.254 = (bf16[1024,512]{1,0:T(8,128)(2,1)}, f32[8,1024]{1,0:T(8,128)S(1)}) custom-call(s32[8]{0:T(128)S(1)} %select_reduce_fusion.place, bf16[1024,1536]{1,0:T(8,128)(2,1)S(1)} %add_convert_fusion.11.qkv), custom_call_target="tpu_custom_call" | custom-call | tf_op jit(solution)/shard_map/pallas_call | solution.py:86
  198.1 15.4 %conditional.18 = (bf16[1,256,512]{2,1,0:T(8,128)(2,1)}, bf16[1,256,512]{2,1,0:T(8,128)(2,1)}, bf16[1,256,512]{2,1,0:T(8,128)(2,1)}) conditional(s32[]{:T(128)} %bitcast.29, () %tuple.258, bf16[1024,512]{1,0:T(8,128)(2,1)} %get-tuple-element.399), branch_computations={%region_6.7_spmd, %region_7.8_spmd} | conditional | bytes 4718736 | solution.py:266
  201.5 6.8 collective-permute-done.21
  232.8 23.1 %conditional.19 = (bf16[256,1600]{0,1:T(8,128)(2,1)}, bf16[256,1600]{0,1:T(8,128)(2,1)}, bf16[256,1600]{0,1:T(8,128)(2,1)}) conditional(s32[]{:T(128)} %bitcast.29, () %tuple.259, bf16[256,1600]{0,1:T(8,128)(2,1)S(1)} %add_convert_fusion.18), branch_computations={%region_10.11_spmd, %region_11.12_spmd} | conditional | bytes 9830544 | solution.py:266
  235.0 17.0 %collective-permute-done.4 = bf16[256,1600]{0,1:T(8,128)(2,1)} collective-permute-done((bf16[256,1600]{0,1:T(8,128)(2,1)S(1)}, bf16[256,1600]{0,1:T(8,128)(2,1)}, u32[]{:S(2)}, u32[]{:S(2)}) %collective-permute-start.4) | collective-permute-done | bytes 819232 | tf_op jit(solution)/shard_map/cond/branch_1_fun/ppermute | solution.py:199
  266.0 7.2 fusion.31
  277.9 29.5 %collective-permute-done.66.refs_2_ = bf16[448,1600]{1,0:T(8,128)(2,1)S(1)} collective-permute-done((bf16[448,1600]{1,0:T(8,128)(2,1)}, bf16[448,1600]{1,0:T(8,128)(2,1)S(1)}, u32[]{:S(2)}, u32[]{:S(2)}) %collective-permute-start.66) | collective-permute-done | bytes 1433632 | tf_op jit(solution)/shard_map/ppermute | solution.py:199
  315.7 6.9 add_convert_fusion.9
  329.6 26.1 %conditional.20 = (f32[256,1600]{0,1:T(8,128)}) conditional(s32[]{:T(128)} %bitcast.29, () %tuple.268, bf16[1024,1600]{0,1:T(8,128)(2,1)} %add_convert_fusion.9), branch_computations={%region_12.13_spmd, %region_13.14_spmd} | conditional | flops 3686400 | bytes 32768156 | solution.py:266
  335.9 18.4 %collective-permute-done.27 = bf16[256,1600]{0,1:T(8,128)(2,1)S(1)} collective-permute-done((bf16[256,1600]{0,1:T(8,128)(2,1)S(1)}, bf16[256,1600]{0,1:T(8,128)(2,1)S(1)}, u32[]{:S(2)}, u32[]{:S(2)}) %collective-permute-start.27) | collective-permute-done | bytes 819232 | tf_op jit(solution)/shard_map/cond/branch_1_fun/ppermute | solution.py:199
  359.8 23.2 %conditional.21 = (bf16[256,1600]{0,1:T(8,128)(2,1)}, bf16[256,1600]{0,1:T(8,128)(2,1)}, bf16[256,1600]{0,1:T(8,128)(2,1)}) conditional(s32[]{:T(128)} %bitcast.29, () %tuple.269, bf16[256,1600]{0,1:T(8,128)(2,1)S(1)} %fusion.64), branch_computations={%region_16.17_spmd, %region_17.18_spmd} | conditional | bytes 9830544 | solution.py:266
  362.4 16.2 %collective-permute-done.7 = bf16[256,1600]{0,1:T(8,128)(2,1)} collective-permute-done((bf16[256,1600]{0,1:T(8,128)(2,1)S(1)}, bf16[256,1600]{0,1:T(8,128)(2,1)}, u32[]{:S(2)}, u32[]{:S(2)}) %collective-permute-start.7) | collective-permute-done | bytes 819232 | tf_op jit(solution)/shard_map/cond/branch_1_fun/ppermute | solution.py:199
  405.2 6.5 add_convert_fusion.10.qkv
  411.7 15.6 %shard_map.256 = (bf16[1024,512]{1,0:T(8,128)(2,1)S(1)}, f32[8,1024]{1,0:T(8,128)S(1)}) custom-call(s32[8]{0:T(128)S(1)} %select_reduce_fusion.place, bf16[1024,1536]{1,0:T(8,128)(2,1)S(1)} %add_convert_fusion.10.qkv), custom_call_target="tpu_custom_call" | custom-call | tf_op jit(solution)/shard_map/pallas_call | solution.py:86
  429.1 14.4 %conditional.22 = (bf16[1,256,512]{2,1,0:T(8,128)(2,1)}, bf16[1,256,512]{2,1,0:T(8,128)(2,1)}, bf16[1,256,512]{2,1,0:T(8,128)(2,1)}) conditional(s32[]{:T(128)} %bitcast.29, () %tuple.274, bf16[1024,512]{1,0:T(8,128)(2,1)S(1)} %get-tuple-element.454), branch_computations={%region_18.19_spmd, %region_19.20_spmd} | conditional | bytes 4718736 | solution.py:266
  431.3 6.9 collective-permute-done.24
  457.6 23.4 %conditional.23 = (bf16[256,1600]{0,1:T(8,128)(2,1)}, bf16[256,1600]{0,1:T(8,128)(2,1)}, bf16[256,1600]{0,1:T(8,128)(2,1)}) conditional(s32[]{:T(128)} %bitcast.29, () %tuple.275, bf16[256,1600]{0,1:T(8,128)(2,1)S(1)} %add_convert_fusion.16), branch_computations={%region_22.23_spmd, %region_23.24_spmd} | conditional | bytes 9830544 | solution.py:266
  459.6 17.3 %collective-permute-done.10 = bf16[256,1600]{0,1:T(8,128)(2,1)} collective-permute-done((bf16[256,1600]{0,1:T(8,128)(2,1)S(1)}, bf16[256,1600]{0,1:T(8,128)(2,1)}, u32[]{:S(2)}, u32[]{:S(2)}) %collective-permute-start.10) | collective-permute-done | bytes 819232 | tf_op jit(solution)/shard_map/cond/branch_1_fun/ppermute | solution.py:199
  494.1 6.7 collective-permute-done.71
  502.0 7.1 fusion.41
  555.4 24.5 %conditional.24 = (f32[256,1600]{0,1:T(8,128)}, f32[1,4,400]{2,1,0:T(4,128)S(1)}) conditional(s32[]{:T(128)} %bitcast.29, () %tuple.282, bf16[1024,1600]{0,1:T(8,128)(2,1)S(1)} %add_convert_fusion.8), branch_computations={%region_25.26_spmd, %region_26.28_spmd} | conditional | flops 4094400 | bytes 19680136 | solution.py:266
  559.6 18.4 %collective-permute-done.33 = bf16[256,1600]{0,1:T(8,128)(2,1)S(1)} collective-permute-done((bf16[256,1600]{0,1:T(8,128)(2,1)S(1)}, bf16[256,1600]{0,1:T(8,128)(2,1)S(1)}, u32[]{:S(2)}, u32[]{:S(2)}) %collective-permute-start.33) | collective-permute-done | bytes 819232 | tf_op jit(solution)/shard_map/cond/branch_1_fun/ppermute | solution.py:199
  594.5 16.4 %conditional.25 = (bf16[256,512]{1,0:T(8,128)(2,1)}, bf16[256,512]{1,0:T(8,128)(2,1)}, bf16[256,512]{1,0:T(8,128)(2,1)}, bf16[4,112,1600]{2,1,0:T(8,128)(2,1)}, ...) conditional(s32[]{:T(128)} %bitcast.29, () %tuple.281, ...), branch_computations={%region_30.31_spmd, %region_31.32_spmd} | conditional | flops 1313280000 | bytes 22946264 | solution.py:266
  619.4 8.5 add_convert_fusion.13
  628.0 7.6 conditional.26
  638.0 21.2 %shard_map.258 = bf16[1024,1536]{1,0:T(8,128)(2,1)} custom-call(s32[8]{0:T(128)S(1)} %select_reduce_fusion.place, bf16[1024,1536]{1,0:T(8,128)(2,1)S(1)} %add_convert_fusion.10.qkv, bf16[1024,512]{1,0:T(8,128)(2,1)S(1)} %copy-done.3, f32[8,1024]{1,0:T(8,128)S(1)} %get-tuple-element.496.log_total), custom_call_target="tpu_custom_call" | custom-call | tf_op jit(solution)/shard_map/pallas_call | solution.py:167
  659.2 12.0 %collective-permute-done.74 = bf16[4,112,1600]{2,1,0:T(8,128)(2,1)S(1)} collective-permute-done((bf16[4,112,1600]{2,1,0:T(8,128)(2,1)S(1)}, bf16[4,112,1600]{2,1,0:T(8,128)(2,1)S(1)}, u32[]{:S(2)}, u32[]{:S(2)}) %collective-permute-start.74) | collective-permute-done | bytes 1433632 | tf_op jit(solution)/shard_map/ppermute | solution.py:199
  676.5 9.1 convolution_convert_fusion.6
  685.6 25.4 %conditional.27 = (f32[256,1600]{0,1:T(8,128)S(1)}, bf16[4,2,200,1536]{3,2,1,0:T(8,128)(2,1)}) conditional(s32[]{:T(128)} %bitcast.29, () %tuple.292, (bf16[1024,1600]{0,1:T(8,128)(2,1)}, bf16[1024,1600]{0,1:T(8,128)(2,1)}, bf16[1024,1536]{1,0:T(8,128)(2,1)S(1)}) %tuple.529), branch_computations={%region_36.37_spmd, %region_37.38_spmd} | conditional | flops 5039308800 | bytes 44105892 | solution.py:266
  692.1 8.8 convolution_convert_fusion.1
  701.0 9.7 collective-permute-done.45
  720.6 23.4 %conditional.28 = (bf16[256,1600]{0,1:T(8,128)(2,1)}, bf16[256,1600]{0,1:T(8,128)(2,1)}, bf16[256,1600]{0,1:T(8,128)(2,1)}) conditional(s32[]{:T(128)} %bitcast.29, () %tuple.297, bf16[256,1600]{0,1:T(8,128)(2,1)S(1)} %get-tuple-element.516), branch_computations={%region_40.41_spmd, %region_41.42_spmd} | conditional | bytes 9830544 | solution.py:266
  723.1 16.3 %collective-permute-done.13 = bf16[256,1600]{0,1:T(8,128)(2,1)} collective-permute-done((bf16[256,1600]{0,1:T(8,128)(2,1)S(1)}, bf16[256,1600]{0,1:T(8,128)(2,1)}, u32[]{:S(2)}, u32[]{:S(2)}) %collective-permute-start.13) | collective-permute-done | bytes 819232 | tf_op jit(solution)/shard_map/cond/branch_1_fun/ppermute | solution.py:199
  744.0 6.8 convolution_convert_fusion.10
  761.2 7.7 multiply_convert_fusion
  784.1 6.1 fusion.118
  794.1 34.0 %conditional.29 = (f32[256,1600]{0,1:T(8,128)S(1)}, f32[800,1600]{1,0:T(8,128)}) conditional(s32[]{:T(128)} %bitcast.29, () %tuple.302, (bf16[1024,1600]{0,1:T(8,128)(2,1)S(1)}, bf16[256,1600]{0,1:T(8,128)(2,1)S(1)}, bf16[256,1600]{0,1:T(8,128)(2,1)}, bf16[256,1600]{0,1:T(8,128)(2,1)}, bf16[256,1600]{0,1:T(8,128)(2,1)}, ...), branch_computations={%region_43.44_spmd, %region_44.45_spmd} | conditional | flops 2640793600 | bytes 49356964 | solution.py:266
  808.1 7.5 convert_bitcast_fusion
  815.5 10.8 collective-permute-done.39
  828.1 8.8 collective-permute-done.77
  842.5 7.2 convolution_convert_fusion.9
  858.8 17.1 %conditional.30 = (bf16[256,512]{1,0:T(8,128)(2,1)}, bf16[256,512]{1,0:T(8,128)(2,1)}, bf16[256,512]{1,0:T(8,128)(2,1)}, bf16[4,112,1600]{2,1,0:T(8,128)(2,1)}, ...) conditional(s32[]{:T(128)} %bitcast.29, () %tuple.308, ...), branch_computations={%region_48.49_spmd, %region_49.50_spmd} | conditional | flops 1313280000 | bytes 22946264 | solution.py:266
  875.9 7.5 conditional.31
  893.3 21.1 %shard_map.259 = bf16[1024,1536]{1,0:T(8,128)(2,1)S(1)} custom-call(s32[8]{0:T(128)S(1)} %select_reduce_fusion.place, bf16[1024,1536]{1,0:T(8,128)(2,1)} %copy-done.2, bf16[1024,512]{1,0:T(8,128)(2,1)S(1)} %copy-done.4, f32[8,1024]{1,0:T(8,128)S(1)} %get-tuple-element.546.log_total), custom_call_target="tpu_custom_call" | custom-call | tf_op jit(solution)/shard_map/pallas_call | solution.py:167
  914.4 8.2 collective-permute-done.79
  932.1 8.5 add_convert_fusion.12
  941.1 7.4 convolution_convert_fusion.4
  954.1 8.0 convolution_convert_fusion.5
  965.9 48.1 %conditional.32 = (f32[256,1600]{0,1:T(8,128)}, f32[1,4,400]{2,1,0:T(4,128)S(1)}) conditional(s32[]{:T(128)} %bitcast.29, () %tuple.320, bf16[1024,1600]{0,1:T(8,128)(2,1)S(1)} %convolution_convert_fusion.5), branch_computations={%region_53.54_spmd, %region_54.56_spmd} | conditional | flops 4094400 | bytes 19680136 | solution.py:266
  971.2 41.2 %collective-permute-done.36 = bf16[256,1600]{0,1:T(8,128)(2,1)S(1)} collective-permute-done((bf16[256,1600]{0,1:T(8,128)(2,1)S(1)}, bf16[256,1600]{0,1:T(8,128)(2,1)S(1)}, u32[]{:S(2)}, u32[]{:S(2)}) %collective-permute-start.36) | collective-permute-done | bytes 819232 | tf_op jit(solution)/shard_map/cond/branch_1_fun/ppermute | solution.py:199
  1041.8 9.0 collective-permute-done.82
  1051.6 25.9 %conditional.33 = (f32[256,1600]{0,1:T(8,128)}) conditional(s32[]{:T(128)} %bitcast.29, () %tuple.327, bf16[1024,1600]{0,1:T(8,128)(2,1)} %add_convert_fusion.6), branch_computations={%region_58.59_spmd, %region_59.60_spmd} | conditional | flops 3686400 | bytes 32768156 | solution.py:266
  1057.3 18.6 %collective-permute-done.30 = bf16[256,1600]{0,1:T(8,128)(2,1)S(1)} collective-permute-done((bf16[256,1600]{0,1:T(8,128)(2,1)S(1)}, bf16[256,1600]{0,1:T(8,128)(2,1)S(1)}, u32[]{:S(2)}, u32[]{:S(2)}) %collective-permute-start.30) | collective-permute-done | bytes 819232 | tf_op jit(solution)/shard_map/cond/branch_1_fun/ppermute | solution.py:199
  1098.7 17.7 %reduce-scatter.23.cloned.1.call-done = bf16[112,1600]{1,0:T(8,128)(2,1)} async-done(((bf16[448,1600]{1,0:T(8,128)(2,1)}), bf16[112,1600]{1,0:T(8,128)(2,1)}) %reduce-scatter.23.cloned.1.call-update) | async-done | bytes 358416 | tf_op jit(solution)/shard_map/reduce_scatter | solution.py:290
  1123.3 6.9 collective-permute-done.94
  1132.8 19.1 %collective-permute-done.99.refs_2_ = bf16[400,800]{1,0:T(8,128)(2,1)S(1)} collective-permute-done((bf16[400,800]{1,0:T(8,128)(2,1)S(1)}, bf16[400,800]{1,0:T(8,128)(2,1)S(1)}, u32[]{:S(2)}, u32[]{:S(2)}) %collective-permute-start.99) | collective-permute-done | bytes 640032 | tf_op jit(solution)/shard_map/ppermute | solution.py:199
  1167.7 6.6 shard_map.262
  (868 shorter events, 586.5 us)
Async XLA Ops:
  7.2 88.4 %all-gather.10.cloned.1.call-start = ((), (), s32[]{:S(2)}) async-start(), calls=%async_computation.8 | async-start | bytes 3072000 | tf_op jit(solution)/shard_map/all_gather | solution.py:286
  32.3 90.5 %all-gather.12.cloned.1.call-start = ((), (), s32[]{:S(2)}) async-start(), calls=%async_computation.9 | async-start | bytes 1863680 | tf_op jit(solution)/shard_map/all_gather | solution.py:286
  33.3 29.2 %collective-permute-start.50 = (bf16[256,1600]{0,1:T(8,128)(2,1)}, bf16[256,1600]{0,1:T(8,128)(2,1)}, u32[]{:S(2)}, u32[]{:S(2)}) collective-permute-start(bf16[256,1600]{0,1:T(8,128)(2,1)} %dynamic-slice_bitcast_fusion), channel_id=1, source_target_pairs={{0,16},{16,0},{1,17},{17,1},{2,18},{18,2},{3,19},{19,3},{4,20},{20... | collective-permute-start | bytes 2457608 | tf_op jit(solution)/shard_map/ppermute | solution.py:199
  37.1 23.2 %collective-permute-start.52 = (bf16[112,1600]{1,0:T(8,128)(2,1)}, bf16[112,1600]{1,0:T(8,128)(2,1)}, u32[]{:S(2)}, u32[]{:S(2)}) collective-permute-start(bf16[112,1600]{1,0:T(8,128)(2,1)} %dynamic-slice_bitcast_fusion.3), channel_id=1, source_target_pairs={{0,16},{16,0},{1,17},{17,1},{2,18},{18,2},{3,19},{19,3},{4,20},{20... | collective-permute-start | bytes 1075208 | tf_op jit(solution)/shard_map/ppermute | solution.py:199
  62.5 126.8 %all-gather.14.cloned.1.call-start = ((), (), s32[]{:S(2)}) async-start(), calls=%async_computation.10 | async-start | bytes 3584000 | tf_op jit(solution)/shard_map/all_gather | solution.py:286
  76.7 179.2 %all-gather.16.cloned.1.call-start = ((), (), s32[]{:S(2)}) async-start(), calls=%async_computation.11 | async-start | bytes 3328000 | tf_op jit(solution)/shard_map/all_gather | solution.py:286
  94.9 179.5 %all-gather.18.cloned.1.call-start = ((), (), s32[]{:S(2)}) async-start(), calls=%async_computation.12 | async-start | bytes 1863680 | tf_op jit(solution)/shard_map/all_gather | solution.py:286
  95.5 232.1 %all-gather.20.cloned.1.call-start = ((), (), s32[]{:S(2)}) async-start(), calls=%async_computation.13 | async-start | bytes 3072000 | tf_op jit(solution)/shard_map/all_gather | solution.py:286
  95.6 62.5 %collective-permute-start.58 = (bf16[800,1536]{1,0:T(8,128)(2,1)}, bf16[800,1536]{1,0:T(8,128)(2,1)}, u32[]{:S(2)}, u32[]{:S(2)}) collective-permute-start(bf16[800,1536]{1,0:T(8,128)(2,1)} %all-gather.10.cloned.1.call-done), channel_id=1, source_target_pairs={{0,16},{16,0},{1,17},{17,1},{2,18},{18,2},{3,19},{19,3},{4,20},{20... | collective-permute-start | bytes 7372808 | tf_op jit(solution)/shard_map/ppermute | solution.py:199
  99.2 19.6 %collective-permute-start = (bf16[256,1600]{0,1:T(8,128)(2,1)S(1)}, bf16[256,1600]{0,1:T(8,128)(2,1)}, u32[]{:S(2)}, u32[]{:S(2)}) collective-permute-start(bf16[256,1600]{0,1:T(8,128)(2,1)S(1)} %param.1), channel_id=1, source_target_pairs={{0,4},{4,0},{8,12},{12,8},{1,5},{5,1},{9,13},{13,9},{2,6},{6,2},{1... | collective-permute-start | bytes 2457608 | tf_op jit(solution)/shard_map/cond/branch_1_fun/ppermute | solution.py:199
  122.8 33.0 %collective-permute-start.60 = (bf16[448,1600]{1,0:T(8,128)(2,1)}, bf16[448,1600]{1,0:T(8,128)(2,1)S(1)}, u32[]{:S(2)}, u32[]{:S(2)}) collective-permute-start(bf16[448,1600]{1,0:T(8,128)(2,1)} %all-gather.12.cloned.1.call-done.refs_0_), channel_id=1, source_target_pairs={{0,8},{4,12},{8,0},{12,4},{1,9},{5,13},{9,1},{13,5},{2,10},{6,14},... | collective-permute-start | bytes 4300808 | tf_op jit(solution)/shard_map/ppermute | solution.py:199
  124.3 61.2 %collective-permute-start.62 = (bf16[200,1600]{1,0:T(8,128)(2,1)}, bf16[200,1600]{1,0:T(8,128)(2,1)}, u32[]{:S(2)}, u32[]{:S(2)}) collective-permute-start(bf16[200,1600]{1,0:T(8,128)(2,1)} %get-tuple-element.390), channel_id=1, source_target_pairs={{0,16},{16,0},{1,17},{17,1},{2,18},{18,2},{3,19},{19,3},{4,20},{20... | collective-permute-start | bytes 1920008 | tf_op jit(solution)/shard_map/ppermute | solution.py:199
  125.6 263.7 %all-gather.22.cloned.1.call-start = ((), (), s32[]{:S(2)}) async-start(), calls=%async_computation.14 | async-start | bytes 3584000 | tf_op jit(solution)/shard_map/all_gather | solution.py:286
  125.8 62.3 %collective-permute-start.59 = (bf16[448,1600]{1,0:T(8,128)(2,1)}, bf16[448,1600]{1,0:T(8,128)(2,1)S(1)}, u32[]{:S(2)}, u32[]{:S(2)}) collective-permute-start(bf16[448,1600]{1,0:T(8,128)(2,1)} %all-gather.12.cloned.1.call-done.refs_0_), channel_id=1, source_target_pairs={{0,4},{4,0},{8,12},{12,8},{1,5},{5,1},{9,13},{13,9},{2,6},{6,2},{1... | collective-permute-start | bytes 4300808 | tf_op jit(solution)/shard_map/ppermute | solution.py:199
  155.8 33.4 %collective-permute-start.61 = (bf16[448,1600]{1,0:T(8,128)(2,1)S(1)}, bf16[448,1600]{1,0:T(8,128)(2,1)}, u32[]{:S(2)}, u32[]{:S(2)}) collective-permute-start(bf16[448,1600]{1,0:T(8,128)(2,1)S(1)} %collective-permute-done.60.refs_2_), channel_id=1, source_target_pairs={{0,4},{4,0},{8,12},{12,8},{1,5},{5,1},{9,13},{13,9},{2,6},{6,2},{1... | collective-permute-start | bytes 4300808 | tf_op jit(solution)/shard_map/ppermute | solution.py:199
  194.4 61.4 %collective-permute-start.63 = (bf16[1600,800]{0,1:T(8,128)(2,1)}, bf16[1600,800]{0,1:T(8,128)(2,1)}, u32[]{:S(2)}, u32[]{:S(2)}) collective-permute-start(bf16[1600,800]{0,1:T(8,128)(2,1)} %copy.197), channel_id=1, source_target_pairs={{0,16},{16,0},{1,17},{17,1},{2,18},{18,2},{3,19},{19,3},{4,20},{20... | collective-permute-start | bytes 7680008 | tf_op jit(solution)/shard_map/ppermute | solution.py:199
  234.0 19.6 %collective-permute-start.3 = (bf16[256,1600]{0,1:T(8,128)(2,1)S(1)}, bf16[256,1600]{0,1:T(8,128)(2,1)}, u32[]{:S(2)}, u32[]{:S(2)}) collective-permute-start(bf16[256,1600]{0,1:T(8,128)(2,1)S(1)} %param.5), channel_id=1, source_target_pairs={{0,4},{4,0},{8,12},{12,8},{1,5},{5,1},{9,13},{13,9},{2,6},{6,2},{1... | collective-permute-start | bytes 2457608 | tf_op jit(solution)/shard_map/cond/branch_1_fun/ppermute | solution.py:199
  255.9 59.8 %collective-permute-start.64 = (bf16[800,1600]{1,0:T(8,128)(2,1)}, bf16[800,1600]{1,0:T(8,128)(2,1)}, u32[]{:S(2)}, u32[]{:S(2)}) collective-permute-start(bf16[800,1600]{1,0:T(8,128)(2,1)} %all-gather.16.cloned.1.call-done), channel_id=1, source_target_pairs={{0,16},{16,0},{1,17},{17,1},{2,18},{18,2},{3,19},{19,3},{4,20},{20... | collective-permute-start | bytes 7680008 | tf_op jit(solution)/shard_map/ppermute | solution.py:199
  274.4 33.0 %collective-permute-start.66 = (bf16[448,1600]{1,0:T(8,128)(2,1)}, bf16[448,1600]{1,0:T(8,128)(2,1)S(1)}, u32[]{:S(2)}, u32[]{:S(2)}) collective-permute-start(bf16[448,1600]{1,0:T(8,128)(2,1)} %all-gather.18.cloned.1.call-done.refs_0_), channel_id=1, source_target_pairs={{0,8},{4,12},{8,0},{12,4},{1,9},{5,13},{9,1},{13,5},{2,10},{6,14},... | collective-permute-start | bytes 4300808 | tf_op jit(solution)/shard_map/ppermute | solution.py:199
  275.6 247.8 %all-gather.24.cloned.1.call-start = ((), (), s32[]{:S(2)}) async-start(), calls=%async_computation.22 | async-start | bytes 6656000 | tf_op jit(solution)/shard_map/all_gather | solution.py:286
  276.1 46.4 %collective-permute-start.65 = (bf16[448,1600]{1,0:T(8,128)(2,1)}, bf16[448,1600]{1,0:T(8,128)(2,1)S(1)}, u32[]{:S(2)}, u32[]{:S(2)}) collective-permute-start(bf16[448,1600]{1,0:T(8,128)(2,1)} %all-gather.18.cloned.1.call-done.refs_0_), channel_id=1, source_target_pairs={{0,4},{4,0},{8,12},{12,8},{1,5},{5,1},{9,13},{13,9},{2,6},{6,2},{1... | collective-permute-start | bytes 4300808 | tf_op jit(solution)/shard_map/ppermute | solution.py:199
  327.6 61.6 %collective-permute-start.68 = (bf16[800,1536]{1,0:T(8,128)(2,1)}, bf16[800,1536]{1,0:T(8,128)(2,1)}, u32[]{:S(2)}, u32[]{:S(2)}) collective-permute-start(bf16[800,1536]{1,0:T(8,128)(2,1)} %all-gather.20.cloned.1.call-done), channel_id=1, source_target_pairs={{0,16},{16,0},{1,17},{17,1},{2,18},{18,2},{3,19},{19,3},{4,20},{20... | collective-permute-start | bytes 7372808 | tf_op jit(solution)/shard_map/ppermute | solution.py:199
  329.6 343.0 %reduce-scatter.11.cloned.1.call-start = ((), (), s32[]{:S(2)}) async-start(), calls=%async_computation.15 | async-start | bytes 6656000 | tf_op jit(solution)/shard_map/reduce_scatter | solution.py:290
  334.6 19.6 %collective-permute-start.27 = (bf16[256,1600]{0,1:T(8,128)(2,1)S(1)}, bf16[256,1600]{0,1:T(8,128)(2,1)S(1)}, u32[]{:S(2)}, u32[]{:S(2)}) collective-permute-start(bf16[256,1600]{0,1:T(8,128)(2,1)S(1)} %add_convert_fusion), channel_id=1, source_target_pairs={{0,8},{4,12},{8,0},{12,4},{1,9},{5,13},{9,1},{13,5},{2,10},{6,14},... | collective-permute-start | bytes 2457608 | tf_op jit(solution)/shard_map/cond/branch_1_fun/ppermute | solution.py:199
  361.0 19.6 %collective-permute-start.6 = (bf16[256,1600]{0,1:T(8,128)(2,1)S(1)}, bf16[256,1600]{0,1:T(8,128)(2,1)}, u32[]{:S(2)}, u32[]{:S(2)}) collective-permute-start(bf16[256,1600]{0,1:T(8,128)(2,1)S(1)} %param.9), channel_id=1, source_target_pairs={{0,4},{4,0},{8,12},{12,8},{1,5},{5,1},{9,13},{13,9},{2,6},{6,2},{1... | collective-permute-start | bytes 2457608 | tf_op jit(solution)/shard_map/cond/branch_1_fun/ppermute | solution.py:199
  396.6 84.4 %collective-permute-start.69 = (bf16[1600,800]{0,1:T(8,128)(2,1)}, bf16[1600,800]{0,1:T(8,128)(2,1)}, u32[]{:S(2)}, u32[]{:S(2)}) collective-permute-start(bf16[1600,800]{0,1:T(8,128)(2,1)} %copy.198), channel_id=1, source_target_pairs={{0,16},{16,0},{1,17},{17,1},{2,18},{18,2},{3,19},{19,3},{4,20},{20... | collective-permute-start | bytes 7680008 | tf_op jit(solution)/shard_map/ppermute | solution.py:199
  457.6 19.3 %collective-permute-start.10 = (bf16[256,1600]{0,1:T(8,128)(2,1)S(1)}, bf16[256,1600]{0,1:T(8,128)(2,1)}, u32[]{:S(2)}, u32[]{:S(2)}) collective-permute-start(bf16[256,1600]{0,1:T(8,128)(2,1)S(1)} %param.13), channel_id=1, source_target_pairs={{0,8},{4,12},{8,0},{12,4},{1,9},{5,13},{9,1},{13,5},{2,10},{6,14},... | collective-permute-start | bytes 2457608 | tf_op jit(solution)/shard_map/cond/branch_1_fun/ppermute | solution.py:199
  458.7 19.7 %collective-permute-start.9 = (bf16[256,1600]{0,1:T(8,128)(2,1)S(1)}, bf16[256,1600]{0,1:T(8,128)(2,1)}, u32[]{:S(2)}, u32[]{:S(2)}) collective-permute-start(bf16[256,1600]{0,1:T(8,128)(2,1)S(1)} %param.13), channel_id=1, source_target_pairs={{0,4},{4,0},{8,12},{12,8},{1,5},{5,1},{9,13},{13,9},{2,6},{6,2},{1... | collective-permute-start | bytes 2457608 | tf_op jit(solution)/shard_map/cond/branch_1_fun/ppermute | solution.py:199
  481.0 19.7 %collective-permute-start.71 = (bf16[256,1600]{0,1:T(8,128)(2,1)}, bf16[256,1600]{0,1:T(8,128)(2,1)S(1)}, u32[]{:S(2)}, u32[]{:S(2)}) collective-permute-start(bf16[256,1600]{0,1:T(8,128)(2,1)} %get-tuple-element.472), channel_id=1, source_target_pairs={{0,8},{4,12},{8,0},{12,4},{1,9},{5,13},{9,1},{13,5},{2,10},{6,14},... | collective-permute-start | bytes 2457608 | tf_op jit(solution)/shard_map/ppermute | solution.py:199
  482.2 27.0 %collective-permute-start.70 = (bf16[256,1600]{0,1:T(8,128)(2,1)}, bf16[256,1600]{0,1:T(8,128)(2,1)S(1)}, u32[]{:S(2)}, u32[]{:S(2)}) collective-permute-start(bf16[256,1600]{0,1:T(8,128)(2,1)} %get-tuple-element.472), channel_id=1, source_target_pairs={{0,4},{4,0},{8,12},{12,8},{1,5},{5,1},{9,13},{13,9},{2,6},{6,2},{1... | collective-permute-start | bytes 2457608 | tf_op jit(solution)/shard_map/ppermute | solution.py:199
  521.0 229.8 %reduce-scatter.13.cloned.1.call-start = ((), (), s32[]{:S(2)}) async-start(), calls=%async_computation.16 | async-start | bytes 3584000 | tf_op jit(solution)/shard_map/reduce_scatter | solution.py:290
  544.8 69.3 %collective-permute-start.73 = (bf16[1600,800]{0,1:T(8,128)(2,1)}, bf16[1600,800]{0,1:T(8,128)(2,1)}, u32[]{:S(2)}, u32[]{:S(2)}) collective-permute-start(bf16[1600,800]{0,1:T(8,128)(2,1)} %convolution_convert_fusion.11), channel_id=1, source_target_pairs={{0,16},{16,0},{1,17},{17,1},{2,18},{18,2},{3,19},{19,3},{4,20},{20... | collective-permute-start | bytes 7680008 | tf_op jit(solution)/shard_map/ppermute | solution.py:199
  558.4 19.6 %collective-permute-start.33 = (bf16[256,1600]{0,1:T(8,128)(2,1)S(1)}, bf16[256,1600]{0,1:T(8,128)(2,1)S(1)}, u32[]{:S(2)}, u32[]{:S(2)}) collective-permute-start(bf16[256,1600]{0,1:T(8,128)(2,1)S(1)} %add_convert_fusion.1), channel_id=1, source_target_pairs={{0,8},{4,12},{8,0},{12,4},{1,9},{5,13},{9,1},{13,5},{2,10},{6,14},... | collective-permute-start | bytes 2457608 | tf_op jit(solution)/shard_map/cond/branch_1_fun/ppermute | solution.py:199
  627.9 221.8 %reduce-scatter.15.cloned.1.call-start = ((), (), s32[]{:S(2)}) async-start(), calls=%async_computation.17 | async-start | bytes 1863680 | tf_op jit(solution)/shard_map/reduce_scatter | solution.py:290
  637.1 34.0 %collective-permute-start.74 = (bf16[4,112,1600]{2,1,0:T(8,128)(2,1)S(1)}, bf16[4,112,1600]{2,1,0:T(8,128)(2,1)S(1)}, u32[]{:S(2)}, u32[]{:S(2)}) collective-permute-start(bf16[4,112,1600]{2,1,0:T(8,128)(2,1)S(1)} %convert_element_type.474), channel_id=1, source_target_pairs={{0,8},{4,12},{8,0},{12,4},{1,9},{5,13},{9,1},{13,5},{2,10},{6,14},... | collective-permute-start | bytes 4300808 | tf_op jit(solution)/shard_map/ppermute | solution.py:199
  672.6 43.7 %collective-permute-start.75 = (bf16[400,1600]{1,0:T(8,128)(2,1)}, bf16[400,1600]{1,0:T(8,128)(2,1)}, u32[]{:S(2)}, u32[]{:S(2)}) collective-permute-start(bf16[400,1600]{1,0:T(8,128)(2,1)} %reduce-scatter.11.cloned.1.call-done), channel_id=1, source_target_pairs={{0,16},{1,17},{2,18},{3,19},{4,20},{5,21},{6,22},{7,23},{8,24},{9,... | collective-permute-start | bytes 3840008 | tf_op jit(solution)/shard_map/ppermute | solution.py:836
  691.2 19.5 %collective-permute-start.45 = (bf16[256,1600]{0,1:T(8,128)(2,1)S(1)}, bf16[256,1600]{0,1:T(8,128)(2,1)S(1)}, u32[]{:S(2)}, u32[]{:S(2)}) collective-permute-start(bf16[256,1600]{0,1:T(8,128)(2,1)S(1)} %add_convert_fusion.2), channel_id=1, source_target_pairs={{0,8},{4,12},{8,0},{12,4},{1,9},{5,13},{9,1},{13,5},{2,10},{6,14},... | collective-permute-start | bytes 2457608 | tf_op jit(solution)/shard_map/cond/branch_1_fun/ppermute | solution.py:199
  711.0 214.5 %reduce-scatter.17.cloned.1.call-start = ((), (), s32[]{:S(2)}) async-start(), calls=%async_computation.18 | async-start | bytes 3072000 | tf_op jit(solution)/shard_map/reduce_scatter | solution.py:290
  717.3 54.0 %collective-permute-start.76 = (bf16[800,1536]{1,0:T(8,128)(2,1)}, bf16[800,1536]{1,0:T(8,128)(2,1)}, u32[]{:S(2)}, u32[]{:S(2)}) collective-permute-start(bf16[800,1536]{1,0:T(8,128)(2,1)} %bitcast.66), channel_id=1, source_target_pairs={{0,16},{16,0},{1,17},{17,1},{2,18},{18,2},{3,19},{19,3},{4,20},{20... | collective-permute-start | bytes 7372808 | tf_op jit(solution)/shard_map/ppermute | solution.py:199
  721.8 19.7 %collective-permute-start.12 = (bf16[256,1600]{0,1:T(8,128)(2,1)S(1)}, bf16[256,1600]{0,1:T(8,128)(2,1)}, u32[]{:S(2)}, u32[]{:S(2)}) collective-permute-start(bf16[256,1600]{0,1:T(8,128)(2,1)S(1)} %param.23), channel_id=1, source_target_pairs={{0,4},{4,0},{8,12},{12,8},{1,5},{5,1},{9,13},{13,9},{2,6},{6,2},{1... | collective-permute-start | bytes 2457608 | tf_op jit(solution)/shard_map/cond/branch_1_fun/ppermute | solution.py:199
  775.2 150.4 %reduce-scatter.25.cloned.1.call-start = ((), (), s32[]{:S(2)}) async-start(), calls=%async_computation.23 | async-start | bytes 3328000
  779.4 57.5 %collective-permute-start.77 = (bf16[800,1600]{1,0:T(8,128)(2,1)}, bf16[800,1600]{1,0:T(8,128)(2,1)}, u32[]{:S(2)}, u32[]{:S(2)}) collective-permute-start(bf16[800,1600]{1,0:T(8,128)(2,1)} %convolution_convert_fusion.10), channel_id=1, source_target_pairs={{0,16},{16,0},{1,17},{17,1},{2,18},{18,2},{3,19},{19,3},{4,20},{20... | collective-permute-start | bytes 7680008 | tf_op jit(solution)/shard_map/ppermute | solution.py:199
  806.9 19.5 %collective-permute-start.39 = (bf16[256,1600]{0,1:T(8,128)(2,1)S(1)}, bf16[256,1600]{0,1:T(8,128)(2,1)S(1)}, u32[]{:S(2)}, u32[]{:S(2)}) collective-permute-start(bf16[256,1600]{0,1:T(8,128)(2,1)S(1)} %add_convert_fusion.3), channel_id=1, source_target_pairs={{0,8},{4,12},{8,0},{12,4},{1,9},{5,13},{9,1},{13,5},{2,10},{6,14},... | collective-permute-start | bytes 2457608 | tf_op jit(solution)/shard_map/cond/branch_1_fun/ppermute | solution.py:199
  842.2 177.7 %reduce-scatter.19.cloned.1.call-start = ((), (), s32[]{:S(2)}) async-start(), calls=%async_computation.19 | async-start | bytes 3584000 | tf_op jit(solution)/shard_map/reduce_scatter | solution.py:290
  849.8 75.8 %collective-permute-start.78 = (bf16[1600,800]{0,1:T(8,128)(2,1)}, bf16[1600,800]{0,1:T(8,128)(2,1)}, u32[]{:S(2)}, u32[]{:S(2)}) collective-permute-start(bf16[1600,800]{0,1:T(8,128)(2,1)} %convolution_convert_fusion.9), channel_id=1, source_target_pairs={{0,16},{16,0},{1,17},{17,1},{2,18},{18,2},{3,19},{19,3},{4,20},{20... | collective-permute-start | bytes 7680008 | tf_op jit(solution)/shard_map/ppermute | solution.py:199
  888.2 34.4 %collective-permute-start.79 = (bf16[4,112,1600]{2,1,0:T(8,128)(2,1)}, bf16[4,112,1600]{2,1,0:T(8,128)(2,1)}, u32[]{:S(2)}, u32[]{:S(2)}) collective-permute-start(bf16[4,112,1600]{2,1,0:T(8,128)(2,1)} %convert_element_type.497), channel_id=1, source_target_pairs={{0,8},{4,12},{8,0},{12,4},{1,9},{5,13},{9,1},{13,5},{2,10},{6,14},... | collective-permute-start | bytes 4300808 | tf_op jit(solution)/shard_map/ppermute | solution.py:199
  925.6 28.5 %collective-permute-start.81 = (bf16[200,1600]{1,0:T(8,128)(2,1)}, bf16[200,1600]{1,0:T(8,128)(2,1)}, u32[]{:S(2)}, u32[]{:S(2)}) collective-permute-start(bf16[200,1600]{1,0:T(8,128)(2,1)} %reduce-scatter.25.cloned.1.call-done), channel_id=1, source_target_pairs={{16,0},{17,1},{18,2},{19,3},{20,4},{21,5},{22,6},{23,7},{24,8},{25... | collective-permute-start | bytes 1920008 | tf_op jit(solution)/shard_map/ppermute | solution.py:836
  940.6 140.2 %reduce-scatter.21.cloned.1.call-start = ((), (), s32[]{:S(2)}) async-start(), calls=%async_computation.20 | async-start | bytes 3072000 | tf_op jit(solution)/shard_map/reduce_scatter | solution.py:290
  951.2 71.0 %collective-permute-start.80 = (bf16[800,1536]{1,0:T(8,128)(2,1)}, bf16[800,1536]{1,0:T(8,128)(2,1)}, u32[]{:S(2)}, u32[]{:S(2)}) collective-permute-start(bf16[800,1536]{1,0:T(8,128)(2,1)} %bitcast.69), channel_id=1, source_target_pairs={{0,16},{16,0},{1,17},{17,1},{2,18},{18,2},{3,19},{19,3},{4,20},{20... | collective-permute-start | bytes 7372808 | tf_op jit(solution)/shard_map/ppermute | solution.py:199
  965.4 61.6 %collective-permute-start.104 = (bf16[400,1600]{1,0:T(8,128)(2,1)}, bf16[400,1600]{1,0:T(8,128)(2,1)}, u32[]{:S(2)}, u32[]{:S(2)}) collective-permute-start(bf16[400,1600]{1,0:T(8,128)(2,1)} %pad_maximum_fusion.5.refs_0_), channel_id=1, source_target_pairs={{0,8},{4,12},{8,0},{12,4},{1,9},{5,13},{9,1},{13,5},{2,10},{6,14},... | collective-permute-start | bytes 3840008 | tf_op jit(solution)/shard_map/ppermute | solution.py:199
  970.2 42.2 %collective-permute-start.36 = (bf16[256,1600]{0,1:T(8,128)(2,1)S(1)}, bf16[256,1600]{0,1:T(8,128)(2,1)S(1)}, u32[]{:S(2)}, u32[]{:S(2)}) collective-permute-start(bf16[256,1600]{0,1:T(8,128)(2,1)S(1)} %add_convert_fusion.4), channel_id=1, source_target_pairs={{0,8},{4,12},{8,0},{12,4},{1,9},{5,13},{9,1},{13,5},{2,10},{6,14},... | collective-permute-start | bytes 2457608 | tf_op jit(solution)/shard_map/cond/branch_1_fun/ppermute | solution.py:199
  1026.0 90.3 %reduce-scatter.23.cloned.1.call-start = ((), (), s32[]{:S(2)}) async-start(), calls=%async_computation.21 | async-start | bytes 1863680 | tf_op jit(solution)/shard_map/reduce_scatter | solution.py:290
  1030.6 86.8 %collective-permute-start.105 = (bf16[800,1600]{1,0:T(8,128)(2,1)}, bf16[800,1600]{1,0:T(8,128)(2,1)}, u32[]{:S(2)}, u32[]{:S(2)}) collective-permute-start(bf16[800,1600]{1,0:T(8,128)(2,1)} %pad_maximum_fusion.3), channel_id=1, source_target_pairs={{0,4},{4,0},{8,12},{12,8},{1,5},{5,1},{9,13},{13,9},{2,6},{6,2},{1... | collective-permute-start | bytes 7680008 | tf_op jit(solution)/shard_map/ppermute | solution.py:199
  1056.4 19.5 %collective-permute-start.30 = (bf16[256,1600]{0,1:T(8,128)(2,1)S(1)}, bf16[256,1600]{0,1:T(8,128)(2,1)S(1)}, u32[]{:S(2)}, u32[]{:S(2)}) collective-permute-start(bf16[256,1600]{0,1:T(8,128)(2,1)S(1)} %add_convert_fusion.5), channel_id=1, source_target_pairs={{0,8},{4,12},{8,0},{12,4},{1,9},{5,13},{9,1},{13,5},{2,10},{6,14},... | collective-permute-start | bytes 2457608 | tf_op jit(solution)/shard_map/cond/branch_1_fun/ppermute | solution.py:199
  1093.6 26.3 %collective-permute-start.102 = (bf16[400,800]{1,0:T(8,128)(2,1)S(1)}, bf16[400,800]{1,0:T(8,128)(2,1)S(1)}, u32[]{:S(2)}, u32[]{:S(2)}) collective-permute-start(bf16[400,800]{1,0:T(8,128)(2,1)S(1)} %get-tuple-element.815.refs_4_), channel_id=1, source_target_pairs={{0,8},{4,12},{8,0},{12,4},{1,9},{5,13},{9,1},{13,5},{2,10},{6,14},... | collective-permute-start | bytes 1920008 | tf_op jit(solution)/shard_map/ppermute | solution.py:199
  1094.1 24.3 %collective-permute-start.87 = (f32[4800]{0:T(1024)S(1)}, f32[4800]{0:T(1024)S(1)}, u32[]{:S(2)}, u32[]{:S(2)}) collective-permute-start(f32[4800]{0:T(1024)S(1)} %get-tuple-element.711), channel_id=1, source_target_pairs={{0,1},{1,0},{2,3},{3,2},{4,5},{5,4},{6,7},{7,6},{8,9},{9,8},{10,11... | collective-permute-start | bytes 57608 | tf_op jit(solution)/shard_map/ppermute | solution.py:199
  1096.7 22.9 %collective-permute-start.89 = (f32[4800]{0:T(1024)S(1)}, f32[4800]{0:T(1024)S(1)}, u32[]{:S(2)}, u32[]{:S(2)}) collective-permute-start(f32[4800]{0:T(1024)S(1)} %add.765), channel_id=1, source_target_pairs={{0,2},{1,3},{2,0},{3,1},{4,6},{5,7},{6,4},{7,5},{8,10},{9,11},{10,... | collective-permute-start | bytes 57608 | tf_op jit(solution)/shard_map/ppermute | solution.py:199
  1098.1 55.8 %collective-permute-start.92 = (bf16[400,1536]{1,0:T(8,128)(2,1)S(1)}, bf16[400,1536]{1,0:T(8,128)(2,1)}, u32[]{:S(2)}, u32[]{:S(2)}) collective-permute-start(bf16[400,1536]{1,0:T(8,128)(2,1)S(1)} %pad_maximum_fusion.7.refs_0_), channel_id=1, source_target_pairs={{0,8},{4,12},{8,0},{12,4},{1,9},{5,13},{9,1},{13,5},{2,10},{6,14},... | collective-permute-start | bytes 3686408 | tf_op jit(solution)/shard_map/ppermute | solution.py:199
  1118.4 33.5 %collective-permute-start.99 = (bf16[400,800]{1,0:T(8,128)(2,1)S(1)}, bf16[400,800]{1,0:T(8,128)(2,1)S(1)}, u32[]{:S(2)}, u32[]{:S(2)}) collective-permute-start(bf16[400,800]{1,0:T(8,128)(2,1)S(1)} %get-tuple-element.816.refs_0_), channel_id=1, source_target_pairs={{0,8},{4,12},{8,0},{12,4},{1,9},{5,13},{9,1},{13,5},{2,10},{6,14},... | collective-permute-start | bytes 1920008 | tf_op jit(solution)/shard_map/ppermute | solution.py:199
  1119.6 34.3 %collective-permute-start.98 = (bf16[400,800]{1,0:T(8,128)(2,1)S(1)}, bf16[400,800]{1,0:T(8,128)(2,1)S(1)}, u32[]{:S(2)}, u32[]{:S(2)}) collective-permute-start(bf16[400,800]{1,0:T(8,128)(2,1)S(1)} %get-tuple-element.816.refs_0_), channel_id=1, source_target_pairs={{0,4},{4,0},{8,12},{12,8},{1,5},{5,1},{9,13},{13,9},{2,6},{6,2},{1... | collective-permute-start | bytes 1920008 | tf_op jit(solution)/shard_map/ppermute | solution.py:199
  1130.2 32.2 %collective-permute-start.83 = (bf16[256,1600]{0,1:T(8,128)(2,1)}, bf16[256,1600]{0,1:T(8,128)(2,1)S(1)}, u32[]{:S(2)}, u32[]{:S(2)}) collective-permute-start(bf16[256,1600]{0,1:T(8,128)(2,1)} %broadcast_select_fusion.4), channel_id=1, source_target_pairs={{0,16},{16,0},{1,17},{17,1},{2,18},{18,2},{3,19},{19,3},{4,20},{20... | collective-permute-start | bytes 2457608 | tf_op jit(solution)/shard_map/ppermute | solution.py:199
  1131.6 31.5 %collective-permute-start.103 = (bf16[400,800]{1,0:T(8,128)(2,1)S(1)}, bf16[400,800]{1,0:T(8,128)(2,1)S(1)}, u32[]{:S(2)}, u32[]{:S(2)}) collective-permute-start(bf16[400,800]{1,0:T(8,128)(2,1)S(1)} %collective-permute-done.102.refs_6_), channel_id=1, source_target_pairs={{0,4},{4,0},{8,12},{12,8},{1,5},{5,1},{9,13},{13,9},{2,6},{6,2},{1... | collective-permute-start | bytes 1920008 | tf_op jit(solution)/shard_map/ppermute | solution.py:199
  1151.8 22.5 %collective-permute-start.91 = (bf16[400,1536]{1,0:T(8,128)(2,1)S(1)}, bf16[400,1536]{1,0:T(8,128)(2,1)S(1)}, u32[]{:S(2)}, u32[]{:S(2)}) collective-permute-start(bf16[400,1536]{1,0:T(8,128)(2,1)S(1)} %pad_maximum_fusion.7.refs_0_), channel_id=1, source_target_pairs={{0,4},{4,0},{8,12},{12,8},{1,5},{5,1},{9,13},{13,9},{2,6},{6,2},{1... | collective-permute-start | bytes 3686408 | tf_op jit(solution)/shard_map/ppermute | solution.py:199
  1153.8 20.5 %collective-permute-start.93 = (bf16[400,1536]{1,0:T(8,128)(2,1)}, bf16[400,1536]{1,0:T(8,128)(2,1)S(1)}, u32[]{:S(2)}, u32[]{:S(2)}) collective-permute-start(bf16[400,1536]{1,0:T(8,128)(2,1)} %collective-permute-done.92.refs_2_), channel_id=1, source_target_pairs={{0,4},{4,0},{8,12},{12,8},{1,5},{5,1},{9,13},{13,9},{2,6},{6,2},{1... | collective-permute-start | bytes 3686408 | tf_op jit(solution)/shard_map/ppermute | solution.py:199
  (213 other events, 2976.1 us)
Sparse Core Ops, SparseCore 0:
  32.4 54.7 all-gather.9
  88.8 33.9 all-gather.11
  125.0 58.4 all-gather.13
  185.0 54.1 all-gather.15
  240.6 33.7 all-gather.17
  275.8 51.6 all-gather.19
  329.1 57.6 all-gather.21
  388.4 98.2 all-gather.23
  521.1 94.2 reduce-scatter.10
  628.0 54.3 reduce-scatter.12
  711.1 32.9 reduce-scatter.14
  775.3 49.1 reduce-scatter.16
  842.4 53.1 reduce-scatter.24
  940.7 57.3 reduce-scatter.18
  1026.2 49.3 reduce-scatter.20
  1080.9 35.3 reduce-scatter.22

commit v4 on v3

--- a/solution.py
+++ b/solution.py
@@ -354,16 +354,20 @@
     assert kinds * count == len(pieces)
 
 
-def joined_columns(pieces, segments, ci, columns):
-    flat = [piece for kind in pieces for piece in kind]
-    rows = flat[0].shape[0]
+def joined_columns(pieces, kinds, segments, ci, columns):
+    flat = pieces * kinds
+    rows = flat[0].shape[0] // kinds
     tile = 80 if rows % 80 == 0 else rows
     return pl.pallas_call(
-        functools.partial(joined_kernel, len(pieces[0]), segments),
+        functools.partial(joined_kernel, len(pieces), segments),
         out_shape=jax.ShapeDtypeStruct((rows, columns), jnp.float32),
         grid=(rows // tile,),
         in_specs=[pl.BlockSpec(memory_space=pltpu.SMEM)]
-        + [pl.BlockSpec((tile, piece.shape[1]), lambda at: (at, 0)) for piece in flat],
+        + [
+            pl.BlockSpec((tile, piece.shape[1]), lambda at, kind=kind: (kind * (rows // tile) + at, 0))
+            for kind in range(kinds)
+            for piece in pieces
+        ],
         out_specs=pl.BlockSpec((tile, columns), lambda at: (at, 0)),
         compiler_params=pltpu.CompilerParams(vmem_limit_bytes=48 * 1024 * 1024),
         cost_estimate=pl.CostEstimate(
@@ -946,7 +950,7 @@
     ready[QKV, 0] = add((QKV, 0), None)
     sums[QKV, 0] = scatter_wt(after(ready[QKV, 0], sums[FC, 0]))
     fc_halves = (jnp.where(first, fc_own, fc_there), jnp.where(first, fc_there, fc_own))
-    fc_parts = [gathered(value, CTX) for value in fc_halves]
+    fc_parts = gathered(jnp.concatenate(fc_halves), CTX)
     leaving = state([coming], [fc_there])
     sums[PROJ, 0] = scatter_wt(after(ready[PROJ, 0], sums[QKV, 0]))
 
@@ -1005,7 +1009,7 @@
         for owner in range(count)
         for kind in range(2)
     ]
-    fc_grad = joined_columns(fc_parts, segments, ci, owners * hidden_rows)
+    fc_grad = joined_columns(fc_parts, 2, segments, ci, owners * hidden_rows)
     qkv_own, qkv_there = to_owner(QKV)
     qkv_halves = [jnp.where(first, qkv_own, qkv_there), jnp.where(first, qkv_there, qkv_own)]
     qkv_parts = gathered(jnp.concatenate(qkv_halves), CTX)
@@ -1020,7 +1024,7 @@
         for at in range(3)
         for owner in range(count)
     ]
-    qkv_grad = joined_columns([qkv_parts], segments, ci, 3 * width)
+    qkv_grad = joined_columns(qkv_parts, 1, segments, ci, 3 * width)
     proj_own, proj_there = to_owner(PROJ)
     proj_parts = gathered(low(wide(proj_own) + wide(proj_there)), CTX)
     starts = [plan.proj_start(ci ^ at) for at in range(count)]

time: 1200 us -> 1200 us (level)
    ppermute x104 -> x101, starting transfers between devices: 112 us -> 108 us  [swap(): return lax.ppermute(value, axis, flip(axis, bit))]
    ppermute x104 -> x101, waiting for transfers between devices: 434 us -> 433 us  [swap(): return lax.ppermute(value, axis, flip(axis, bit))]
    unnamed x335 -> x343, local copies, waits for them, and re-layouts: 46.8 us -> 47 us
  transfers between devices with their start and end apart: 122 -> 119, of which waited for: 61 -> 62; matrix products, arithmetic and copies ran while one was open for 38% -> 38% of each run, Pallas kernels for 8% -> 9%
where the time goes in v4:
time: 1200 us; the launch traced here: 1190 us
  waiting for transfers between devices  455 us (38%)
  matrix products  211 us (18%)
  local copies, waits for them, and re-layouts  159 us (13%)
  other arithmetic  122 us (10%)
  starting transfers between devices  115 us (10%)
  Pallas kernels  104 us (9%)
  between operations  16.8 us (1%)
    ppermute x101, waiting for transfers between devices, swap(): return lax.ppermute(value, axis, flip(axis, bit))  433 us
    ppermute x101, starting transfers between devices, swap(): return lax.ppermute(value, axis, flip(axis, bit))  108 us
    dot_general x12, matrix products, dot_tn(): lax.dot_general(left, right, (((0,), (0,)), ((), ())), preferred_element_...  72.1 us
    dot_general x12, matrix products, dot(): return jnp.dot(left, right, preferred_element_type=jnp.float32)  70.6 us
    dot_general x12, matrix products, dot_nt(): lax.dot_general(left, right, (((1,), (1,)), ((), ())), preferred_element_...  68.6 us
    unnamed x343, local copies, waits for them, and re-layouts  47 us
    pallas_call x2, Pallas kernels, attend_back(): pl.pallas_call(functools.partial(attend_back_kernel, block, tile, heads),...  42.4 us
    pallas_call x2, Pallas kernels, attend(): pl.pallas_call(functools.partial(attend_kernel, block, tile, heads), out_...  32.2 us
  transfers between devices with their start and end apart: 119, of which 62 were waited for; matrix products, arithmetic and copies ran while one was open for 38% of the time, Pallas kernels for 9%

profile of v4, /device:TPU:1, one launch (start us, length us, event | category | flops | bytes accessed | tf_op | source)
XLA Modules:
  0.0 1185.8 jit_solution(1172987641436540374)
XLA Ops:
  17.2 13.8 %collective-permute-done.49 = bf16[200,1536]{1,0:T(8,128)(2,1)S(1)} collective-permute-done((bf16[200,1536]{1,0:T(8,128)(2,1)}, bf16[200,1536]{1,0:T(8,128)(2,1)S(1)}, u32[]{:S(2)}, u32[]{:S(2)}) %collective-permute-start.49) | collective-permute-done | bytes 614432 | tf_op jit(solution)/shard_map/ppermute | solution.py:199
  40.8 11.5 collective-permute-done.51
  79.1 11.4 collective-permute-done.54
  97.9 23.1 %conditional.17 = (bf16[256,1600]{0,1:T(8,128)(2,1)}, bf16[256,1600]{0,1:T(8,128)(2,1)}, bf16[256,1600]{0,1:T(8,128)(2,1)}) conditional(s32[]{:T(128)} %bitcast.29, () %tuple.252, bf16[256,1600]{0,1:T(8,128)(2,1)S(1)} %fusion.73), branch_computations={%region_2.3_spmd, %region_3.4_spmd} | conditional | bytes 9830544 | solution.py:266
  104.6 8.0 collective-permute-done.1
  133.2 22.6 %collective-permute-done.60.refs_2_ = bf16[448,1600]{1,0:T(8,128)(2,1)S(1)} collective-permute-done((bf16[448,1600]{1,0:T(8,128)(2,1)}, bf16[448,1600]{1,0:T(8,128)(2,1)S(1)}, u32[]{:S(2)}, u32[]{:S(2)}) %collective-permute-start.60) | collective-permute-done | bytes 1433632 | tf_op jit(solution)/shard_map/ppermute | solution.py:199
  160.6 6.5 add_convert_fusion.11.qkv
  167.1 16.6 %shard_map.254 = (bf16[1024,512]{1,0:T(8,128)(2,1)}, f32[8,1024]{1,0:T(8,128)S(1)}) custom-call(s32[8]{0:T(128)S(1)} %select_reduce_fusion.place, bf16[1024,1536]{1,0:T(8,128)(2,1)S(1)} %add_convert_fusion.11.qkv), custom_call_target="tpu_custom_call" | custom-call | tf_op jit(solution)/shard_map/pallas_call | solution.py:86
  198.1 15.4 %conditional.18 = (bf16[1,256,512]{2,1,0:T(8,128)(2,1)}, bf16[1,256,512]{2,1,0:T(8,128)(2,1)}, bf16[1,256,512]{2,1,0:T(8,128)(2,1)}) conditional(s32[]{:T(128)} %bitcast.29, () %tuple.258, bf16[1024,512]{1,0:T(8,128)(2,1)} %get-tuple-element.399), branch_computations={%region_6.7_spmd, %region_7.8_spmd} | conditional | bytes 4718736 | solution.py:266
  201.5 6.8 collective-permute-done.21
  232.8 23.1 %conditional.19 = (bf16[256,1600]{0,1:T(8,128)(2,1)}, bf16[256,1600]{0,1:T(8,128)(2,1)}, bf16[256,1600]{0,1:T(8,128)(2,1)}) conditional(s32[]{:T(128)} %bitcast.29, () %tuple.259, bf16[256,1600]{0,1:T(8,128)(2,1)S(1)} %add_convert_fusion.18), branch_computations={%region_10.11_spmd, %region_11.12_spmd} | conditional | bytes 9830544 | solution.py:266
  235.0 17.0 %collective-permute-done.4 = bf16[256,1600]{0,1:T(8,128)(2,1)} collective-permute-done((bf16[256,1600]{0,1:T(8,128)(2,1)S(1)}, bf16[256,1600]{0,1:T(8,128)(2,1)}, u32[]{:S(2)}, u32[]{:S(2)}) %collective-permute-start.4) | collective-permute-done | bytes 819232 | tf_op jit(solution)/shard_map/cond/branch_1_fun/ppermute | solution.py:199
  266.0 7.2 fusion.31
  277.9 29.5 %collective-permute-done.66.refs_2_ = bf16[448,1600]{1,0:T(8,128)(2,1)S(1)} collective-permute-done((bf16[448,1600]{1,0:T(8,128)(2,1)}, bf16[448,1600]{1,0:T(8,128)(2,1)S(1)}, u32[]{:S(2)}, u32[]{:S(2)}) %collective-permute-start.66) | collective-permute-done | bytes 1433632 | tf_op jit(solution)/shard_map/ppermute | solution.py:199
  315.7 6.9 add_convert_fusion.9
  329.6 26.1 %conditional.20 = (f32[256,1600]{0,1:T(8,128)}) conditional(s32[]{:T(128)} %bitcast.29, () %tuple.268, bf16[1024,1600]{0,1:T(8,128)(2,1)} %add_convert_fusion.9), branch_computations={%region_12.13_spmd, %region_13.14_spmd} | conditional | flops 3686400 | bytes 32768156 | solution.py:266
  335.9 18.4 %collective-permute-done.27 = bf16[256,1600]{0,1:T(8,128)(2,1)S(1)} collective-permute-done((bf16[256,1600]{0,1:T(8,128)(2,1)S(1)}, bf16[256,1600]{0,1:T(8,128)(2,1)S(1)}, u32[]{:S(2)}, u32[]{:S(2)}) %collective-permute-start.27) | collective-permute-done | bytes 819232 | tf_op jit(solution)/shard_map/cond/branch_1_fun/ppermute | solution.py:199
  359.8 23.2 %conditional.21 = (bf16[256,1600]{0,1:T(8,128)(2,1)}, bf16[256,1600]{0,1:T(8,128)(2,1)}, bf16[256,1600]{0,1:T(8,128)(2,1)}) conditional(s32[]{:T(128)} %bitcast.29, () %tuple.269, bf16[256,1600]{0,1:T(8,128)(2,1)S(1)} %fusion.64), branch_computations={%region_16.17_spmd, %region_17.18_spmd} | conditional | bytes 9830544 | solution.py:266
  362.4 16.2 %collective-permute-done.7 = bf16[256,1600]{0,1:T(8,128)(2,1)} collective-permute-done((bf16[256,1600]{0,1:T(8,128)(2,1)S(1)}, bf16[256,1600]{0,1:T(8,128)(2,1)}, u32[]{:S(2)}, u32[]{:S(2)}) %collective-permute-start.7) | collective-permute-done | bytes 819232 | tf_op jit(solution)/shard_map/cond/branch_1_fun/ppermute | solution.py:199
  405.2 6.5 add_convert_fusion.10.qkv
  411.7 15.6 %shard_map.256 = (bf16[1024,512]{1,0:T(8,128)(2,1)S(1)}, f32[8,1024]{1,0:T(8,128)S(1)}) custom-call(s32[8]{0:T(128)S(1)} %select_reduce_fusion.place, bf16[1024,1536]{1,0:T(8,128)(2,1)S(1)} %add_convert_fusion.10.qkv), custom_call_target="tpu_custom_call" | custom-call | tf_op jit(solution)/shard_map/pallas_call | solution.py:86
  429.1 14.3 %conditional.22 = (bf16[1,256,512]{2,1,0:T(8,128)(2,1)}, bf16[1,256,512]{2,1,0:T(8,128)(2,1)}, bf16[1,256,512]{2,1,0:T(8,128)(2,1)}) conditional(s32[]{:T(128)} %bitcast.29, () %tuple.274, bf16[1024,512]{1,0:T(8,128)(2,1)S(1)} %get-tuple-element.454), branch_computations={%region_18.19_spmd, %region_19.20_spmd} | conditional | bytes 4718736 | solution.py:266
  431.4 6.9 collective-permute-done.24
  457.5 23.4 %conditional.23 = (bf16[256,1600]{0,1:T(8,128)(2,1)}, bf16[256,1600]{0,1:T(8,128)(2,1)}, bf16[256,1600]{0,1:T(8,128)(2,1)}) conditional(s32[]{:T(128)} %bitcast.29, () %tuple.275, bf16[256,1600]{0,1:T(8,128)(2,1)S(1)} %add_convert_fusion.16), branch_computations={%region_22.23_spmd, %region_23.24_spmd} | conditional | bytes 9830544 | solution.py:266
  459.6 17.2 %collective-permute-done.10 = bf16[256,1600]{0,1:T(8,128)(2,1)} collective-permute-done((bf16[256,1600]{0,1:T(8,128)(2,1)S(1)}, bf16[256,1600]{0,1:T(8,128)(2,1)}, u32[]{:S(2)}, u32[]{:S(2)}) %collective-permute-start.10) | collective-permute-done | bytes 819232 | tf_op jit(solution)/shard_map/cond/branch_1_fun/ppermute | solution.py:199
  494.1 6.7 collective-permute-done.71
  502.0 7.1 fusion.41
  555.4 24.6 %conditional.24 = (f32[256,1600]{0,1:T(8,128)}, f32[1,4,400]{2,1,0:T(4,128)S(1)}) conditional(s32[]{:T(128)} %bitcast.29, () %tuple.282, bf16[1024,1600]{0,1:T(8,128)(2,1)S(1)} %add_convert_fusion.8), branch_computations={%region_25.26_spmd, %region_26.28_spmd} | conditional | flops 4094400 | bytes 19680136 | solution.py:266
  559.7 18.4 %collective-permute-done.33 = bf16[256,1600]{0,1:T(8,128)(2,1)S(1)} collective-permute-done((bf16[256,1600]{0,1:T(8,128)(2,1)S(1)}, bf16[256,1600]{0,1:T(8,128)(2,1)S(1)}, u32[]{:S(2)}, u32[]{:S(2)}) %collective-permute-start.33) | collective-permute-done | bytes 819232 | tf_op jit(solution)/shard_map/cond/branch_1_fun/ppermute | solution.py:199
  594.5 16.4 %conditional.25 = (bf16[256,512]{1,0:T(8,128)(2,1)}, bf16[256,512]{1,0:T(8,128)(2,1)}, bf16[256,512]{1,0:T(8,128)(2,1)}, bf16[4,112,1600]{2,1,0:T(8,128)(2,1)}, ...) conditional(s32[]{:T(128)} %bitcast.29, () %tuple.281, ...), branch_computations={%region_30.31_spmd, %region_31.32_spmd} | conditional | flops 1313280000 | bytes 22946264 | solution.py:266
  619.5 8.5 add_convert_fusion.13
  628.0 7.6 conditional.26
  638.0 21.2 %shard_map.258 = bf16[1024,1536]{1,0:T(8,128)(2,1)} custom-call(s32[8]{0:T(128)S(1)} %select_reduce_fusion.place, bf16[1024,1536]{1,0:T(8,128)(2,1)S(1)} %add_convert_fusion.10.qkv, bf16[1024,512]{1,0:T(8,128)(2,1)S(1)} %copy-done.3, f32[8,1024]{1,0:T(8,128)S(1)} %get-tuple-element.496.log_total), custom_call_target="tpu_custom_call" | custom-call | tf_op jit(solution)/shard_map/pallas_call | solution.py:167
  659.2 12.0 %collective-permute-done.74 = bf16[4,112,1600]{2,1,0:T(8,128)(2,1)S(1)} collective-permute-done((bf16[4,112,1600]{2,1,0:T(8,128)(2,1)S(1)}, bf16[4,112,1600]{2,1,0:T(8,128)(2,1)S(1)}, u32[]{:S(2)}, u32[]{:S(2)}) %collective-permute-start.74) | collective-permute-done | bytes 1433632 | tf_op jit(solution)/shard_map/ppermute | solution.py:199
  676.5 9.1 convolution_convert_fusion.6
  685.7 25.4 %conditional.27 = (f32[256,1600]{0,1:T(8,128)S(1)}, bf16[4,2,200,1536]{3,2,1,0:T(8,128)(2,1)}) conditional(s32[]{:T(128)} %bitcast.29, () %tuple.292, (bf16[1024,1600]{0,1:T(8,128)(2,1)}, bf16[1024,1600]{0,1:T(8,128)(2,1)}, bf16[1024,1536]{1,0:T(8,128)(2,1)S(1)}) %tuple.529), branch_computations={%region_36.37_spmd, %region_37.38_spmd} | conditional | flops 5039308800 | bytes 44105892 | solution.py:266
  692.2 8.8 convolution_convert_fusion.1
  701.1 9.7 collective-permute-done.45
  720.7 23.4 %conditional.28 = (bf16[256,1600]{0,1:T(8,128)(2,1)}, bf16[256,1600]{0,1:T(8,128)(2,1)}, bf16[256,1600]{0,1:T(8,128)(2,1)}) conditional(s32[]{:T(128)} %bitcast.29, () %tuple.297, bf16[256,1600]{0,1:T(8,128)(2,1)S(1)} %get-tuple-element.516), branch_computations={%region_40.41_spmd, %region_41.42_spmd} | conditional | bytes 9830544 | solution.py:266
  723.2 16.3 %collective-permute-done.13 = bf16[256,1600]{0,1:T(8,128)(2,1)} collective-permute-done((bf16[256,1600]{0,1:T(8,128)(2,1)S(1)}, bf16[256,1600]{0,1:T(8,128)(2,1)}, u32[]{:S(2)}, u32[]{:S(2)}) %collective-permute-start.13) | collective-permute-done | bytes 819232 | tf_op jit(solution)/shard_map/cond/branch_1_fun/ppermute | solution.py:199
  744.1 6.8 convolution_convert_fusion.10
  761.3 7.7 multiply_convert_fusion
  794.2 33.9 %conditional.29 = (f32[256,1600]{0,1:T(8,128)S(1)}, f32[800,1600]{1,0:T(8,128)}) conditional(s32[]{:T(128)} %bitcast.29, () %tuple.302, (bf16[1024,1600]{0,1:T(8,128)(2,1)S(1)}, bf16[256,1600]{0,1:T(8,128)(2,1)S(1)}, bf16[256,1600]{0,1:T(8,128)(2,1)}, bf16[256,1600]{0,1:T(8,128)(2,1)}, bf16[256,1600]{0,1:T(8,128)(2,1)}, ...), branch_computations={%region_43.44_spmd, %region_44.45_spmd} | conditional | flops 2640793600 | bytes 49356964 | solution.py:266
  808.1 7.5 convert_bitcast_fusion
  815.6 10.8 collective-permute-done.39
  828.1 8.8 collective-permute-done.77
  842.7 7.2 convolution_convert_fusion.9
  858.9 17.2 %conditional.30 = (bf16[256,512]{1,0:T(8,128)(2,1)}, bf16[256,512]{1,0:T(8,128)(2,1)}, bf16[256,512]{1,0:T(8,128)(2,1)}, bf16[4,112,1600]{2,1,0:T(8,128)(2,1)}, ...) conditional(s32[]{:T(128)} %bitcast.29, () %tuple.308, ...), branch_computations={%region_48.49_spmd, %region_49.50_spmd} | conditional | flops 1313280000 | bytes 22946264 | solution.py:266
  876.0 7.5 conditional.31
  894.4 21.2 %shard_map.259 = bf16[1024,1536]{1,0:T(8,128)(2,1)S(1)} custom-call(s32[8]{0:T(128)S(1)} %select_reduce_fusion.place, bf16[1024,1536]{1,0:T(8,128)(2,1)} %copy-done.2, bf16[1024,512]{1,0:T(8,128)(2,1)S(1)} %copy-done.4, f32[8,1024]{1,0:T(8,128)S(1)} %get-tuple-element.546.log_total), custom_call_target="tpu_custom_call" | custom-call | tf_op jit(solution)/shard_map/pallas_call | solution.py:167
  915.6 7.2 collective-permute-done.79
  932.2 8.5 add_convert_fusion.12
  941.2 7.4 convolution_convert_fusion.4
  954.2 8.0 convolution_convert_fusion.5
  966.1 48.1 %conditional.32 = (f32[256,1600]{0,1:T(8,128)}, f32[1,4,400]{2,1,0:T(4,128)S(1)}) conditional(s32[]{:T(128)} %bitcast.29, () %tuple.320, bf16[1024,1600]{0,1:T(8,128)(2,1)S(1)} %convolution_convert_fusion.5), branch_computations={%region_53.54_spmd, %region_54.56_spmd} | conditional | flops 4094400 | bytes 19680136 | solution.py:266
  971.3 41.3 %collective-permute-done.36 = bf16[256,1600]{0,1:T(8,128)(2,1)S(1)} collective-permute-done((bf16[256,1600]{0,1:T(8,128)(2,1)S(1)}, bf16[256,1600]{0,1:T(8,128)(2,1)S(1)}, u32[]{:S(2)}, u32[]{:S(2)}) %collective-permute-start.36) | collective-permute-done | bytes 819232 | tf_op jit(solution)/shard_map/cond/branch_1_fun/ppermute | solution.py:199
  1041.9 9.0 collective-permute-done.82
  1051.8 25.9 %conditional.33 = (f32[256,1600]{0,1:T(8,128)}) conditional(s32[]{:T(128)} %bitcast.29, () %tuple.327, bf16[1024,1600]{0,1:T(8,128)(2,1)} %add_convert_fusion.6), branch_computations={%region_58.59_spmd, %region_59.60_spmd} | conditional | flops 3686400 | bytes 32768156 | solution.py:266
  1057.4 18.6 %collective-permute-done.30 = bf16[256,1600]{0,1:T(8,128)(2,1)S(1)} collective-permute-done((bf16[256,1600]{0,1:T(8,128)(2,1)S(1)}, bf16[256,1600]{0,1:T(8,128)(2,1)S(1)}, u32[]{:S(2)}, u32[]{:S(2)}) %collective-permute-start.30) | collective-permute-done | bytes 819232 | tf_op jit(solution)/shard_map/cond/branch_1_fun/ppermute | solution.py:199
  1089.6 8.6 collective-permute-done.90
  1099.8 15.4 %reduce-scatter.23.cloned.1.call-done = bf16[112,1600]{1,0:T(8,128)(2,1)} async-done(((bf16[448,1600]{1,0:T(8,128)(2,1)}), bf16[112,1600]{1,0:T(8,128)(2,1)}) %reduce-scatter.23.cloned.1.call-update) | async-done | bytes 358416 | tf_op jit(solution)/shard_map/reduce_scatter | solution.py:290
  1137.0 11.6 collective-permute-done.92.refs_2_
  1163.2 6.7 shard_map.262
  1169.9 6.9 shard_map.260
  (871 shorter events, 591.1 us)
Async XLA Ops:
  7.2 88.4 %all-gather.10.cloned.1.call-start = ((), (), s32[]{:S(2)}) async-start(), calls=%async_computation.8 | async-start | bytes 3072000 | tf_op jit(solution)/shard_map/all_gather | solution.py:286
  32.3 90.5 %all-gather.12.cloned.1.call-start = ((), (), s32[]{:S(2)}) async-start(), calls=%async_computation.9 | async-start | bytes 1863680 | tf_op jit(solution)/shard_map/all_gather | solution.py:286
  33.3 29.2 %collective-permute-start.50 = (bf16[256,1600]{0,1:T(8,128)(2,1)}, bf16[256,1600]{0,1:T(8,128)(2,1)}, u32[]{:S(2)}, u32[]{:S(2)}) collective-permute-start(bf16[256,1600]{0,1:T(8,128)(2,1)} %dynamic-slice_bitcast_fusion), channel_id=1, source_target_pairs={{0,16},{16,0},{1,17},{17,1},{2,18},{18,2},{3,19},{19,3},{4,20},{20... | collective-permute-start | bytes 2457608 | tf_op jit(solution)/shard_map/ppermute | solution.py:199
  37.1 23.2 %collective-permute-start.52 = (bf16[112,1600]{1,0:T(8,128)(2,1)}, bf16[112,1600]{1,0:T(8,128)(2,1)}, u32[]{:S(2)}, u32[]{:S(2)}) collective-permute-start(bf16[112,1600]{1,0:T(8,128)(2,1)} %dynamic-slice_bitcast_fusion.3), channel_id=1, source_target_pairs={{0,16},{16,0},{1,17},{17,1},{2,18},{18,2},{3,19},{19,3},{4,20},{20... | collective-permute-start | bytes 1075208 | tf_op jit(solution)/shard_map/ppermute | solution.py:199
  62.5 126.7 %all-gather.14.cloned.1.call-start = ((), (), s32[]{:S(2)}) async-start(), calls=%async_computation.10 | async-start | bytes 3584000 | tf_op jit(solution)/shard_map/all_gather | solution.py:286
  76.7 179.1 %all-gather.16.cloned.1.call-start = ((), (), s32[]{:S(2)}) async-start(), calls=%async_computation.11 | async-start | bytes 3328000 | tf_op jit(solution)/shard_map/all_gather | solution.py:286
  94.9 179.5 %all-gather.18.cloned.1.call-start = ((), (), s32[]{:S(2)}) async-start(), calls=%async_computation.12 | async-start | bytes 1863680 | tf_op jit(solution)/shard_map/all_gather | solution.py:286
  95.5 232.1 %all-gather.20.cloned.1.call-start = ((), (), s32[]{:S(2)}) async-start(), calls=%async_computation.13 | async-start | bytes 3072000 | tf_op jit(solution)/shard_map/all_gather | solution.py:286
  95.6 62.5 %collective-permute-start.58 = (bf16[800,1536]{1,0:T(8,128)(2,1)}, bf16[800,1536]{1,0:T(8,128)(2,1)}, u32[]{:S(2)}, u32[]{:S(2)}) collective-permute-start(bf16[800,1536]{1,0:T(8,128)(2,1)} %all-gather.10.cloned.1.call-done), channel_id=1, source_target_pairs={{0,16},{16,0},{1,17},{17,1},{2,18},{18,2},{3,19},{19,3},{4,20},{20... | collective-permute-start | bytes 7372808 | tf_op jit(solution)/shard_map/ppermute | solution.py:199
  99.2 19.6 %collective-permute-start = (bf16[256,1600]{0,1:T(8,128)(2,1)S(1)}, bf16[256,1600]{0,1:T(8,128)(2,1)}, u32[]{:S(2)}, u32[]{:S(2)}) collective-permute-start(bf16[256,1600]{0,1:T(8,128)(2,1)S(1)} %param.1), channel_id=1, source_target_pairs={{0,4},{4,0},{8,12},{12,8},{1,5},{5,1},{9,13},{13,9},{2,6},{6,2},{1... | collective-permute-start | bytes 2457608 | tf_op jit(solution)/shard_map/cond/branch_1_fun/ppermute | solution.py:199
  122.8 33.0 %collective-permute-start.60 = (bf16[448,1600]{1,0:T(8,128)(2,1)}, bf16[448,1600]{1,0:T(8,128)(2,1)S(1)}, u32[]{:S(2)}, u32[]{:S(2)}) collective-permute-start(bf16[448,1600]{1,0:T(8,128)(2,1)} %all-gather.12.cloned.1.call-done.refs_0_), channel_id=1, source_target_pairs={{0,8},{4,12},{8,0},{12,4},{1,9},{5,13},{9,1},{13,5},{2,10},{6,14},... | collective-permute-start | bytes 4300808 | tf_op jit(solution)/shard_map/ppermute | solution.py:199
  124.3 61.2 %collective-permute-start.62 = (bf16[200,1600]{1,0:T(8,128)(2,1)}, bf16[200,1600]{1,0:T(8,128)(2,1)}, u32[]{:S(2)}, u32[]{:S(2)}) collective-permute-start(bf16[200,1600]{1,0:T(8,128)(2,1)} %get-tuple-element.390), channel_id=1, source_target_pairs={{0,16},{16,0},{1,17},{17,1},{2,18},{18,2},{3,19},{19,3},{4,20},{20... | collective-permute-start | bytes 1920008 | tf_op jit(solution)/shard_map/ppermute | solution.py:199
  125.6 263.7 %all-gather.22.cloned.1.call-start = ((), (), s32[]{:S(2)}) async-start(), calls=%async_computation.14 | async-start | bytes 3584000 | tf_op jit(solution)/shard_map/all_gather | solution.py:286
  125.8 62.3 %collective-permute-start.59 = (bf16[448,1600]{1,0:T(8,128)(2,1)}, bf16[448,1600]{1,0:T(8,128)(2,1)S(1)}, u32[]{:S(2)}, u32[]{:S(2)}) collective-permute-start(bf16[448,1600]{1,0:T(8,128)(2,1)} %all-gather.12.cloned.1.call-done.refs_0_), channel_id=1, source_target_pairs={{0,4},{4,0},{8,12},{12,8},{1,5},{5,1},{9,13},{13,9},{2,6},{6,2},{1... | collective-permute-start | bytes 4300808 | tf_op jit(solution)/shard_map/ppermute | solution.py:199
  155.8 33.4 %collective-permute-start.61 = (bf16[448,1600]{1,0:T(8,128)(2,1)S(1)}, bf16[448,1600]{1,0:T(8,128)(2,1)}, u32[]{:S(2)}, u32[]{:S(2)}) collective-permute-start(bf16[448,1600]{1,0:T(8,128)(2,1)S(1)} %collective-permute-done.60.refs_2_), channel_id=1, source_target_pairs={{0,4},{4,0},{8,12},{12,8},{1,5},{5,1},{9,13},{13,9},{2,6},{6,2},{1... | collective-permute-start | bytes 4300808 | tf_op jit(solution)/shard_map/ppermute | solution.py:199
  194.4 61.4 %collective-permute-start.63 = (bf16[1600,800]{0,1:T(8,128)(2,1)}, bf16[1600,800]{0,1:T(8,128)(2,1)}, u32[]{:S(2)}, u32[]{:S(2)}) collective-permute-start(bf16[1600,800]{0,1:T(8,128)(2,1)} %copy.197), channel_id=1, source_target_pairs={{0,16},{16,0},{1,17},{17,1},{2,18},{18,2},{3,19},{19,3},{4,20},{20... | collective-permute-start | bytes 7680008 | tf_op jit(solution)/shard_map/ppermute | solution.py:199
  232.8 19.2 %collective-permute-start.4 = (bf16[256,1600]{0,1:T(8,128)(2,1)S(1)}, bf16[256,1600]{0,1:T(8,128)(2,1)}, u32[]{:S(2)}, u32[]{:S(2)}) collective-permute-start(bf16[256,1600]{0,1:T(8,128)(2,1)S(1)} %param.5), channel_id=1, source_target_pairs={{0,8},{4,12},{8,0},{12,4},{1,9},{5,13},{9,1},{13,5},{2,10},{6,14},... | collective-permute-start | bytes 2457608 | tf_op jit(solution)/shard_map/cond/branch_1_fun/ppermute | solution.py:199
  234.0 19.6 %collective-permute-start.3 = (bf16[256,1600]{0,1:T(8,128)(2,1)S(1)}, bf16[256,1600]{0,1:T(8,128)(2,1)}, u32[]{:S(2)}, u32[]{:S(2)}) collective-permute-start(bf16[256,1600]{0,1:T(8,128)(2,1)S(1)} %param.5), channel_id=1, source_target_pairs={{0,4},{4,0},{8,12},{12,8},{1,5},{5,1},{9,13},{13,9},{2,6},{6,2},{1... | collective-permute-start | bytes 2457608 | tf_op jit(solution)/shard_map/cond/branch_1_fun/ppermute | solution.py:199
  255.9 59.8 %collective-permute-start.64 = (bf16[800,1600]{1,0:T(8,128)(2,1)}, bf16[800,1600]{1,0:T(8,128)(2,1)}, u32[]{:S(2)}, u32[]{:S(2)}) collective-permute-start(bf16[800,1600]{1,0:T(8,128)(2,1)} %all-gather.16.cloned.1.call-done), channel_id=1, source_target_pairs={{0,16},{16,0},{1,17},{17,1},{2,18},{18,2},{3,19},{19,3},{4,20},{20... | collective-permute-start | bytes 7680008 | tf_op jit(solution)/shard_map/ppermute | solution.py:199
  274.4 33.0 %collective-permute-start.66 = (bf16[448,1600]{1,0:T(8,128)(2,1)}, bf16[448,1600]{1,0:T(8,128)(2,1)S(1)}, u32[]{:S(2)}, u32[]{:S(2)}) collective-permute-start(bf16[448,1600]{1,0:T(8,128)(2,1)} %all-gather.18.cloned.1.call-done.refs_0_), channel_id=1, source_target_pairs={{0,8},{4,12},{8,0},{12,4},{1,9},{5,13},{9,1},{13,5},{2,10},{6,14},... | collective-permute-start | bytes 4300808 | tf_op jit(solution)/shard_map/ppermute | solution.py:199
  275.6 247.7 %all-gather.24.cloned.1.call-start = ((), (), s32[]{:S(2)}) async-start(), calls=%async_computation.22 | async-start | bytes 6656000 | tf_op jit(solution)/shard_map/all_gather | solution.py:286
  276.1 46.4 %collective-permute-start.65 = (bf16[448,1600]{1,0:T(8,128)(2,1)}, bf16[448,1600]{1,0:T(8,128)(2,1)S(1)}, u32[]{:S(2)}, u32[]{:S(2)}) collective-permute-start(bf16[448,1600]{1,0:T(8,128)(2,1)} %all-gather.18.cloned.1.call-done.refs_0_), channel_id=1, source_target_pairs={{0,4},{4,0},{8,12},{12,8},{1,5},{5,1},{9,13},{13,9},{2,6},{6,2},{1... | collective-permute-start | bytes 4300808 | tf_op jit(solution)/shard_map/ppermute | solution.py:199
  327.6 61.6 %collective-permute-start.68 = (bf16[800,1536]{1,0:T(8,128)(2,1)}, bf16[800,1536]{1,0:T(8,128)(2,1)}, u32[]{:S(2)}, u32[]{:S(2)}) collective-permute-start(bf16[800,1536]{1,0:T(8,128)(2,1)} %all-gather.20.cloned.1.call-done), channel_id=1, source_target_pairs={{0,16},{16,0},{1,17},{17,1},{2,18},{18,2},{3,19},{19,3},{4,20},{20... | collective-permute-start | bytes 7372808 | tf_op jit(solution)/shard_map/ppermute | solution.py:199
  329.6 343.1 %reduce-scatter.11.cloned.1.call-start = ((), (), s32[]{:S(2)}) async-start(), calls=%async_computation.15 | async-start | bytes 6656000 | tf_op jit(solution)/shard_map/reduce_scatter | solution.py:290
  334.6 19.6 %collective-permute-start.27 = (bf16[256,1600]{0,1:T(8,128)(2,1)S(1)}, bf16[256,1600]{0,1:T(8,128)(2,1)S(1)}, u32[]{:S(2)}, u32[]{:S(2)}) collective-permute-start(bf16[256,1600]{0,1:T(8,128)(2,1)S(1)} %add_convert_fusion), channel_id=1, source_target_pairs={{0,8},{4,12},{8,0},{12,4},{1,9},{5,13},{9,1},{13,5},{2,10},{6,14},... | collective-permute-start | bytes 2457608 | tf_op jit(solution)/shard_map/cond/branch_1_fun/ppermute | solution.py:199
  361.0 19.6 %collective-permute-start.6 = (bf16[256,1600]{0,1:T(8,128)(2,1)S(1)}, bf16[256,1600]{0,1:T(8,128)(2,1)}, u32[]{:S(2)}, u32[]{:S(2)}) collective-permute-start(bf16[256,1600]{0,1:T(8,128)(2,1)S(1)} %param.9), channel_id=1, source_target_pairs={{0,4},{4,0},{8,12},{12,8},{1,5},{5,1},{9,13},{13,9},{2,6},{6,2},{1... | collective-permute-start | bytes 2457608 | tf_op jit(solution)/shard_map/cond/branch_1_fun/ppermute | solution.py:199
  396.6 84.4 %collective-permute-start.69 = (bf16[1600,800]{0,1:T(8,128)(2,1)}, bf16[1600,800]{0,1:T(8,128)(2,1)}, u32[]{:S(2)}, u32[]{:S(2)}) collective-permute-start(bf16[1600,800]{0,1:T(8,128)(2,1)} %copy.198), channel_id=1, source_target_pairs={{0,16},{16,0},{1,17},{17,1},{2,18},{18,2},{3,19},{19,3},{4,20},{20... | collective-permute-start | bytes 7680008 | tf_op jit(solution)/shard_map/ppermute | solution.py:199
  457.5 19.3 %collective-permute-start.10 = (bf16[256,1600]{0,1:T(8,128)(2,1)S(1)}, bf16[256,1600]{0,1:T(8,128)(2,1)}, u32[]{:S(2)}, u32[]{:S(2)}) collective-permute-start(bf16[256,1600]{0,1:T(8,128)(2,1)S(1)} %param.13), channel_id=1, source_target_pairs={{0,8},{4,12},{8,0},{12,4},{1,9},{5,13},{9,1},{13,5},{2,10},{6,14},... | collective-permute-start | bytes 2457608 | tf_op jit(solution)/shard_map/cond/branch_1_fun/ppermute | solution.py:199
  458.7 19.6 %collective-permute-start.9 = (bf16[256,1600]{0,1:T(8,128)(2,1)S(1)}, bf16[256,1600]{0,1:T(8,128)(2,1)}, u32[]{:S(2)}, u32[]{:S(2)}) collective-permute-start(bf16[256,1600]{0,1:T(8,128)(2,1)S(1)} %param.13), channel_id=1, source_target_pairs={{0,4},{4,0},{8,12},{12,8},{1,5},{5,1},{9,13},{13,9},{2,6},{6,2},{1... | collective-permute-start | bytes 2457608 | tf_op jit(solution)/shard_map/cond/branch_1_fun/ppermute | solution.py:199
  481.0 19.7 %collective-permute-start.71 = (bf16[256,1600]{0,1:T(8,128)(2,1)}, bf16[256,1600]{0,1:T(8,128)(2,1)S(1)}, u32[]{:S(2)}, u32[]{:S(2)}) collective-permute-start(bf16[256,1600]{0,1:T(8,128)(2,1)} %get-tuple-element.472), channel_id=1, source_target_pairs={{0,8},{4,12},{8,0},{12,4},{1,9},{5,13},{9,1},{13,5},{2,10},{6,14},... | collective-permute-start | bytes 2457608 | tf_op jit(solution)/shard_map/ppermute | solution.py:199
  482.2 27.0 %collective-permute-start.70 = (bf16[256,1600]{0,1:T(8,128)(2,1)}, bf16[256,1600]{0,1:T(8,128)(2,1)S(1)}, u32[]{:S(2)}, u32[]{:S(2)}) collective-permute-start(bf16[256,1600]{0,1:T(8,128)(2,1)} %get-tuple-element.472), channel_id=1, source_target_pairs={{0,4},{4,0},{8,12},{12,8},{1,5},{5,1},{9,13},{13,9},{2,6},{6,2},{1... | collective-permute-start | bytes 2457608 | tf_op jit(solution)/shard_map/ppermute | solution.py:199
  521.0 229.9 %reduce-scatter.13.cloned.1.call-start = ((), (), s32[]{:S(2)}) async-start(), calls=%async_computation.16 | async-start | bytes 3584000 | tf_op jit(solution)/shard_map/reduce_scatter | solution.py:290
  544.8 69.5 %collective-permute-start.73 = (bf16[1600,800]{0,1:T(8,128)(2,1)}, bf16[1600,800]{0,1:T(8,128)(2,1)}, u32[]{:S(2)}, u32[]{:S(2)}) collective-permute-start(bf16[1600,800]{0,1:T(8,128)(2,1)} %convolution_convert_fusion.11), channel_id=1, source_target_pairs={{0,16},{16,0},{1,17},{17,1},{2,18},{18,2},{3,19},{19,3},{4,20},{20... | collective-permute-start | bytes 7680008 | tf_op jit(solution)/shard_map/ppermute | solution.py:199
  558.4 19.6 %collective-permute-start.33 = (bf16[256,1600]{0,1:T(8,128)(2,1)S(1)}, bf16[256,1600]{0,1:T(8,128)(2,1)S(1)}, u32[]{:S(2)}, u32[]{:S(2)}) collective-permute-start(bf16[256,1600]{0,1:T(8,128)(2,1)S(1)} %add_convert_fusion.1), channel_id=1, source_target_pairs={{0,8},{4,12},{8,0},{12,4},{1,9},{5,13},{9,1},{13,5},{2,10},{6,14},... | collective-permute-start | bytes 2457608 | tf_op jit(solution)/shard_map/cond/branch_1_fun/ppermute | solution.py:199
  628.0 221.9 %reduce-scatter.15.cloned.1.call-start = ((), (), s32[]{:S(2)}) async-start(), calls=%async_computation.17 | async-start | bytes 1863680 | tf_op jit(solution)/shard_map/reduce_scatter | solution.py:290
  637.2 34.0 %collective-permute-start.74 = (bf16[4,112,1600]{2,1,0:T(8,128)(2,1)S(1)}, bf16[4,112,1600]{2,1,0:T(8,128)(2,1)S(1)}, u32[]{:S(2)}, u32[]{:S(2)}) collective-permute-start(bf16[4,112,1600]{2,1,0:T(8,128)(2,1)S(1)} %convert_element_type.474), channel_id=1, source_target_pairs={{0,8},{4,12},{8,0},{12,4},{1,9},{5,13},{9,1},{13,5},{2,10},{6,14},... | collective-permute-start | bytes 4300808 | tf_op jit(solution)/shard_map/ppermute | solution.py:199
  672.6 43.7 %collective-permute-start.75 = (bf16[400,1600]{1,0:T(8,128)(2,1)}, bf16[400,1600]{1,0:T(8,128)(2,1)}, u32[]{:S(2)}, u32[]{:S(2)}) collective-permute-start(bf16[400,1600]{1,0:T(8,128)(2,1)} %reduce-scatter.11.cloned.1.call-done), channel_id=1, source_target_pairs={{0,16},{1,17},{2,18},{3,19},{4,20},{5,21},{6,22},{7,23},{8,24},{9,... | collective-permute-start | bytes 3840008 | tf_op jit(solution)/shard_map/ppermute | solution.py:840
  691.2 19.5 %collective-permute-start.45 = (bf16[256,1600]{0,1:T(8,128)(2,1)S(1)}, bf16[256,1600]{0,1:T(8,128)(2,1)S(1)}, u32[]{:S(2)}, u32[]{:S(2)}) collective-permute-start(bf16[256,1600]{0,1:T(8,128)(2,1)S(1)} %add_convert_fusion.2), channel_id=1, source_target_pairs={{0,8},{4,12},{8,0},{12,4},{1,9},{5,13},{9,1},{13,5},{2,10},{6,14},... | collective-permute-start | bytes 2457608 | tf_op jit(solution)/shard_map/cond/branch_1_fun/ppermute | solution.py:199
  711.1 214.6 %reduce-scatter.17.cloned.1.call-start = ((), (), s32[]{:S(2)}) async-start(), calls=%async_computation.18 | async-start | bytes 3072000 | tf_op jit(solution)/shard_map/reduce_scatter | solution.py:290
  717.3 54.0 %collective-permute-start.76 = (bf16[800,1536]{1,0:T(8,128)(2,1)}, bf16[800,1536]{1,0:T(8,128)(2,1)}, u32[]{:S(2)}, u32[]{:S(2)}) collective-permute-start(bf16[800,1536]{1,0:T(8,128)(2,1)} %bitcast.66), channel_id=1, source_target_pairs={{0,16},{16,0},{1,17},{17,1},{2,18},{18,2},{3,19},{19,3},{4,20},{20... | collective-permute-start | bytes 7372808 | tf_op jit(solution)/shard_map/ppermute | solution.py:199
  721.8 19.7 %collective-permute-start.12 = (bf16[256,1600]{0,1:T(8,128)(2,1)S(1)}, bf16[256,1600]{0,1:T(8,128)(2,1)}, u32[]{:S(2)}, u32[]{:S(2)}) collective-permute-start(bf16[256,1600]{0,1:T(8,128)(2,1)S(1)} %param.23), channel_id=1, source_target_pairs={{0,4},{4,0},{8,12},{12,8},{1,5},{5,1},{9,13},{13,9},{2,6},{6,2},{1... | collective-permute-start | bytes 2457608 | tf_op jit(solution)/shard_map/cond/branch_1_fun/ppermute | solution.py:199
  775.3 150.4 %reduce-scatter.25.cloned.1.call-start = ((), (), s32[]{:S(2)}) async-start(), calls=%async_computation.23 | async-start | bytes 3328000
  779.5 57.5 %collective-permute-start.77 = (bf16[800,1600]{1,0:T(8,128)(2,1)}, bf16[800,1600]{1,0:T(8,128)(2,1)}, u32[]{:S(2)}, u32[]{:S(2)}) collective-permute-start(bf16[800,1600]{1,0:T(8,128)(2,1)} %convolution_convert_fusion.10), channel_id=1, source_target_pairs={{0,16},{16,0},{1,17},{17,1},{2,18},{18,2},{3,19},{19,3},{4,20},{20... | collective-permute-start | bytes 7680008 | tf_op jit(solution)/shard_map/ppermute | solution.py:199
  807.0 19.5 %collective-permute-start.39 = (bf16[256,1600]{0,1:T(8,128)(2,1)S(1)}, bf16[256,1600]{0,1:T(8,128)(2,1)S(1)}, u32[]{:S(2)}, u32[]{:S(2)}) collective-permute-start(bf16[256,1600]{0,1:T(8,128)(2,1)S(1)} %add_convert_fusion.3), channel_id=1, source_target_pairs={{0,8},{4,12},{8,0},{12,4},{1,9},{5,13},{9,1},{13,5},{2,10},{6,14},... | collective-permute-start | bytes 2457608 | tf_op jit(solution)/shard_map/cond/branch_1_fun/ppermute | solution.py:199
  842.3 177.7 %reduce-scatter.19.cloned.1.call-start = ((), (), s32[]{:S(2)}) async-start(), calls=%async_computation.19 | async-start | bytes 3584000 | tf_op jit(solution)/shard_map/reduce_scatter | solution.py:290
  849.9 75.8 %collective-permute-start.78 = (bf16[1600,800]{0,1:T(8,128)(2,1)}, bf16[1600,800]{0,1:T(8,128)(2,1)}, u32[]{:S(2)}, u32[]{:S(2)}) collective-permute-start(bf16[1600,800]{0,1:T(8,128)(2,1)} %convolution_convert_fusion.9), channel_id=1, source_target_pairs={{0,16},{16,0},{1,17},{17,1},{2,18},{18,2},{3,19},{19,3},{4,20},{20... | collective-permute-start | bytes 7680008 | tf_op jit(solution)/shard_map/ppermute | solution.py:199
  888.4 34.4 %collective-permute-start.79 = (bf16[4,112,1600]{2,1,0:T(8,128)(2,1)}, bf16[4,112,1600]{2,1,0:T(8,128)(2,1)}, u32[]{:S(2)}, u32[]{:S(2)}) collective-permute-start(bf16[4,112,1600]{2,1,0:T(8,128)(2,1)} %convert_element_type.497), channel_id=1, source_target_pairs={{0,8},{4,12},{8,0},{12,4},{1,9},{5,13},{9,1},{13,5},{2,10},{6,14},... | collective-permute-start | bytes 4300808 | tf_op jit(solution)/shard_map/ppermute | solution.py:199
  925.7 28.5 %collective-permute-start.81 = (bf16[200,1600]{1,0:T(8,128)(2,1)}, bf16[200,1600]{1,0:T(8,128)(2,1)}, u32[]{:S(2)}, u32[]{:S(2)}) collective-permute-start(bf16[200,1600]{1,0:T(8,128)(2,1)} %reduce-scatter.25.cloned.1.call-done), channel_id=1, source_target_pairs={{16,0},{17,1},{18,2},{19,3},{20,4},{21,5},{22,6},{23,7},{24,8},{25... | collective-permute-start | bytes 1920008 | tf_op jit(solution)/shard_map/ppermute | solution.py:840
  940.7 140.3 %reduce-scatter.21.cloned.1.call-start = ((), (), s32[]{:S(2)}) async-start(), calls=%async_computation.20 | async-start | bytes 3072000 | tf_op jit(solution)/shard_map/reduce_scatter | solution.py:290
  951.3 71.1 %collective-permute-start.80 = (bf16[800,1536]{1,0:T(8,128)(2,1)}, bf16[800,1536]{1,0:T(8,128)(2,1)}, u32[]{:S(2)}, u32[]{:S(2)}) collective-permute-start(bf16[800,1536]{1,0:T(8,128)(2,1)} %bitcast.69), channel_id=1, source_target_pairs={{0,16},{16,0},{1,17},{17,1},{2,18},{18,2},{3,19},{19,3},{4,20},{20... | collective-permute-start | bytes 7372808 | tf_op jit(solution)/shard_map/ppermute | solution.py:199
  965.6 61.6 %collective-permute-start.101 = (bf16[400,1600]{1,0:T(8,128)(2,1)}, bf16[400,1600]{1,0:T(8,128)(2,1)}, u32[]{:S(2)}, u32[]{:S(2)}) collective-permute-start(bf16[400,1600]{1,0:T(8,128)(2,1)} %pad_maximum_fusion.6.refs_0_), channel_id=1, source_target_pairs={{0,8},{4,12},{8,0},{12,4},{1,9},{5,13},{9,1},{13,5},{2,10},{6,14},... | collective-permute-start | bytes 3840008 | tf_op jit(solution)/shard_map/ppermute | solution.py:199
  970.4 42.2 %collective-permute-start.36 = (bf16[256,1600]{0,1:T(8,128)(2,1)S(1)}, bf16[256,1600]{0,1:T(8,128)(2,1)S(1)}, u32[]{:S(2)}, u32[]{:S(2)}) collective-permute-start(bf16[256,1600]{0,1:T(8,128)(2,1)S(1)} %add_convert_fusion.4), channel_id=1, source_target_pairs={{0,8},{4,12},{8,0},{12,4},{1,9},{5,13},{9,1},{13,5},{2,10},{6,14},... | collective-permute-start | bytes 2457608 | tf_op jit(solution)/shard_map/cond/branch_1_fun/ppermute | solution.py:199
  1026.2 89.0 %reduce-scatter.23.cloned.1.call-start = ((), (), s32[]{:S(2)}) async-start(), calls=%async_computation.21 | async-start | bytes 1863680 | tf_op jit(solution)/shard_map/reduce_scatter | solution.py:290
  1030.8 92.7 %collective-permute-start.102 = (bf16[800,1600]{1,0:T(8,128)(2,1)}, bf16[800,1600]{1,0:T(8,128)(2,1)}, u32[]{:S(2)}, u32[]{:S(2)}) collective-permute-start(bf16[800,1600]{1,0:T(8,128)(2,1)} %pad_maximum_fusion.3), channel_id=1, source_target_pairs={{0,4},{4,0},{8,12},{12,8},{1,5},{5,1},{9,13},{13,9},{2,6},{6,2},{1... | collective-permute-start | bytes 7680008 | tf_op jit(solution)/shard_map/ppermute | solution.py:199
  1056.5 19.5 %collective-permute-start.30 = (bf16[256,1600]{0,1:T(8,128)(2,1)S(1)}, bf16[256,1600]{0,1:T(8,128)(2,1)S(1)}, u32[]{:S(2)}, u32[]{:S(2)}) collective-permute-start(bf16[256,1600]{0,1:T(8,128)(2,1)S(1)} %add_convert_fusion.5), channel_id=1, source_target_pairs={{0,8},{4,12},{8,0},{12,4},{1,9},{5,13},{9,1},{13,5},{2,10},{6,14},... | collective-permute-start | bytes 2457608 | tf_op jit(solution)/shard_map/cond/branch_1_fun/ppermute | solution.py:199
  1087.4 45.4 %collective-permute-start.99 = (bf16[800,800]{1,0:T(8,128)(2,1)S(1)}, bf16[800,800]{1,0:T(8,128)(2,1)S(1)}, u32[]{:S(2)}, u32[]{:S(2)}) collective-permute-start(bf16[800,800]{1,0:T(8,128)(2,1)S(1)} %pad_maximum_fusion.4.refs_0_.refs_4_), channel_id=1, source_target_pairs={{0,8},{4,12},{8,0},{12,4},{1,9},{5,13},{9,1},{13,5},{2,10},{6,14},... | collective-permute-start | bytes 3840008 | tf_op jit(solution)/shard_map/ppermute | solution.py:199
  1088.8 33.4 %collective-permute-start.86 = (f32[4,4800]{1,0:T(4,128)}, f32[4,4800]{1,0:T(4,128)}, u32[]{:S(2)}, u32[]{:S(2)}) collective-permute-start(f32[4,4800]{1,0:T(4,128)} %add.762), channel_id=1, source_target_pairs={{0,8},{4,12},{8,0},{12,4},{1,9},{5,13},{9,1},{13,5},{2,10},{6,14},... | collective-permute-start | bytes 230408 | tf_op jit(solution)/shard_map/ppermute | solution.py:199
  1099.4 49.2 %collective-permute-start.92 = (bf16[400,1536]{1,0:T(8,128)(2,1)}, bf16[400,1536]{1,0:T(8,128)(2,1)}, u32[]{:S(2)}, u32[]{:S(2)}) collective-permute-start(bf16[400,1536]{1,0:T(8,128)(2,1)} %pad_maximum_fusion.8.refs_0_), channel_id=1, source_target_pairs={{0,8},{4,12},{8,0},{12,4},{1,9},{5,13},{9,1},{13,5},{2,10},{6,14},... | collective-permute-start | bytes 3686408 | tf_op jit(solution)/shard_map/ppermute | solution.py:199
  1122.3 27.1 %collective-permute-start.83 = (bf16[256,1600]{0,1:T(8,128)(2,1)S(1)}, bf16[256,1600]{0,1:T(8,128)(2,1)S(1)}, u32[]{:S(2)}, u32[]{:S(2)}) collective-permute-start(bf16[256,1600]{0,1:T(8,128)(2,1)S(1)} %broadcast_select_fusion.4), channel_id=1, source_target_pairs={{0,16},{16,0},{1,17},{17,1},{2,18},{18,2},{3,19},{19,3},{4,20},{20... | collective-permute-start | bytes 2457608 | tf_op jit(solution)/shard_map/ppermute | solution.py:199
  1129.6 28.3 %collective-permute-start.98 = (bf16[800,800]{1,0:T(8,128)(2,1)S(1)}, bf16[800,800]{1,0:T(8,128)(2,1)S(1)}, u32[]{:S(2)}, u32[]{:S(2)}) collective-permute-start(bf16[800,800]{1,0:T(8,128)(2,1)S(1)} %pad_maximum_fusion.4.refs_0_.refs_4_), channel_id=1, source_target_pairs={{0,4},{4,0},{8,12},{12,8},{1,5},{5,1},{9,13},{13,9},{2,6},{6,2},{1... | collective-permute-start | bytes 3840008 | tf_op jit(solution)/shard_map/ppermute | solution.py:199
  1132.8 30.4 %collective-permute-start.100 = (bf16[800,800]{1,0:T(8,128)(2,1)S(1)}, bf16[800,800]{1,0:T(8,128)(2,1)S(1)}, u32[]{:S(2)}, u32[]{:S(2)}) collective-permute-start(bf16[800,800]{1,0:T(8,128)(2,1)S(1)} %collective-permute-done.99.refs_2_.refs_6_), channel_id=1, source_target_pairs={{0,4},{4,0},{8,12},{12,8},{1,5},{5,1},{9,13},{13,9},{2,6},{6,2},{1... | collective-permute-start | bytes 3840008 | tf_op jit(solution)/shard_map/ppermute | solution.py:199
  1135.9 33.9 %collective-permute-start.91 = (bf16[400,1536]{1,0:T(8,128)(2,1)}, bf16[400,1536]{1,0:T(8,128)(2,1)S(1)}, u32[]{:S(2)}, u32[]{:S(2)}) collective-permute-start(bf16[400,1536]{1,0:T(8,128)(2,1)} %pad_maximum_fusion.8.refs_0_), channel_id=1, source_target_pairs={{0,4},{4,0},{8,12},{12,8},{1,5},{5,1},{9,13},{13,9},{2,6},{6,2},{1... | collective-permute-start | bytes 3686408 | tf_op jit(solution)/shard_map/ppermute | solution.py:199
  1148.6 21.3 %collective-permute-start.93 = (bf16[400,1536]{1,0:T(8,128)(2,1)}, bf16[400,1536]{1,0:T(8,128)(2,1)S(1)}, u32[]{:S(2)}, u32[]{:S(2)}) collective-permute-start(bf16[400,1536]{1,0:T(8,128)(2,1)} %collective-permute-done.92.refs_2_), channel_id=1, source_target_pairs={{0,4},{4,0},{8,12},{12,8},{1,5},{5,1},{9,13},{13,9},{2,6},{6,2},{1... | collective-permute-start | bytes 3686408 | tf_op jit(solution)/shard_map/ppermute | solution.py:199
  1157.8 19.0 %collective-permute-start.95 = (bf16[112,1600]{1,0:T(8,128)(2,1)S(1)}, bf16[112,1600]{1,0:T(8,128)(2,1)S(1)}, u32[]{:S(2)}, u32[]{:S(2)}) collective-permute-start(bf16[112,1600]{1,0:T(8,128)(2,1)S(1)} %add_convert_fusion.21.refs_0_), channel_id=1, source_target_pairs={{0,4},{4,0},{8,12},{12,8},{1,5},{5,1},{9,13},{13,9},{2,6},{6,2},{1... | collective-permute-start | bytes 1075208 | tf_op jit(solution)/shard_map/ppermute | solution.py:199
  (214 other events, 2927.9 us)
Sparse Core Ops, SparseCore 0:
  32.4 54.7 all-gather.9
  88.8 33.9 all-gather.11
  125.0 58.4 all-gather.13
  185.0 54.1 all-gather.15
  240.6 33.7 all-gather.17
  275.8 51.6 all-gather.19
  329.1 57.6 all-gather.21
  388.4 98.2 all-gather.23
  521.1 94.2 reduce-scatter.10
  628.1 54.2 reduce-scatter.12
  711.2 32.7 reduce-scatter.14
  775.4 49.0 reduce-scatter.16
  842.5 53.0 reduce-scatter.24
  940.8 57.2 reduce-scatter.18
  1026.3 49.1 reduce-scatter.20
  1081.1 33.9 reduce-scatter.22
